TPU v7x, 256 devices: a whole 4x4x8 slice. The times are simulated.
256 devices in a mesh: img: 8 (over x, core), txt: 32 (over z, y).
Axes of the slice: x: 4, y: 4, z: 8, core: 2. Of those that a mesh axis runs over, the one named last changes fastest.
Arguments:
- picture_embedding_matrix: bfloat16 [8192, 1280], P(('img', 'txt')), may hold values from -0.5 to 0.5
- caption_embedding_matrix: bfloat16 [8192, 1280], P(('txt', 'img')), may hold values from -0.5 to 0.5
- log_scaling_parameter: float32 [1], replicated, may hold values from 2.3 to 5.7
Outputs:
- grad_image: bfloat16 [8192, 1280], P(('img', 'txt'))
- grad_text: bfloat16 [8192, 1280], P(('txt', 'img'))
- loss: float32 [1], replicated
- temp_grad: float32 [1], replicated
All inputs are finite; a program needn't handle non-finite values.
Results may differ from a plain program's by a relative error of at most 0.019.
Values may be sent and summed in bfloat16 or wider, within the bound.
No kernel may reach another device: no remote copies, remote signals or barrier semaphores. Data moves between devices by JAX's collectives and lax.ppermute only.
A program may use at most 64 MiB of HBM per device.

v0:
```python
import math

import jax
import jax.numpy as jnp
from jax import lax
from jax.sharding import PartitionSpec as P


def unit_rows(features):
    values = features.astype(jnp.float32)
    inverse_norm_factor = lax.rsqrt(jnp.sum(values * values, axis=1, keepdims=True) + 1e-06)
    return (values * inverse_norm_factor, inverse_norm_factor)


def unit_sphere_backward(gradient, direction, inverse_norm_factor):
    inner = jnp.sum(direction * gradient, axis=1, keepdims=True)
    return ((gradient - direction * inner) * inverse_norm_factor).astype(jnp.bfloat16)


def shards(picture_embedding_matrix, caption_embedding_matrix, log_scaling_parameter):
    fitted_similarity_scaling = jnp.exp(log_scaling_parameter[0])
    img_dir, img_inv = unit_rows(picture_embedding_matrix)
    txt_dir, txt_inv = unit_rows(caption_embedding_matrix)
    img_block = lax.all_gather(img_dir.astype(jnp.bfloat16), "txt", axis=0, tiled=True)
    txt_block = lax.all_gather(txt_dir.astype(jnp.bfloat16), "img", axis=0, tiled=True)
    own_rows = picture_embedding_matrix.shape[0]
    feat_width = picture_embedding_matrix.shape[1]
    pair_count = own_rows * lax.axis_size("img") * lax.axis_size("txt")
    tile_rows = img_block.shape[0]
    tile_cols = txt_block.shape[0]
    img_pos = lax.axis_index("img")
    txt_pos = lax.axis_index("txt")
    step_rows = math.gcd(tile_rows, 512)
    step_count = tile_rows // step_rows
    blocks = img_block.reshape(step_count, step_rows, feat_width)
    block_starts = img_pos * tile_rows + jnp.arange(step_count, dtype=jnp.int32) * step_rows
    col_index = txt_pos * tile_cols + jnp.arange(tile_cols, dtype=jnp.int32)

    def logits_of(img_piece):
        return fitted_similarity_scaling * jnp.einsum(
            "rd,cd->rc", img_piece, txt_block, preferred_element_type=jnp.float32
        )

    lowest = jnp.full((tile_cols,), -jnp.inf, jnp.float32)

    def peak_pass(col_peak, img_piece):
        logits = logits_of(img_piece)
        return (jnp.maximum(col_peak, jnp.max(logits, axis=0)), jnp.max(logits, axis=1))

    col_peak, entrywise_maximum_along_line = lax.scan(peak_pass, lowest, blocks)
    entrywise_maximum_along_line = lax.pmax(entrywise_maximum_along_line.reshape(tile_rows), "txt")
    col_peak = lax.pmax(col_peak, "img")

    def total_pass(col_total, scan_item):
        img_piece, peak_part = scan_item
        logits = logits_of(img_piece)
        col_total = col_total + jnp.sum(jnp.exp(logits - col_peak[None, :]), axis=0)
        return (col_total, jnp.sum(jnp.exp(logits - peak_part[:, None]), axis=1))

    col_total, row_total = lax.scan(
        total_pass,
        jnp.zeros((tile_cols,), jnp.float32),
        (blocks, entrywise_maximum_along_line.reshape(step_count, step_rows)),
    )
    row_total = lax.psum(row_total.reshape(tile_rows), "txt")
    col_total = lax.psum(col_total, "img")
    row_lse = entrywise_maximum_along_line + jnp.log(row_total)
    col_lse = col_peak + jnp.log(col_total)

    def grad_pass(carried, scan_item):
        txt_sum, temp_sum, pos_sum = carried
        img_piece, row_start, lse_part = scan_item
        logits = logits_of(img_piece)
        row_index = row_start + jnp.arange(step_rows, dtype=jnp.int32)
        matching_pair_mask = row_index[:, None] == col_index[None, :]
        weights = (
            jnp.exp(logits - lse_part[:, None])
            + jnp.exp(logits - col_lse[None, :])
            - 2.0 * matching_pair_mask.astype(jnp.float32)
        )
        logit_grads = (0.5 * weights).astype(jnp.bfloat16)
        img_term = fitted_similarity_scaling * jnp.dot(
            logit_grads, txt_block, preferred_element_type=jnp.float32
        )
        txt_sum = txt_sum + jnp.einsum(
            "rc,rd->cd", logit_grads, img_piece, preferred_element_type=jnp.float32
        )
        temp_sum = temp_sum + jnp.sum(logit_grads.astype(jnp.float32) * logits)
        pos_sum = pos_sum + jnp.sum(jnp.where(matching_pair_mask, logits, jnp.float32(0.0)))
        return ((txt_sum, temp_sum, pos_sum), img_term)

    start_state = (
        jnp.zeros((tile_cols, feat_width), jnp.float32),
        jnp.float32(0.0),
        jnp.float32(0.0),
    )
    (txt_sum, temp_sum, pos_sum), img_terms = lax.scan(
        grad_pass, start_state, (blocks, block_starts, row_lse.reshape(step_count, step_rows))
    )
    img_terms = img_terms.reshape(tile_rows, feat_width)
    img_grad = lax.psum_scatter(
        img_terms.astype(jnp.bfloat16), "txt", scatter_dimension=0, tiled=True
    ).astype(jnp.float32)
    txt_grad = lax.psum_scatter(
        (fitted_similarity_scaling * txt_sum).astype(jnp.bfloat16),
        "img",
        scatter_dimension=0,
        tiled=True,
    ).astype(jnp.float32)
    diagonal_entry_logsumexp = lax.dynamic_slice_in_dim(row_lse, txt_pos * own_rows, own_rows)
    own_col_lse = lax.dynamic_slice_in_dim(col_lse, img_pos * own_rows, own_rows)
    local_loss = jnp.sum(diagonal_entry_logsumexp) + jnp.sum(own_col_lse) - 2.0 * pos_sum
    loss_sum, temp_total = lax.psum((local_loss, temp_sum), ("img", "txt"))
    loss = (loss_sum / (2 * pair_count)).reshape(1)
    temp_grad = (temp_total / pair_count).reshape(1)
    return (
        unit_sphere_backward(img_grad, img_dir, img_inv),
        unit_sphere_backward(txt_grad, txt_dir, txt_inv),
        loss,
        temp_grad,
    )


def solution(mesh):
    return jax.shard_map(
        shards,
        mesh=mesh,
        in_specs=(P(("img", "txt"), None), P(("txt", "img"), None), P()),
        out_specs=(P(("img", "txt"), None), P(("txt", "img"), None), P(), P()),
        check_vma=False,
    )
```

profile of v0, /device:TPU:2, one launch (start us, length us, event | category | flops | bytes accessed | tf_op | source)
XLA Modules:
  0.0 551.7 jit_solution(13951274625505979260)
XLA Ops:
  7.2 0.0 all-gather.2.cloned.1.call-start
  7.2 1.0 fusion.38
  8.2 1.6 fusion.37
  9.8 0.0 all-gather.2.cloned.1.call-update
  9.9 0.0 reduce-scatter.5.cloned.1.call-start
  10.7 1.0 fusion.39
  11.7 1.0 fusion.35
  12.7 13.3 %all_gather.7 = bf16[256,1280]{1,0:T(8,128)(2,1)S(1)} all-gather(bf16[32,1280]{1,0:T(8,128)(2,1)S(1)} %fusion.35), channel_id=1, replica_groups=mesh['img'=8,'txt'=32] {'img'}, dimensions={0}, use_global_device_ids=true | all-gather | bytes 737280 | tf_op jit(solution)/shard_map/all_gather | solution.py:25
  26.0 67.1 %all-gather.2.cloned.1.call-done = bf16[1024,1280]{1,0:T(8,128)(2,1)} async-done(((bf16[32,1280]{1,0:T(8,128)(2,1)}), bf16[1024,1280]{1,0:T(8,128)(2,1)}) %all-gather.2.cloned.1.call-update) | async-done | bytes 2621456 | tf_op jit(solution)/shard_map/all_gather | solution.py:24
  93.1 4.0 while.43
  93.1 1.9 fusion.62
  95.1 1.9 fusion.62
  97.1 72.0 %pmax.14 = f32[1024]{0:T(1024)S(1)} all-reduce(f32[1024]{0:T(1024)S(1)} %bitcast.83), channel_id=1, replica_groups=mesh['img'=8,'txt'=32] {'txt'}, use_global_device_ids=true, to_apply=%region_6.7 | all-reduce | flops 1024 | bytes 8192 | tf_op jit(solution)/shard_map/pmax | solution.py:51
  169.1 10.0 %pmax.15 = f32[256]{0:T(256)S(1)} all-reduce(f32[256]{0:T(256)S(1)} %get-tuple-element.146), channel_id=1, replica_groups=mesh['img'=8,'txt'=32] {'img'}, use_global_device_ids=true, to_apply=%region_7.8 | all-reduce | flops 256 | bytes 2048 | tf_op jit(solution)/shard_map/pmax | solution.py:52
  179.1 4.1 while.44
  179.2 2.0 exponential_reduce_fusion.3
  181.2 2.0 exponential_reduce_fusion.3
  183.3 69.6 %psum.28 = f32[1024]{0:T(1024)S(1)} all-reduce(f32[1024]{0:T(1024)S(1)} %bitcast.84), channel_id=1, replica_groups=mesh['img'=8,'txt'=32] {'txt'}, use_global_device_ids=true, to_apply=%region_12.13 | all-reduce | flops 1024 | bytes 8192 | tf_op jit(solution)/shard_map/psum | solution.py:65
  252.9 11.9 %psum.29 = f32[256]{0:T(256)S(1)} all-reduce(f32[256]{0:T(256)S(1)} %get-tuple-element.148), channel_id=1, replica_groups=mesh['img'=8,'txt'=32] {'img'}, use_global_device_ids=true, to_apply=%region_13.14 | all-reduce | flops 256 | bytes 2048 | tf_op jit(solution)/shard_map/psum | solution.py:66
  264.9 20.2 %while.45 = (s32[]{:T(128)}, f32[256,1280]{1,0:T(8,128)S(1)}, f32[]{:T(128)}, f32[]{:T(128)}, bf16[2,512,1280]{2,1,0:T(8,128)(2,1)}, /*index=5*/f32[]{:T(128)}, ...) while((s32[]{:T(128)}, f32[256,1280]{1,0:T(8,128)S(1)}, ...), condition=%wide.region_17.18_spmd.clone, body=%wide.region_14.17_spmd.clone.sunk | while | flops 1011876608 | bytes 31745816 | solution.py:97
  264.9 0.6 dynamic_slice.78
  265.5 0.6 iota_add_fusion.5
  266.1 2.7 fusion.69
  270.2 2.5 convolution_add_fusion.2
  272.7 0.7 fusion.70
  273.4 1.5 copy-done.1
  274.9 0.6 dynamic_slice.78
  275.5 0.6 iota_add_fusion.5
  276.2 2.7 fusion.69
  280.3 2.5 convolution_add_fusion.2
  282.8 0.7 fusion.70
  283.5 1.5 copy-done.1
  285.0 0.9 multiply_convert_fusion
  285.9 0.0 reduce-scatter.5.cloned.1.call-update
  286.0 0.0 reduce-scatter.3.cloned.1.call-start
  286.0 0.0 copy-start.2
  286.0 0.0 copy-start.3
  286.0 0.7 reduce-scatter.3.cloned.1.call-update
  286.7 0.7 dynamic-slice_reduce_fusion.1
  287.4 0.7 dynamic-slice_reduce_fusion
  289.3 76.7 %all-reduce = (f32[]{:T(128)}, f32[]{:T(128)}) all-reduce(f32[]{:T(128)S(6)} %sub.50, f32[]{:T(128)} %get-tuple-element.152), channel_id=1, replica_groups=mesh['img'=8,'txt'=32] {'img','txt'}, use_global_device_ids=true, to_apply=%region_24.25 | all-reduce | flops 2 | bytes 16 | tf_op jit(solution)/shard_map/psum | solution.py:113
  367.4 0.0 reduce-scatter.5.cloned.1.call-done
  367.4 1.1 fusion.43
  368.5 1.6 fusion.45
  370.1 170.0 %reduce-scatter.3.cloned.1.call-done = bf16[32,1280]{1,0:T(8,128)(2,1)} async-done(((bf16[1024,1280]{1,0:T(8,128)(2,1)}), bf16[32,1280]{1,0:T(8,128)(2,1)}) %reduce-scatter.3.cloned.1.call-update) | async-done | bytes 81936 | tf_op jit(solution)/shard_map/reduce_scatter | solution.py:101
  540.1 0.0 copy-done.3
  540.2 1.1 fusion.40
  541.2 1.6 fusion.42
  (36 shorter events, 0.4 us)
Async XLA Ops:
  7.2 85.9 %all-gather.2.cloned.1.call-start = ((), (), s32[]{:S(2)}) async-start(), calls=%async_computation.2 | async-start | bytes 2703360 | tf_op jit(solution)/shard_map/all_gather | solution.py:24
  9.9 357.5 %reduce-scatter.5.cloned.1.call-start = ((), (), s32[]{:S(2)}) async-start(), calls=%async_computation.4 | async-start | bytes 737280 | tf_op jit(solution)/shard_map/reduce_scatter | solution.py:104
  270.2 2.6 copy-start
  273.4 1.5 copy-start.1
  280.2 2.6 copy-start
  283.5 1.5 copy-start.1
  286.0 254.2 %reduce-scatter.3.cloned.1.call-start = ((), (), s32[]{:S(2)}) async-start(), calls=%async_computation.3 | async-start | bytes 2703360 | tf_op jit(solution)/shard_map/reduce_scatter | solution.py:101
  286.0 81.4 %copy-start.2 = (bf16[32,1280]{1,0:T(8,128)(2,1)S(1)}, bf16[32,1280]{1,0:T(8,128)(2,1)}, u32[]{:S(2)}) copy-start(bf16[32,1280]{1,0:T(8,128)(2,1)} %param.10) | copy-start | bytes 245764
  286.0 254.1 %copy-start.3 = (bf16[32,1280]{1,0:T(8,128)(2,1)S(1)}, bf16[32,1280]{1,0:T(8,128)(2,1)}, u32[]{:S(2)}) copy-start(bf16[32,1280]{1,0:T(8,128)(2,1)} %param.9) | copy-start | bytes 245764
Sparse Core Ops, SparseCore 0:
  11.2 81.8 all-gather.1
  286.1 30.2 reduce-scatter.4
  320.3 219.8 reduce-scatter.2
where the time goes:
time: 553 us; the launch traced here: 552 us
  blocking collectives  254 us (46%)
  waiting for transfers between devices  238 us (43%)
  matrix products  19.7 us (4%)
  between operations  19.4 us (4%)
  other arithmetic  13.7 us (2%)
    reduce_scatter x1, waiting for transfers between devices, shards(): lax.psum_scatter(img_terms.astype(jnp.bfloat16), 'txt', scatter_dimension...  170 us
    psum x1, blocking collectives, shards(): loss_sum, temp_total = lax.psum((local_loss, temp_sum), ('img', 'txt'))  76.7 us
    pmax x1, blocking collectives, shards(): lax.pmax(entrywise_maximum_along_line.reshape(tile_rows), 'txt')  72 us
    psum x1, blocking collectives, shards(): row_total = lax.psum(row_total.reshape(tile_rows), 'txt')  69.6 us
    all_gather x1, waiting for transfers between devices, shards(): lax.all_gather(img_dir.astype(jnp.bfloat16), 'txt', axis=0, tiled=True)  67.1 us
    all_gather x1, blocking collectives, shards(): lax.all_gather(txt_dir.astype(jnp.bfloat16), 'img', axis=0, tiled=True)  13.3 us
    dot_general x6, matrix products, logits_of(): jnp.einsum('rd,cd->rc', img_piece, txt_block, preferred_element_type=jnp....  13.2 us
    psum x1, blocking collectives, shards(): col_total = lax.psum(col_total, 'img')  11.9 us
  transfers between devices with their start and end apart: 3, of which 2 were waited for; matrix products, arithmetic and copies ran while one was open for 1% of the time, Pallas kernels for 0%

commit v1 on v0

v1 whole, which is shorter than its diff:
```python
import jax
import jax.numpy as jnp
from jax import lax
from jax.experimental import pallas as pl
from jax.experimental.pallas import tpu as pltpu
from jax.sharding import Mesh, PartitionSpec as P

F32 = jnp.float32
BF16 = jnp.bfloat16
NX, NC, NZ, NY = 4, 2, 8, 4
NXY = NX * NY
OWN = 32
TILE = 512
LANE = 128
NB = TILE // LANE
PAD = 128
VMEM_LIMIT = 48 * 1024 * 1024
PARAMS = pltpu.CompilerParams(vmem_limit_bytes=VMEM_LIMIT)


def inverse_norm(values):
    return lax.rsqrt(jnp.sum(values * values, axis=1, keepdims=True) + 1e-06)


def position():
    return lax.axis_index("x"), lax.axis_index("c"), lax.axis_index("z"), lax.axis_index("y")


def rows_at(start, size):
    return pl.ds(pl.multiple_of(start, size), size)


def normalize_kernel(pic_ref, cap_ref, img_ref, txt_ref):
    pic = pic_ref[...].astype(F32)
    img = (pic * inverse_norm(pic)).astype(BF16)
    for slot in range(NXY):
        img_ref[slot] = img
    cap = cap_ref[...].astype(F32)
    txt_ref[...] = (cap * inverse_norm(cap)).astype(BF16)


def scale_row(log_ref):
    return jnp.exp(jnp.full((1, LANE), log_ref[0], F32))


def pair_mask(j, q, x, c, z, y):
    row = lax.broadcasted_iota(jnp.int32, (LANE, 1), 0) + j * LANE
    col = lax.broadcasted_iota(jnp.int32, (1, LANE), 1) + q * LANE
    slot = row // OWN
    image = (((slot // NY) * NC + c) * (NZ * NY) + z * NY + slot % NY) * OWN + row % OWN
    part = col // OWN
    text = (((part % NZ) * NY + y) * (NX * NC) + x * NC + part // NZ) * OWN + col % OWN
    return image == text


def to_lanes(column):
    return jnp.transpose(jnp.broadcast_to(column, (LANE, LANE)))[0:1, :]


def logits_kernel(log_ref, img_ref, own_ref, other_ref, logit_ref, txt_ref, rowp_ref, colp_ref):
    x, c, z, y = position()
    for k in range(NZ):
        start = lax.rem(z - k + NZ, NZ) * OWN
        txt_ref[rows_at(c * (NZ * OWN) + start, OWN), :] = own_ref[k * OWN : (k + 1) * OWN, :]
        txt_ref[rows_at((1 - c) * (NZ * OWN) + start, OWN), :] = other_ref[k * OWN : (k + 1) * OWN, :]
    img = img_ref[...].reshape(TILE, img_ref.shape[2])
    scale = jnp.tile(scale_row(log_ref), (1, NB))
    logit_ref[...] = scale * lax.dot_general(
        img, txt_ref[...], (((1,), (1,)), ((), ())), preferred_element_type=F32
    )
    pos = jnp.zeros((LANE, LANE), F32)
    for j in range(NB):
        piece = logit_ref[j * LANE : (j + 1) * LANE, :]
        peak = jnp.max(piece, axis=1, keepdims=True)
        shifted = jnp.exp(piece - peak)
        total = jnp.sum(shifted, axis=1, keepdims=True)
        mean = to_lanes(jnp.sum(shifted * piece, axis=1, keepdims=True) / total)
        lse = to_lanes(peak + jnp.log(total))
        for slot in range(NXY):
            rowp_ref[slot, j : j + 1, :] = lse
            rowp_ref[slot, NB + j : NB + j + 1, :] = mean
        for q in range(NB):
            pos += jnp.where(pair_mask(j, q, x, c, z, y), piece[:, q * LANE : (q + 1) * LANE], 0.0)
    for q in range(NB):
        piece = logit_ref[:, q * LANE : (q + 1) * LANE]
        peak = jnp.max(piece, axis=0, keepdims=True)
        shifted = jnp.exp(piece - peak)
        total = jnp.sum(shifted, axis=0, keepdims=True)
        colp_ref[q : q + 1, :] = peak + jnp.log(total)
        colp_ref[NB + q : NB + q + 1, :] = jnp.sum(shifted * piece, axis=0, keepdims=True) / total
    pos = jnp.sum(pos, axis=0, keepdims=True)
    first = lax.broadcasted_iota(jnp.int32, (2 * NB, LANE), 0) == 0
    colp_ref[2 * NB :, :] = jnp.where(first, pos, 0.0)


def combine(lse, mean):
    peak = jnp.max(lse, axis=0)
    weight = jnp.exp(lse - peak)
    total = jnp.sum(weight, axis=0)
    return peak + jnp.log(total), jnp.sum(weight * mean, axis=0) / total


def all_sum(values):
    return jnp.sum(jnp.sum(values, axis=1, keepdims=True), axis=0, keepdims=True)


def scalar_block(source, loss_part, temp_part):
    lane = lax.broadcasted_iota(jnp.int32, (OWN, PAD), 1)
    row = lax.broadcasted_iota(jnp.int32, (OWN, PAD), 0)
    value = jnp.where(lane == source * 8, loss_part, jnp.where(lane == source * 8 + 1, temp_part, 0.0))
    high = value.astype(BF16).astype(F32)
    rest = value - high
    middle = rest.astype(BF16).astype(F32)
    low = rest - middle
    return jnp.where(row == 0, high, jnp.where(row == 1, middle, jnp.where(row == 2, low, 0.0))).astype(BF16)


def grad_kernel(log_ref, logit_ref, img_ref, txt_ref, rowg_ref, *refs):
    colg_refs = refs[:NZ]
    term_ref, keep_ref, send_ref, grad, gradt, colg = refs[NZ:]
    x, c, z, y = position()
    width = txt_ref.shape[1]
    for k in range(NZ):
        start = lax.rem(z - k + NZ, NZ)
        colg[c * NZ + start] = colg_refs[k][0]
        colg[(1 - c) * NZ + start] = colg_refs[k][1]
    row_lse, row_mean = combine(rowg_ref[:, :NB, :], rowg_ref[:, NB:, :])
    col_lse, col_mean = combine(colg[:, :NB, :], colg[:, NB : 2 * NB, :])
    pos = all_sum(jnp.sum(colg[:, 2 * NB :, :], axis=0))
    row_block = scalar_block(z * NC + c, all_sum(row_lse), 0.5 * all_sum(row_mean))
    col_block = scalar_block(x * NY + y, all_sum(col_lse) - 2.0 * pos, 0.5 * all_sum(col_mean) - pos)
    for j in range(NB):
        line = jnp.transpose(jnp.broadcast_to(row_lse[j : j + 1, :], (LANE, LANE)))
        for q in range(NB):
            piece = logit_ref[j * LANE : (j + 1) * LANE, q * LANE : (q + 1) * LANE]
            pair = pair_mask(j, q, x, c, z, y)
            weight = 0.5 * (jnp.exp(piece - line) + jnp.exp(piece - col_lse[q : q + 1, :]))
            weight = weight - jnp.where(pair, 1.0, 0.0)
            grad[j * LANE : (j + 1) * LANE, q * LANE : (q + 1) * LANE] = weight.astype(BF16)
            gradt[q * LANE : (q + 1) * LANE, j * LANE : (j + 1) * LANE] = jnp.transpose(weight).astype(BF16)
    scale = scale_row(log_ref)
    step = 2 * LANE
    scale = jnp.tile(scale, (1, 2))
    half = NZ * OWN
    for start in range(0, width, step):
        span = slice(start, start + step)
        img = img_ref[:, :, span].reshape(TILE, step)
        keep_ref[:, span] = (
            scale * jnp.dot(gradt[rows_at(c * half, half), :], img, preferred_element_type=F32)
        ).astype(BF16)
        send_ref[:, span] = (
            scale * jnp.dot(gradt[rows_at((1 - c) * half, half), :], img, preferred_element_type=F32)
        ).astype(BF16)
        term_ref[:, :, span] = (
            (scale * jnp.dot(grad[...], txt_ref[:, span], preferred_element_type=F32))
            .astype(BF16)
            .reshape(NXY, OWN, step)
        )
    for slot in range(NXY):
        term_ref[slot, :, width:] = col_block
    for k in range(NZ):
        keep_ref[k * OWN : (k + 1) * OWN, width:] = row_block
        send_ref[k * OWN : (k + 1) * OWN, width:] = row_block


def add_kernel(keep_ref, other_ref, *out_refs):
    z = lax.axis_index("z")
    for k in range(NZ):
        rows = rows_at(lax.rem(z + k, NZ) * OWN, OWN)
        out_refs[k][...] = (keep_ref[rows, :].astype(F32) + other_ref[rows, :].astype(F32)).astype(BF16)


def unit_backward(values, gradient):
    inverse = inverse_norm(values)
    direction = values * inverse
    inner = jnp.sum(direction * gradient, axis=1, keepdims=True)
    return ((gradient - direction * inner) * inverse).astype(BF16)


def final_kernel(pic_ref, cap_ref, term_ref, *refs):
    part_refs = refs[:NZ]
    gpic_ref, gcap_ref, loss_ref, temp_ref = refs[NZ:]
    width = pic_ref.shape[1]
    img = term_ref[0].astype(F32)
    for slot in range(1, NXY):
        img += term_ref[slot].astype(F32)
    txt = part_refs[0][...].astype(F32)
    for ref in part_refs[1:]:
        txt += ref[...].astype(F32)
    gpic_ref[...] = unit_backward(pic_ref[...].astype(F32), img[:, :width])
    gcap_ref[...] = unit_backward(cap_ref[...].astype(F32), txt[:, :width])
    scalars = jnp.sum(img[:8, width:], axis=0, keepdims=True) + jnp.sum(txt[:8, width:], axis=0, keepdims=True)
    lane = lax.broadcasted_iota(jnp.int32, (1, PAD), 1) % 8
    pairs = TILE * NXY
    loss_ref[0] = jnp.sum(jnp.where(lane == 0, scalars, 0.0)) / (2 * pairs)
    temp_ref[0] = jnp.sum(jnp.where(lane == 1, scalars, 0.0)) / pairs


def shape(dims, dtype):
    return jax.ShapeDtypeStruct(dims, dtype)


def shift(values, k):
    return lax.ppermute(values, "z", [(i, (i + k) % NZ) for i in range(NZ)])


def swap(values):
    return lax.ppermute(values, "c", [(0, 1), (1, 0)])


def exchange(values):
    return lax.all_to_all(values, ("x", "y"), 0, 0, tiled=True)


VM = pl.BlockSpec(memory_space=pltpu.VMEM)
SM = pl.BlockSpec(memory_space=pltpu.SMEM)


def call(kernel, out_shape, in_specs, out_specs=None, scratch=()):
    return pl.pallas_call(
        kernel,
        out_shape=out_shape,
        in_specs=in_specs,
        out_specs=out_specs if out_specs is not None else [VM] * len(out_shape),
        scratch_shapes=scratch,
        compiler_params=PARAMS,
    )


def shards(pic, cap, log_scale):
    width = pic.shape[1]
    wide = width + PAD
    half = NZ * OWN
    img_out, txt_own = call(
        normalize_kernel,
        [shape((NXY, OWN, width), BF16), shape((OWN, width), BF16)],
        [VM, VM],
    )(pic, cap)
    img = exchange(img_out)
    own = jnp.concatenate([txt_own] + [shift(txt_own, k) for k in range(1, NZ)], axis=0)
    other = swap(own)
    logits, txt, rowp, colp = call(
        logits_kernel,
        [
            shape((TILE, TILE), F32),
            shape((TILE, width), BF16),
            shape((NXY, 2 * NB, LANE), F32),
            shape((4 * NB, LANE), F32),
        ],
        [SM, VM, VM, VM],
    )(log_scale, img, own, other)
    rowg = exchange(rowp)
    colp = jnp.stack([colp, swap(colp)])
    colg = [colp] + [shift(colp, k) for k in range(1, NZ)]
    terms, keep, send = call(
        grad_kernel,
        [shape((NXY, OWN, wide), BF16), shape((half, wide), BF16), shape((half, wide), BF16)],
        [SM] + [VM] * (4 + NZ),
        scratch=[
            pltpu.VMEM((TILE, TILE), BF16),
            pltpu.VMEM((TILE, TILE), BF16),
            pltpu.VMEM((NC * NZ, 4 * NB, LANE), F32),
        ],
    )(log_scale, logits, img, txt, rowg, *colg)
    terms = exchange(terms)
    parts = call(add_kernel, [shape((OWN, wide), BF16)] * NZ, [VM, VM])(keep, swap(send))
    parts = [parts[0]] + [shift(parts[k], k) for k in range(1, NZ)]
    return call(
        final_kernel,
        [shape((OWN, width), BF16), shape((OWN, width), BF16), shape((1,), F32), shape((1,), F32)],
        [VM] * (3 + NZ),
        [VM, VM, SM, SM],
    )(pic, cap, terms, *parts)


def solution(mesh):
    grid = Mesh(mesh.devices.reshape(NX, NC, NZ, NY), ("x", "c", "z", "y"))
    rows = P(("x", "c", "z", "y"), None)
    columns = P(("z", "y", "x", "c"), None)
    return jax.shard_map(
        shards,
        mesh=grid,
        in_specs=(rows, columns, P()),
        out_specs=(rows, columns, P(), P()),
        check_vma=False,
    )
```

time: 553 us -> 113 us (0.20)
  blocking collectives: 254 us -> 0 us
  waiting for transfers between devices: 238 us -> 32.1 us
  starting transfers between devices: 0.12 us -> 63.2 us
  matrix products: 19.7 us -> 0 us
  between operations: 19.4 us -> 1.63 us
  other arithmetic: 13.7 us -> 0.01 us
  Pallas kernels: 0 us -> 8.4 us
    reduce_scatter x2 -> x0, waiting for transfers between devices: 170 us -> none  [the longest x1 170 us: shards(): lax.psum_scatter(img_terms.astype(jnp.bfloat16), 'txt', scatter_dimension...]
    psum x3 -> x0, blocking collectives: 158 us -> none  [the longest x1 76.7 us: shards(): loss_sum, temp_total = lax.psum((local_loss, temp_sum), ('img', 'txt'))]
    pmax x2 -> x0, blocking collectives: 82 us -> none  [the longest x1 72 us: shards(): lax.pmax(entrywise_maximum_along_line.reshape(tile_rows), 'txt')]
    all_gather x1 -> x0, waiting for transfers between devices: 67.1 us -> none  [shards(): lax.all_gather(img_dir.astype(jnp.bfloat16), 'txt', axis=0, tiled=True)]
    ppermute x0 -> x24, starting transfers between devices: none -> 41.1 us  [the longest x21 40.8 us: shift(): return lax.ppermute(values, 'z', [(i, (i + k) % NZ) for i in range(NZ)])]
    ppermute x0 -> x24, waiting for transfers between devices: none -> 32.1 us  [the longest x21 28.5 us: shift(): return lax.ppermute(values, 'z', [(i, (i + k) % NZ) for i in range(NZ)])]
    all_to_all x0 -> x3, starting transfers between devices: none -> 22.1 us  [exchange(): return lax.all_to_all(values, ('x', 'y'), 0, 0, tiled=True)]
    dot_general x10 -> x0, matrix products: 19.7 us -> none  [the longest x6 13.2 us: logits_of(): jnp.einsum('rd,cd->rc', img_piece, txt_block, preferred_element_type=jnp....]
  transfers between devices with their start and end apart: 3 -> 27, of which waited for: 2 -> 12; matrix products, arithmetic and copies ran while one was open for 1% -> 0% of each run, Pallas kernels for 0% -> 0%
where the time goes in v1:
time: 113 us; the launch traced here: 112 us
  starting transfers between devices  63.2 us (56%)
  waiting for transfers between devices  32.1 us (28%)
  Pallas kernels  8.4 us (7%)
  local copies, waits for them, and re-layouts  6.86 us (6%)
  between operations  1.63 us (1%)
    ppermute x21, starting transfers between devices, shift(): return lax.ppermute(values, 'z', [(i, (i + k) % NZ) for i in range(NZ)])  40.8 us
    ppermute x21, waiting for transfers between devices, shift(): return lax.ppermute(values, 'z', [(i, (i + k) % NZ) for i in range(NZ)])  28.5 us
    all_to_all x3, starting transfers between devices, exchange(): return lax.all_to_all(values, ('x', 'y'), 0, 0, tiled=True)  22.1 us
    unnamed x27, local copies, waits for them, and re-layouts  6.85 us
    ppermute x3, waiting for transfers between devices, swap(): return lax.ppermute(values, 'c', [(0, 1), (1, 0)])  3.62 us
    pallas_call x1, Pallas kernels, shards(): call(grad_kernel, [shape((NXY, OWN, wide), BF16), shape((half, wide), BF1...  3.38 us
    pallas_call x1, Pallas kernels, shards(): call(logits_kernel, [shape((TILE, TILE), F32), shape((TILE, width), BF16)...  2.5 us
  transfers between devices with their start and end apart: 27, of which 12 were waited for; matrix products, arithmetic and copies ran while one was open for 0% of the time, Pallas kernels for 0%

profile of v1, /device:TPU:2, one launch (start us, length us, event | category | flops | bytes accessed | tf_op | source)
XLA Modules:
  0.0 112.2 jit_solution(6894390342642965930)
XLA Ops:
  0.6 0.9 copy-done.4
  1.5 0.9 copy-done.6
  2.4 1.3 %shard_map.66 = (bf16[16,32,1280]{2,1,0:T(8,128)(2,1)}, bf16[32,1280]{1,0:T(8,128)(2,1)S(1)}) custom-call(bf16[32,1280]{1,0:T(8,128)(2,1)S(1)} %copy-done.4, bf16[32,1280]{1,0:T(8,128)(2,1)S(1)} %copy-done.6), custom_call_target="tpu_custom_call" | custom-call | tf_op jit(solution)/shard_map/pallas_call | solution.py:234
  3.7 5.9 %collective-permute-start.6 = (bf16[32,1280]{1,0:T(8,128)(2,1)S(1)}, bf16[32,1280]{1,0:T(8,128)(2,1)S(1)}, u32[]{:S(2)}, u32[]{:S(2)}) collective-permute-start(bf16[32,1280]{1,0:T(8,128)(2,1)S(1)} %get-tuple-element.22), channel_id=1, source_target_pairs={{0,28},{4,0},{8,4},{12,8},{16,12},{20,16},{24,20},{28,24},{1,29},{... | collective-permute-start | bytes 245768 | tf_op jit(solution)/shard_map/ppermute | solution.py:204
  9.6 1.5 %collective-permute-start.5 = (bf16[32,1280]{1,0:T(8,128)(2,1)S(1)}, bf16[32,1280]{1,0:T(8,128)(2,1)S(1)}, u32[]{:S(2)}, u32[]{:S(2)}) collective-permute-start(bf16[32,1280]{1,0:T(8,128)(2,1)S(1)} %get-tuple-element.22), channel_id=1, source_target_pairs={{0,24},{4,28},{8,0},{12,4},{16,8},{20,12},{24,16},{28,20},{1,25},{... | collective-permute-start | bytes 245768 | tf_op jit(solution)/shard_map/ppermute | solution.py:204
  11.0 0.4 collective-permute-start.4
  11.5 5.0 %collective-permute-start.3 = (bf16[32,1280]{1,0:T(8,128)(2,1)S(1)}, bf16[32,1280]{1,0:T(8,128)(2,1)S(1)}, u32[]{:S(2)}, u32[]{:S(2)}) collective-permute-start(bf16[32,1280]{1,0:T(8,128)(2,1)S(1)} %get-tuple-element.22), channel_id=1, source_target_pairs={{0,16},{4,20},{8,24},{12,28},{16,0},{20,4},{24,8},{28,12},{1,17},{... | collective-permute-start | bytes 245768 | tf_op jit(solution)/shard_map/ppermute | solution.py:204
  16.5 1.0 collective-permute-start
  17.5 7.5 %all-to-all-start = ((bf16[16,32,1280]{2,1,0:T(8,128)(2,1)}), bf16[16,32,1280]{2,1,0:T(8,128)(2,1)S(1)}, u32[]{:S(2)}, u32[]{:S(2)}) async-start(bf16[16,32,1280]{2,1,0:T(8,128)(2,1)} %get-tuple-element.21), calls=%async_computation | async-start | bytes 2621440 | tf_op jit(solution)/shard_map/all_to_all | solution.py:212
  25.1 6.6 %collective-permute-done.1 = bf16[32,1280]{1,0:T(8,128)(2,1)S(1)} collective-permute-done((bf16[32,1280]{1,0:T(8,128)(2,1)S(1)}, bf16[32,1280]{1,0:T(8,128)(2,1)S(1)}, u32[]{:S(2)}, u32[]{:S(2)}) %collective-permute-start.1) | collective-permute-done | bytes 81952 | tf_op jit(solution)/shard_map/ppermute | solution.py:204
  31.8 8.8 %collective-permute-done.2 = bf16[32,1280]{1,0:T(8,128)(2,1)S(1)} collective-permute-done((bf16[32,1280]{1,0:T(8,128)(2,1)S(1)}, bf16[32,1280]{1,0:T(8,128)(2,1)S(1)}, u32[]{:S(2)}, u32[]{:S(2)}) %collective-permute-start.2) | collective-permute-done | bytes 81952 | tf_op jit(solution)/shard_map/ppermute | solution.py:204
  40.6 0.1 collective-permute-start.7
  41.4 1.4 %collective-permute-done.7.other_ref = bf16[256,1280]{1,0:T(8,128)(2,1)S(1)} collective-permute-done((bf16[256,1280]{1,0:T(8,128)(2,1)S(1)}, bf16[256,1280]{1,0:T(8,128)(2,1)S(1)}, u32[]{:S(2)}, u32[]{:S(2)}) %collective-permute-start.7) | collective-permute-done | bytes 655392 | tf_op jit(solution)/shard_map/ppermute | solution.py:208
  42.8 0.8 copy-done.2
  43.7 1.1 copy-done.3
  44.7 2.5 %shard_map.67 = (f32[512,512]{1,0:T(8,128)S(1)}, bf16[512,1280]{1,0:T(8,128)(2,1)S(1)}, f32[16,8,128]{2,1,0:T(8,128)}, f32[16,128]{1,0:T(8,128)S(1)}) custom-call(f32[1]{0:T(128)S(6)} %copy.14.log_ref, bf16[16,32,1280]{2,1,0:T(8,128)(2,1)S(1)} %all-to-all-done.img_ref, bf16[256,1280]{1,0:T(8,128)(2,1)S(1)} %constant_dynamic-update-slice_fusion.own_ref, ...), custom_call_target="tpu_custom_call" | custom-call | tf_op jit(solution)/shard_map/pallas_call | solution.py:242
  47.2 1.0 copy-done
  48.2 0.1 collective-permute-start.8
  48.4 7.2 %all-to-all-start.1 = ((f32[16,8,128]{2,1,0:T(8,128)}), f32[16,8,128]{2,1,0:T(8,128)S(1)}, u32[]{:S(2)}, u32[]{:S(2)}) async-start(f32[16,8,128]{2,1,0:T(8,128)} %get-tuple-element.25), calls=%async_computation.1 | async-start | bytes 131072 | tf_op jit(solution)/shard_map/all_to_all | solution.py:212
  55.6 0.1 collective-permute-start.15
  55.7 2.7 %collective-permute-start.14 = (f32[2,16,128]{2,1,0:T(8,128)S(1)}, f32[2,16,128]{2,1,0:T(8,128)S(1)}, u32[]{:S(2)}, u32[]{:S(2)}) collective-permute-start(f32[2,16,128]{2,1,0:T(8,128)S(1)} %pad_maximum_fusion.refs_0_), channel_id=1, source_target_pairs={{0,24},{4,28},{8,0},{12,4},{16,8},{20,12},{24,16},{28,20},{1,25},{... | collective-permute-start | bytes 49160 | tf_op jit(solution)/shard_map/ppermute | solution.py:204
  58.4 3.8 %collective-permute-start.12 = (f32[2,16,128]{2,1,0:T(8,128)S(1)}, f32[2,16,128]{2,1,0:T(8,128)S(1)}, u32[]{:S(2)}, u32[]{:S(2)}) collective-permute-start(f32[2,16,128]{2,1,0:T(8,128)S(1)} %pad_maximum_fusion.refs_0_), channel_id=1, source_target_pairs={{0,16},{4,20},{8,24},{12,28},{16,0},{20,4},{24,8},{28,12},{1,17},{... | collective-permute-start | bytes 49160 | tf_op jit(solution)/shard_map/ppermute | solution.py:204
  62.2 1.1 collective-permute-start.11
  63.3 2.5 %collective-permute-start.10 = (f32[2,16,128]{2,1,0:T(8,128)S(1)}, f32[2,16,128]{2,1,0:T(8,128)S(1)}, u32[]{:S(2)}, u32[]{:S(2)}) collective-permute-start(f32[2,16,128]{2,1,0:T(8,128)S(1)} %pad_maximum_fusion.refs_0_), channel_id=1, source_target_pairs={{0,8},{4,12},{8,16},{12,20},{16,24},{20,28},{24,0},{28,4},{1,9},{5... | collective-permute-start | bytes 49160 | tf_op jit(solution)/shard_map/ppermute | solution.py:204
  65.8 1.6 %collective-permute-start.9 = (f32[2,16,128]{2,1,0:T(8,128)S(1)}, f32[2,16,128]{2,1,0:T(8,128)S(1)}, u32[]{:S(2)}, u32[]{:S(2)}) collective-permute-start(f32[2,16,128]{2,1,0:T(8,128)S(1)} %pad_maximum_fusion.refs_0_), channel_id=1, source_target_pairs={{0,4},{4,8},{8,12},{12,16},{16,20},{20,24},{24,28},{28,0},{1,5},{5... | collective-permute-start | bytes 49160 | tf_op jit(solution)/shard_map/ppermute | solution.py:204
  67.3 1.9 %collective-permute-done.11.refs_3_ = f32[2,16,128]{2,1,0:T(8,128)S(1)} collective-permute-done((f32[2,16,128]{2,1,0:T(8,128)S(1)}, f32[2,16,128]{2,1,0:T(8,128)S(1)}, u32[]{:S(2)}, u32[]{:S(2)}) %collective-permute-start.11) | collective-permute-done | bytes 16416 | tf_op jit(solution)/shard_map/ppermute | solution.py:204
  69.3 0.4 collective-permute-done.10.refs_2_
  69.6 1.1 collective-permute-done.9.refs_1_
  70.7 1.2 %copy-done.1 = f32[512,512]{1,0:T(8,128)S(1)} copy-done((f32[512,512]{1,0:T(8,128)S(1)}, f32[512,512]{1,0:T(8,128)}, u32[]{:S(2)}) %copy-start.1) | copy-done | bytes 1048600
  72.0 3.4 %shard_map.68 = (bf16[16,32,1408]{2,1,0:T(8,128)(2,1)}, bf16[256,1408]{1,0:T(8,128)(2,1)S(1)}, bf16[256,1408]{1,0:T(8,128)(2,1)S(1)}) custom-call(f32[1]{0:T(128)S(6)} %copy.14.log_ref, f32[512,512]{1,0:T(8,128)S(1)} %copy-done.1, bf16[16,32,1280]{2,1,0:T(8,128)(2,1)S(1)} %all-to-all-done.img_ref, bf16[512,1280]{1,0:T(8,128)(2,1)S(1)} %get-tuple-element.24.txt_ref, ...), custom_call_target="tpu_custom_call" | custom-call | tf_op jit(solution)/shard_map/pallas_call | solution.py:255
  75.3 0.9 copy-done.8
  76.2 7.4 %all-to-all-start.2 = ((bf16[16,32,1408]{2,1,0:T(8,128)(2,1)}), bf16[16,32,1408]{2,1,0:T(8,128)(2,1)S(1)}, u32[]{:S(2)}, u32[]{:S(2)}) async-start(bf16[16,32,1408]{2,1,0:T(8,128)(2,1)} %get-tuple-element.27), calls=%async_computation.2 | async-start | bytes 2883584 | tf_op jit(solution)/shard_map/all_to_all | solution.py:212
  83.6 0.1 collective-permute-start.16
  83.7 2.2 %collective-permute-done.16.other_ref = bf16[256,1408]{1,0:T(8,128)(2,1)S(1)} collective-permute-done((bf16[256,1408]{1,0:T(8,128)(2,1)S(1)}, bf16[256,1408]{1,0:T(8,128)(2,1)S(1)}, u32[]{:S(2)}, u32[]{:S(2)}) %collective-permute-start.16) | collective-permute-done | bytes 720928 | tf_op jit(solution)/shard_map/ppermute | solution.py:208
  85.9 0.2 shard_map.69
  86.1 0.7 collective-permute-start.17
  86.7 1.7 %collective-permute-start.18 = (bf16[32,1408]{1,0:T(8,128)(2,1)S(1)}, bf16[32,1408]{1,0:T(8,128)(2,1)S(1)}, u32[]{:S(2)}, u32[]{:S(2)}) collective-permute-start(bf16[32,1408]{1,0:T(8,128)(2,1)S(1)} %get-tuple-element.32), channel_id=1, source_target_pairs={{0,8},{4,12},{8,16},{12,20},{16,24},{20,28},{24,0},{28,4},{1,9},{5... | collective-permute-start | bytes 270344 | tf_op jit(solution)/shard_map/ppermute | solution.py:204
  88.4 2.5 %collective-permute-start.19 = (bf16[32,1408]{1,0:T(8,128)(2,1)S(1)}, bf16[32,1408]{1,0:T(8,128)(2,1)S(1)}, u32[]{:S(2)}, u32[]{:S(2)}) collective-permute-start(bf16[32,1408]{1,0:T(8,128)(2,1)S(1)} %get-tuple-element.33), channel_id=1, source_target_pairs={{0,12},{4,16},{8,20},{12,24},{16,28},{20,0},{24,4},{28,8},{1,13},{... | collective-permute-start | bytes 270344 | tf_op jit(solution)/shard_map/ppermute | solution.py:204
  90.9 3.4 %collective-permute-start.20 = (bf16[32,1408]{1,0:T(8,128)(2,1)S(1)}, bf16[32,1408]{1,0:T(8,128)(2,1)S(1)}, u32[]{:S(2)}, u32[]{:S(2)}) collective-permute-start(bf16[32,1408]{1,0:T(8,128)(2,1)S(1)} %get-tuple-element.34), channel_id=1, source_target_pairs={{0,16},{4,20},{8,24},{12,28},{16,0},{20,4},{24,8},{28,12},{1,17},{... | collective-permute-start | bytes 270344 | tf_op jit(solution)/shard_map/ppermute | solution.py:204
  94.3 2.4 %collective-permute-start.21 = (bf16[32,1408]{1,0:T(8,128)(2,1)S(1)}, bf16[32,1408]{1,0:T(8,128)(2,1)S(1)}, u32[]{:S(2)}, u32[]{:S(2)}) collective-permute-start(bf16[32,1408]{1,0:T(8,128)(2,1)S(1)} %get-tuple-element.35), channel_id=1, source_target_pairs={{0,20},{4,24},{8,28},{12,0},{16,4},{20,8},{24,12},{28,16},{1,21},{... | collective-permute-start | bytes 270344 | tf_op jit(solution)/shard_map/ppermute | solution.py:204
  96.7 3.2 %collective-permute-start.22 = (bf16[32,1408]{1,0:T(8,128)(2,1)S(1)}, bf16[32,1408]{1,0:T(8,128)(2,1)S(1)}, u32[]{:S(2)}, u32[]{:S(2)}) collective-permute-start(bf16[32,1408]{1,0:T(8,128)(2,1)S(1)} %get-tuple-element.36), channel_id=1, source_target_pairs={{0,24},{4,28},{8,0},{12,4},{16,8},{20,12},{24,16},{28,20},{1,25},{... | collective-permute-start | bytes 270344 | tf_op jit(solution)/shard_map/ppermute | solution.py:204
  100.0 1.3 %collective-permute-start.23 = (bf16[32,1408]{1,0:T(8,128)(2,1)S(1)}, bf16[32,1408]{1,0:T(8,128)(2,1)S(1)}, u32[]{:S(2)}, u32[]{:S(2)}) collective-permute-start(bf16[32,1408]{1,0:T(8,128)(2,1)S(1)} %get-tuple-element.37), channel_id=1, source_target_pairs={{0,28},{4,0},{8,4},{12,8},{16,12},{20,16},{24,20},{28,24},{1,29},{... | collective-permute-start | bytes 270344 | tf_op jit(solution)/shard_map/ppermute | solution.py:204
  101.3 0.8 collective-permute-done.19.refs_3_
  102.1 1.9 %collective-permute-done.20.refs_4_ = bf16[32,1408]{1,0:T(8,128)(2,1)S(1)} collective-permute-done((bf16[32,1408]{1,0:T(8,128)(2,1)S(1)}, bf16[32,1408]{1,0:T(8,128)(2,1)S(1)}, u32[]{:S(2)}, u32[]{:S(2)}) %collective-permute-start.20) | collective-permute-done | bytes 90144 | tf_op jit(solution)/shard_map/ppermute | solution.py:204
  104.0 3.5 %collective-permute-done.21.refs_5_ = bf16[32,1408]{1,0:T(8,128)(2,1)S(1)} collective-permute-done((bf16[32,1408]{1,0:T(8,128)(2,1)S(1)}, bf16[32,1408]{1,0:T(8,128)(2,1)S(1)}, u32[]{:S(2)}, u32[]{:S(2)}) %collective-permute-start.21) | collective-permute-done | bytes 90144 | tf_op jit(solution)/shard_map/ppermute | solution.py:204
  107.5 2.9 %collective-permute-done.22.refs_6_ = bf16[32,1408]{1,0:T(8,128)(2,1)S(1)} collective-permute-done((bf16[32,1408]{1,0:T(8,128)(2,1)S(1)}, bf16[32,1408]{1,0:T(8,128)(2,1)S(1)}, u32[]{:S(2)}, u32[]{:S(2)}) %collective-permute-start.22) | collective-permute-done | bytes 90144 | tf_op jit(solution)/shard_map/ppermute | solution.py:204
  110.4 0.6 collective-permute-done.23.refs_7_
  111.0 1.1 shard_map.70
  (40 shorter events, 0.2 us)
Async XLA Ops:
  0.6 0.9 copy-start.4
  1.5 0.9 copy-start.6
  3.7 36.9 %collective-permute-start.6 = (bf16[32,1280]{1,0:T(8,128)(2,1)S(1)}, bf16[32,1280]{1,0:T(8,128)(2,1)S(1)}, u32[]{:S(2)}, u32[]{:S(2)}) collective-permute-start(bf16[32,1280]{1,0:T(8,128)(2,1)S(1)} %get-tuple-element.22), channel_id=1, source_target_pairs={{0,28},{4,0},{8,4},{12,8},{16,12},{20,16},{24,20},{28,24},{1,29},{... | collective-permute-start | bytes 245768 | tf_op jit(solution)/shard_map/ppermute | solution.py:204
  9.6 31.0 %collective-permute-start.5 = (bf16[32,1280]{1,0:T(8,128)(2,1)S(1)}, bf16[32,1280]{1,0:T(8,128)(2,1)S(1)}, u32[]{:S(2)}, u32[]{:S(2)}) collective-permute-start(bf16[32,1280]{1,0:T(8,128)(2,1)S(1)} %get-tuple-element.22), channel_id=1, source_target_pairs={{0,24},{4,28},{8,0},{12,4},{16,8},{20,12},{24,16},{28,20},{1,25},{... | collective-permute-start | bytes 245768 | tf_op jit(solution)/shard_map/ppermute | solution.py:204
  11.0 29.5 %collective-permute-start.4 = (bf16[32,1280]{1,0:T(8,128)(2,1)S(1)}, bf16[32,1280]{1,0:T(8,128)(2,1)S(1)}, u32[]{:S(2)}, u32[]{:S(2)}) collective-permute-start(bf16[32,1280]{1,0:T(8,128)(2,1)S(1)} %get-tuple-element.22), channel_id=1, source_target_pairs={{0,20},{4,24},{8,28},{12,0},{16,4},{20,8},{24,12},{28,16},{1,21},{... | collective-permute-start | bytes 245768 | tf_op jit(solution)/shard_map/ppermute | solution.py:204
  11.5 29.1 %collective-permute-start.3 = (bf16[32,1280]{1,0:T(8,128)(2,1)S(1)}, bf16[32,1280]{1,0:T(8,128)(2,1)S(1)}, u32[]{:S(2)}, u32[]{:S(2)}) collective-permute-start(bf16[32,1280]{1,0:T(8,128)(2,1)S(1)} %get-tuple-element.22), channel_id=1, source_target_pairs={{0,16},{4,20},{8,24},{12,28},{16,0},{20,4},{24,8},{28,12},{1,17},{... | collective-permute-start | bytes 245768 | tf_op jit(solution)/shard_map/ppermute | solution.py:204
  16.5 8.5 %collective-permute-start = (bf16[32,1280]{1,0:T(8,128)(2,1)S(1)}, bf16[32,1280]{1,0:T(8,128)(2,1)S(1)}, u32[]{:S(2)}, u32[]{:S(2)}) collective-permute-start(bf16[32,1280]{1,0:T(8,128)(2,1)S(1)} %get-tuple-element.22), channel_id=1, source_target_pairs={{0,4},{4,8},{8,12},{12,16},{16,20},{20,24},{24,28},{28,0},{1,5},{5... | collective-permute-start | bytes 245768 | tf_op jit(solution)/shard_map/ppermute | solution.py:204
  17.5 26.1 %all-to-all-start = ((bf16[16,32,1280]{2,1,0:T(8,128)(2,1)}), bf16[16,32,1280]{2,1,0:T(8,128)(2,1)S(1)}, u32[]{:S(2)}, u32[]{:S(2)}) async-start(bf16[16,32,1280]{2,1,0:T(8,128)(2,1)} %get-tuple-element.21), calls=%async_computation | async-start | bytes 2621440 | tf_op jit(solution)/shard_map/all_to_all | solution.py:212
  25.0 6.7 %collective-permute-start.1 = (bf16[32,1280]{1,0:T(8,128)(2,1)S(1)}, bf16[32,1280]{1,0:T(8,128)(2,1)S(1)}, u32[]{:S(2)}, u32[]{:S(2)}) collective-permute-start(bf16[32,1280]{1,0:T(8,128)(2,1)S(1)} %get-tuple-element.22), channel_id=1, source_target_pairs={{0,8},{4,12},{8,16},{12,20},{16,24},{20,28},{24,0},{28,4},{1,9},{5... | collective-permute-start | bytes 245768 | tf_op jit(solution)/shard_map/ppermute | solution.py:204
  31.7 8.8 %collective-permute-start.2 = (bf16[32,1280]{1,0:T(8,128)(2,1)S(1)}, bf16[32,1280]{1,0:T(8,128)(2,1)S(1)}, u32[]{:S(2)}, u32[]{:S(2)}) collective-permute-start(bf16[32,1280]{1,0:T(8,128)(2,1)S(1)} %get-tuple-element.22), channel_id=1, source_target_pairs={{0,12},{4,16},{8,20},{12,24},{16,28},{20,0},{24,4},{28,8},{1,13},{... | collective-permute-start | bytes 245768 | tf_op jit(solution)/shard_map/ppermute | solution.py:204
  40.6 2.2 %collective-permute-start.7 = (bf16[256,1280]{1,0:T(8,128)(2,1)S(1)}, bf16[256,1280]{1,0:T(8,128)(2,1)S(1)}, u32[]{:S(2)}, u32[]{:S(2)}) collective-permute-start(bf16[256,1280]{1,0:T(8,128)(2,1)S(1)} %constant_dynamic-update-slice_fusion.own_ref), channel_id=1, source_target_pairs={{0,32},{32,0},{1,33},{33,1},{2,34},{34,2},{3,35},{35,3},{4,36},{36... | collective-permute-start | bytes 1966088 | tf_op jit(solution)/shard_map/ppermute | solution.py:208
  42.8 0.8 copy-start.2
  43.6 1.1 copy-start.3
  47.2 1.0 copy-start
  48.2 7.4 %collective-permute-start.8 = (f32[16,128]{1,0:T(8,128)S(1)}, f32[16,128]{1,0:T(8,128)S(1)}, u32[]{:S(2)}, u32[]{:S(2)}) collective-permute-start(f32[16,128]{1,0:T(8,128)S(1)} %get-tuple-element.26), channel_id=1, source_target_pairs={{0,32},{32,0},{1,33},{33,1},{2,34},{34,2},{3,35},{35,3},{4,36},{36... | collective-permute-start | bytes 24584 | tf_op jit(solution)/shard_map/ppermute | solution.py:208
  48.4 22.4 %all-to-all-start.1 = ((f32[16,8,128]{2,1,0:T(8,128)}), f32[16,8,128]{2,1,0:T(8,128)S(1)}, u32[]{:S(2)}, u32[]{:S(2)}) async-start(f32[16,8,128]{2,1,0:T(8,128)} %get-tuple-element.25), calls=%async_computation.1 | async-start | bytes 131072 | tf_op jit(solution)/shard_map/all_to_all | solution.py:212
  55.6 7.6 %collective-permute-start.15 = (f32[2,16,128]{2,1,0:T(8,128)S(1)}, f32[2,16,128]{2,1,0:T(8,128)S(1)}, u32[]{:S(2)}, u32[]{:S(2)}) collective-permute-start(f32[2,16,128]{2,1,0:T(8,128)S(1)} %pad_maximum_fusion.refs_0_), channel_id=1, source_target_pairs={{0,28},{4,0},{8,4},{12,8},{16,12},{20,16},{24,20},{28,24},{1,29},{... | collective-permute-start | bytes 49160 | tf_op jit(solution)/shard_map/ppermute | solution.py:204
  55.7 10.1 %collective-permute-start.14 = (f32[2,16,128]{2,1,0:T(8,128)S(1)}, f32[2,16,128]{2,1,0:T(8,128)S(1)}, u32[]{:S(2)}, u32[]{:S(2)}) collective-permute-start(f32[2,16,128]{2,1,0:T(8,128)S(1)} %pad_maximum_fusion.refs_0_), channel_id=1, source_target_pairs={{0,24},{4,28},{8,0},{12,4},{16,8},{20,12},{24,16},{28,20},{1,25},{... | collective-permute-start | bytes 49160 | tf_op jit(solution)/shard_map/ppermute | solution.py:204
  58.4 9.0 %collective-permute-start.13 = (f32[2,16,128]{2,1,0:T(8,128)S(1)}, f32[2,16,128]{2,1,0:T(8,128)S(1)}, u32[]{:S(2)}, u32[]{:S(2)}) collective-permute-start(f32[2,16,128]{2,1,0:T(8,128)S(1)} %pad_maximum_fusion.refs_0_), channel_id=1, source_target_pairs={{0,20},{4,24},{8,28},{12,0},{16,4},{20,8},{24,12},{28,16},{1,21},{... | collective-permute-start | bytes 49160 | tf_op jit(solution)/shard_map/ppermute | solution.py:204
  58.4 9.0 %collective-permute-start.12 = (f32[2,16,128]{2,1,0:T(8,128)S(1)}, f32[2,16,128]{2,1,0:T(8,128)S(1)}, u32[]{:S(2)}, u32[]{:S(2)}) collective-permute-start(f32[2,16,128]{2,1,0:T(8,128)S(1)} %pad_maximum_fusion.refs_0_), channel_id=1, source_target_pairs={{0,16},{4,20},{8,24},{12,28},{16,0},{20,4},{24,8},{28,12},{1,17},{... | collective-permute-start | bytes 49160 | tf_op jit(solution)/shard_map/ppermute | solution.py:204
  62.2 7.1 %collective-permute-start.11 = (f32[2,16,128]{2,1,0:T(8,128)S(1)}, f32[2,16,128]{2,1,0:T(8,128)S(1)}, u32[]{:S(2)}, u32[]{:S(2)}) collective-permute-start(f32[2,16,128]{2,1,0:T(8,128)S(1)} %pad_maximum_fusion.refs_0_), channel_id=1, source_target_pairs={{0,12},{4,16},{8,20},{12,24},{16,28},{20,0},{24,4},{28,8},{1,13},{... | collective-permute-start | bytes 49160 | tf_op jit(solution)/shard_map/ppermute | solution.py:204
  63.3 6.4 %collective-permute-start.10 = (f32[2,16,128]{2,1,0:T(8,128)S(1)}, f32[2,16,128]{2,1,0:T(8,128)S(1)}, u32[]{:S(2)}, u32[]{:S(2)}) collective-permute-start(f32[2,16,128]{2,1,0:T(8,128)S(1)} %pad_maximum_fusion.refs_0_), channel_id=1, source_target_pairs={{0,8},{4,12},{8,16},{12,20},{16,24},{20,28},{24,0},{28,4},{1,9},{5... | collective-permute-start | bytes 49160 | tf_op jit(solution)/shard_map/ppermute | solution.py:204
  65.8 5.0 %collective-permute-start.9 = (f32[2,16,128]{2,1,0:T(8,128)S(1)}, f32[2,16,128]{2,1,0:T(8,128)S(1)}, u32[]{:S(2)}, u32[]{:S(2)}) collective-permute-start(f32[2,16,128]{2,1,0:T(8,128)S(1)} %pad_maximum_fusion.refs_0_), channel_id=1, source_target_pairs={{0,4},{4,8},{8,12},{12,16},{16,20},{20,24},{24,28},{28,0},{1,5},{5... | collective-permute-start | bytes 49160 | tf_op jit(solution)/shard_map/ppermute | solution.py:204
  70.7 1.2 %copy-start.1 = (f32[512,512]{1,0:T(8,128)S(1)}, f32[512,512]{1,0:T(8,128)}, u32[]{:S(2)}) copy-start(f32[512,512]{1,0:T(8,128)} %copy-done) | copy-start | bytes 3145732
  75.3 0.9 copy-start.8
  76.2 7.4 %copy-start.9 = (bf16[256,1408]{1,0:T(8,128)(2,1)S(1)}, bf16[256,1408]{1,0:T(8,128)(2,1)}, u32[]{:S(2)}) copy-start(bf16[256,1408]{1,0:T(8,128)(2,1)} %copy-done.8) | copy-start | bytes 2162692
  76.2 34.7 %all-to-all-start.2 = ((bf16[16,32,1408]{2,1,0:T(8,128)(2,1)}), bf16[16,32,1408]{2,1,0:T(8,128)(2,1)S(1)}, u32[]{:S(2)}, u32[]{:S(2)}) async-start(bf16[16,32,1408]{2,1,0:T(8,128)(2,1)} %get-tuple-element.27), calls=%async_computation.2 | async-start | bytes 2883584 | tf_op jit(solution)/shard_map/all_to_all | solution.py:212
  83.6 27.4 %copy-start.5 = (bf16[32,1280]{1,0:T(8,128)(2,1)S(1)}, bf16[32,1280]{1,0:T(8,128)(2,1)}, u32[]{:S(2)}) copy-start(bf16[32,1280]{1,0:T(8,128)(2,1)} %pic_ref.3) | copy-start | bytes 245764
  83.6 27.4 %copy-start.7 = (bf16[32,1280]{1,0:T(8,128)(2,1)S(1)}, bf16[32,1280]{1,0:T(8,128)(2,1)}, u32[]{:S(2)}) copy-start(bf16[32,1280]{1,0:T(8,128)(2,1)} %cap_ref.3) | copy-start | bytes 245764
  83.6 2.3 %collective-permute-start.16 = (bf16[256,1408]{1,0:T(8,128)(2,1)S(1)}, bf16[256,1408]{1,0:T(8,128)(2,1)S(1)}, u32[]{:S(2)}, u32[]{:S(2)}) collective-permute-start(bf16[256,1408]{1,0:T(8,128)(2,1)S(1)} %copy-done.9), channel_id=1, source_target_pairs={{0,32},{32,0},{1,33},{33,1},{2,34},{34,2},{3,35},{35,3},{4,36},{36... | collective-permute-start | bytes 2162696 | tf_op jit(solution)/shard_map/ppermute | solution.py:208
  86.1 10.6 %collective-permute-start.17 = (bf16[32,1408]{1,0:T(8,128)(2,1)S(1)}, bf16[32,1408]{1,0:T(8,128)(2,1)S(1)}, u32[]{:S(2)}, u32[]{:S(2)}) collective-permute-start(bf16[32,1408]{1,0:T(8,128)(2,1)S(1)} %get-tuple-element.31), channel_id=1, source_target_pairs={{0,4},{4,8},{8,12},{12,16},{16,20},{20,24},{24,28},{28,0},{1,5},{5... | collective-permute-start | bytes 270344 | tf_op jit(solution)/shard_map/ppermute | solution.py:204
  86.7 13.2 %collective-permute-start.18 = (bf16[32,1408]{1,0:T(8,128)(2,1)S(1)}, bf16[32,1408]{1,0:T(8,128)(2,1)S(1)}, u32[]{:S(2)}, u32[]{:S(2)}) collective-permute-start(bf16[32,1408]{1,0:T(8,128)(2,1)S(1)} %get-tuple-element.32), channel_id=1, source_target_pairs={{0,8},{4,12},{8,16},{12,20},{16,24},{20,28},{24,0},{28,4},{1,9},{5... | collective-permute-start | bytes 270344 | tf_op jit(solution)/shard_map/ppermute | solution.py:204
  88.4 13.7 %collective-permute-start.19 = (bf16[32,1408]{1,0:T(8,128)(2,1)S(1)}, bf16[32,1408]{1,0:T(8,128)(2,1)S(1)}, u32[]{:S(2)}, u32[]{:S(2)}) collective-permute-start(bf16[32,1408]{1,0:T(8,128)(2,1)S(1)} %get-tuple-element.33), channel_id=1, source_target_pairs={{0,12},{4,16},{8,20},{12,24},{16,28},{20,0},{24,4},{28,8},{1,13},{... | collective-permute-start | bytes 270344 | tf_op jit(solution)/shard_map/ppermute | solution.py:204
  90.9 13.1 %collective-permute-start.20 = (bf16[32,1408]{1,0:T(8,128)(2,1)S(1)}, bf16[32,1408]{1,0:T(8,128)(2,1)S(1)}, u32[]{:S(2)}, u32[]{:S(2)}) collective-permute-start(bf16[32,1408]{1,0:T(8,128)(2,1)S(1)} %get-tuple-element.34), channel_id=1, source_target_pairs={{0,16},{4,20},{8,24},{12,28},{16,0},{20,4},{24,8},{28,12},{1,17},{... | collective-permute-start | bytes 270344 | tf_op jit(solution)/shard_map/ppermute | solution.py:204
  94.3 13.1 %collective-permute-start.21 = (bf16[32,1408]{1,0:T(8,128)(2,1)S(1)}, bf16[32,1408]{1,0:T(8,128)(2,1)S(1)}, u32[]{:S(2)}, u32[]{:S(2)}) collective-permute-start(bf16[32,1408]{1,0:T(8,128)(2,1)S(1)} %get-tuple-element.35), channel_id=1, source_target_pairs={{0,20},{4,24},{8,28},{12,0},{16,4},{20,8},{24,12},{28,16},{1,21},{... | collective-permute-start | bytes 270344 | tf_op jit(solution)/shard_map/ppermute | solution.py:204
  96.7 13.7 %collective-permute-start.22 = (bf16[32,1408]{1,0:T(8,128)(2,1)S(1)}, bf16[32,1408]{1,0:T(8,128)(2,1)S(1)}, u32[]{:S(2)}, u32[]{:S(2)}) collective-permute-start(bf16[32,1408]{1,0:T(8,128)(2,1)S(1)} %get-tuple-element.36), channel_id=1, source_target_pairs={{0,24},{4,28},{8,0},{12,4},{16,8},{20,12},{24,16},{28,20},{1,25},{... | collective-permute-start | bytes 270344 | tf_op jit(solution)/shard_map/ppermute | solution.py:204
  100.0 11.0 %collective-permute-start.23 = (bf16[32,1408]{1,0:T(8,128)(2,1)S(1)}, bf16[32,1408]{1,0:T(8,128)(2,1)S(1)}, u32[]{:S(2)}, u32[]{:S(2)}) collective-permute-start(bf16[32,1408]{1,0:T(8,128)(2,1)S(1)} %get-tuple-element.37), channel_id=1, source_target_pairs={{0,28},{4,0},{8,4},{12,8},{16,12},{20,16},{24,20},{28,24},{1,29},{... | collective-permute-start | bytes 270344 | tf_op jit(solution)/shard_map/ppermute | solution.py:204

commit v2 on v1

v2 whole, which is shorter than its diff:
```python
import jax
import jax.numpy as jnp
from jax import lax
from jax.experimental import pallas as pl
from jax.experimental.pallas import tpu as pltpu
from jax.sharding import Mesh, PartitionSpec as P

F32 = jnp.float32
BF16 = jnp.bfloat16
NX, NC, NZ, NY = 4, 2, 8, 4
NXY = NX * NY
TURN_X, TURN_Y = 2, 2
FAR = NZ // 2
NEAR = range(1, FAR)
OWN = 32
TILE = 512
LANE = 128
NB = TILE // LANE
PAD = 16
VMEM_LIMIT = 20 * 1024 * 1024
PARAMS = pltpu.CompilerParams(vmem_limit_bytes=VMEM_LIMIT)


def inverse_norm(values):
    return lax.rsqrt(jnp.sum(values * values, axis=1, keepdims=True) + 1e-06)


def position():
    return lax.axis_index("x"), lax.axis_index("c"), lax.axis_index("z"), lax.axis_index("y")


def rows_at(start, size):
    return pl.ds(pl.multiple_of(start, size), size)


def ring(z, steps):
    return lax.rem(z + steps + NZ, NZ)


def arrivals(c, z):
    back = 2 * c - 1
    order = []
    for k in NEAR:
        order += [(c, ring(z, back * k)), (1 - c, ring(z, back * k))]
    return order + [(c, ring(z, FAR))]


def images_kernel(pic_ref, img_ref):
    pic = pic_ref[...].astype(F32)
    img = (pic * inverse_norm(pic)).astype(BF16)
    for slot in range(NXY):
        img_ref[slot] = img


def texts_kernel(cap_ref, other_ref, after_ref, txt_ref):
    for part, ref in enumerate((cap_ref, other_ref)):
        cap = ref[...].astype(F32)
        txt_ref[part] = (cap * inverse_norm(cap)).astype(BF16)


def scale_row(log_ref):
    return jnp.exp(jnp.full((1, LANE), log_ref[0], F32))


def pair_mask(j, q, x, c, z, y):
    row = lax.broadcasted_iota(jnp.int32, (LANE, 1), 0) + j * LANE
    col = lax.broadcasted_iota(jnp.int32, (1, LANE), 1) + q * LANE
    slot = row // OWN
    at_x, at_y = plane_member(slot, c)
    image = ((at_x * NC + c) * (NZ * NY) + z * NY + at_y) * OWN + row % OWN
    part = col // OWN
    text = (((part % NZ) * NY + y) * (NX * NC) + x * NC + part // NZ) * OWN + col % OWN
    return image == text


def similarity(img, txt):
    return lax.dot_general(img, txt, (((1,), (1,)), ((), ())), preferred_element_type=F32)


def to_lanes(column):
    return jnp.transpose(jnp.broadcast_to(column, (LANE, LANE)))[0:1, :]


def logits_kernel(log_ref, img_ref, chip_ref, own_ref, other_ref, txt_ref, rowp_ref, colp_ref, logit_ref):
    x, c, z, y = position()
    for ref, order in (
        (chip_ref, [(c, z), (1 - c, z)]),
        (own_ref, arrivals(c, z)),
        (other_ref, arrivals(1 - c, z)),
    ):
        for k, (core, at) in enumerate(order):
            txt_ref[rows_at((core * NZ + at) * OWN, OWN), :] = ref[k]
    img = img_ref[...].reshape(TILE, img_ref.shape[2])
    scale = jnp.tile(scale_row(log_ref), (1, NB))
    logit_ref[...] = scale * similarity(img, txt_ref[...])
    pos = jnp.zeros((LANE, LANE), F32)
    for j in range(NB):
        piece = logit_ref[j * LANE : (j + 1) * LANE, :]
        peak = jnp.max(piece, axis=1, keepdims=True)
        shifted = jnp.exp(piece - peak)
        total = jnp.sum(shifted, axis=1, keepdims=True)
        mean = to_lanes(jnp.sum(shifted * piece, axis=1, keepdims=True) / total)
        lse = to_lanes(peak + jnp.log(total))
        for slot in range(NXY):
            rowp_ref[slot, j : j + 1, :] = lse
            rowp_ref[slot, NB + j : NB + j + 1, :] = mean
        for q in range(NB):
            pos += jnp.where(pair_mask(j, q, x, c, z, y), piece[:, q * LANE : (q + 1) * LANE], 0.0)
    for q in range(NB):
        piece = logit_ref[:, q * LANE : (q + 1) * LANE]
        peak = jnp.max(piece, axis=0, keepdims=True)
        shifted = jnp.exp(piece - peak)
        total = jnp.sum(shifted, axis=0, keepdims=True)
        colp_ref[q : q + 1, :] = peak + jnp.log(total)
        colp_ref[NB + q : NB + q + 1, :] = jnp.sum(shifted * piece, axis=0, keepdims=True) / total
    pos = jnp.sum(pos, axis=0, keepdims=True)
    first = lax.broadcasted_iota(jnp.int32, (2 * NB, LANE), 0) == 0
    colp_ref[2 * NB :, :] = jnp.where(first, pos, 0.0)


def departures(core, z):
    ahead = 1 - 2 * core
    order = []
    for k in NEAR:
        order += [(core, ring(z, ahead * k)), (1 - core, ring(z, ahead * k))]
    return order + [(core, z), (core, ring(z, FAR))]


def combine(lse, mean):
    peak = jnp.max(lse, axis=0)
    weight = jnp.exp(lse - peak)
    total = jnp.sum(weight, axis=0)
    return peak + jnp.log(total), jnp.sum(weight * mean, axis=0) / total


def all_sum(values):
    return jnp.sum(jnp.sum(values, axis=1, keepdims=True), axis=0, keepdims=True)


def group_at(k):
    return slice(k * OWN, (k + 1) * OWN)


def scalar_block(source, loss_part, temp_part):
    lane = lax.broadcasted_iota(jnp.int32, (PAD, LANE), 1)
    row = lax.broadcasted_iota(jnp.int32, (PAD, LANE), 0)
    value = jnp.where(lane == source * 8, loss_part, jnp.where(lane == source * 8 + 1, temp_part, 0.0))
    high = value.astype(BF16).astype(F32)
    rest = value - high
    middle = rest.astype(BF16).astype(F32)
    low = rest - middle
    return jnp.where(row == 0, high, jnp.where(row == 1, middle, jnp.where(row == 2, low, 0.0))).astype(BF16)


def grad_kernel(
    log_ref, txt_ref, img_ref, rowg_ref, chip_ref, own_ref, other_ref,
    grad_ref, keep_ref, send_ref, columns_ref, logit_ref, gradt, order_gradt, colg,
):
    x, c, z, y = position()
    width = img_ref.shape[2]
    for ref, order in (
        (chip_ref, [(c, z), (1 - c, z)]),
        (own_ref, arrivals(c, z)),
        (other_ref, arrivals(1 - c, z)),
    ):
        for k, (core, at) in enumerate(order):
            colg[core * NZ + at] = ref[k]
    logit_ref[...] = jnp.tile(scale_row(log_ref), (1, NB)) * similarity(
        img_ref[...].reshape(TILE, width), txt_ref[...]
    )
    row_lse, row_mean = combine(rowg_ref[:, :NB, :], rowg_ref[:, NB:, :])
    col_lse, col_mean = combine(colg[:, :NB, :], colg[:, NB : 2 * NB, :])
    pos = all_sum(jnp.sum(colg[:, 2 * NB :, :], axis=0))
    rows_block = scalar_block(z * NC + c, all_sum(row_lse), 0.5 * all_sum(row_mean))
    columns_ref[...] = scalar_block(
        y * NX + x, all_sum(col_lse) - 2.0 * pos, 0.5 * all_sum(col_mean) - pos
    )
    for j in range(NB):
        line = jnp.transpose(jnp.broadcast_to(row_lse[j : j + 1, :], (LANE, LANE)))
        for q in range(NB):
            piece = logit_ref[j * LANE : (j + 1) * LANE, q * LANE : (q + 1) * LANE]
            pair = pair_mask(j, q, x, c, z, y)
            weight = 0.5 * (jnp.exp(piece - line) + jnp.exp(piece - col_lse[q : q + 1, :]))
            weight = weight - jnp.where(pair, 1.0, 0.0)
            grad_ref[j * LANE : (j + 1) * LANE, q * LANE : (q + 1) * LANE] = weight.astype(BF16)
            gradt[q * LANE : (q + 1) * LANE, j * LANE : (j + 1) * LANE] = jnp.transpose(weight).astype(BF16)
    for part, core in enumerate((c, 1 - c)):
        for k, (to, at) in enumerate(departures(core, z)):
            start = (part * NZ + k) * OWN
            order_gradt[start : start + OWN, :] = gradt[rows_at((to * NZ + at) * OWN, OWN), :]
    step = 2 * LANE
    half = NZ * OWN
    scale = jnp.tile(scale_row(log_ref), (1, 2))
    for start in range(0, width, step):
        span = slice(start, start + step)
        img = img_ref[:, :, span].reshape(TILE, step)
        term = (scale * jnp.dot(order_gradt[...], img, preferred_element_type=F32)).astype(BF16)
        for k in range(2):
            group = group_at(start // LANE + k)
            lanes = slice(k * LANE, (k + 1) * LANE)
            keep_ref[:, group, :] = term[:half, lanes].reshape(NZ, OWN, LANE)
            send_ref[:, group, :] = term[half:, lanes].reshape(NZ, OWN, LANE)
    last = width // LANE * OWN
    for k in range(NZ):
        keep_ref[k, last:, :] = rows_block
        send_ref[k, last:, :] = rows_block


def terms_kernel(log_ref, grad_ref, txt_ref, columns_ref, term_ref):
    width = txt_ref.shape[1]
    step = 2 * LANE
    scale = jnp.tile(scale_row(log_ref), (1, 2))
    for start in range(0, width, step):
        term = scale * jnp.dot(grad_ref[...], txt_ref[:, start : start + step], preferred_element_type=F32)
        term = term.astype(BF16)
        for k in range(2):
            lanes = slice(k * LANE, (k + 1) * LANE)
            term_ref[:, group_at(start // LANE + k), :] = term[:, lanes].reshape(NXY, OWN, LANE)
    for slot in range(NXY):
        term_ref[slot, width // LANE * OWN :, :] = columns_ref[...]


def add_kernel(keep_ref, other_ref, term_ref, *out_refs):
    total = (keep_ref[...].astype(F32) + other_ref[...].astype(F32)).astype(BF16)
    one_ref, two_ref, keep_out, far_ref = out_refs[:4]
    one_ref[...] = total[:NC]
    two_ref[...] = total[NC : 3 * NC]
    keep_out[...] = total[3 * NC]
    far_ref[...] = total[3 * NC + 1]


def relay_kernel(one_ref, two_ref, out_ref):
    out_ref[...] = (one_ref[...].astype(F32) + two_ref[NC:].astype(F32)).astype(BF16)


def pass_kernel(one_ref, two_ref, out_ref):
    out_ref[...] = (one_ref[1].astype(F32) + two_ref[1].astype(F32)).astype(BF16)


def unit_backward(values, gradient):
    inverse = inverse_norm(values)
    direction = values * inverse
    inner = jnp.sum(direction * gradient, axis=1, keepdims=True)
    return ((gradient - direction * inner) * inverse).astype(BF16)


def columns_of(values, width):
    return jnp.concatenate([values[group_at(k)] for k in range(width // LANE)], axis=1)


def final_kernel(pic_ref, cap_ref, term_ref, *refs):
    near_refs, part_refs = refs[:2], refs[2:5]
    gpic_ref, gcap_ref, loss_ref, temp_ref = refs[5:]
    width = pic_ref.shape[1]
    img = term_ref[0].astype(F32)
    for slot in range(1, NXY):
        img += term_ref[slot].astype(F32)
    txt = near_refs[0][0].astype(F32)
    for ref in near_refs[1:]:
        txt += ref[0].astype(F32)
    for ref in part_refs:
        txt += ref[...].astype(F32)
    gpic_ref[...] = unit_backward(pic_ref[...].astype(F32), columns_of(img, width))
    gcap_ref[...] = unit_backward(cap_ref[...].astype(F32), columns_of(txt, width))
    last = width // LANE * OWN
    scalars = jnp.sum(img[last : last + 8] + txt[last : last + 8], axis=0, keepdims=True)
    lane = lax.broadcasted_iota(jnp.int32, (1, LANE), 1) % 8
    pairs = TILE * NXY
    loss_ref[0] = jnp.sum(jnp.where(lane == 0, scalars, 0.0)) / (2 * pairs)
    temp_ref[0] = jnp.sum(jnp.where(lane == 1, scalars, 0.0)) / pairs


def shape(dims, dtype):
    return jax.ShapeDtypeStruct(dims, dtype)


def shift(values, k):
    pairs = []
    for core, step in ((0, k), (1, -k)):
        pairs += [(core * NZ + i, core * NZ + (i + step) % NZ) for i in range(NZ)]
    return lax.ppermute(values, ("c", "z"), pairs)


def gather(chip, micros):
    one = shift(chip, 1)
    two = shift(hint(jnp.concatenate([chip, one], axis=0), micros), 2)
    own = jnp.concatenate([one, two, shift(chip[:1], FAR)], axis=0)
    return own, swap(own)


def swap(values):
    return lax.ppermute(values, "c", [(0, 1), (1, 0)])


def plane_member(slot, c):
    return (slot + TURN_X * c) % NX, (slot // NX + TURN_Y * c) % NY


def plane(c, z):
    members = [plane_member(slot, c) for slot in range(NXY)]
    return [((x * NC + c) * NZ + z) * NY + y for x, y in members]


PLANES = [plane(c, z) for c in range(NC) for z in range(NZ)]


def exchange(values):
    return lax.all_to_all(values, ("x", "c", "z", "y"), 0, 0, axis_index_groups=PLANES, tiled=True)


VM = pl.BlockSpec(memory_space=pltpu.VMEM)
ANY = pl.BlockSpec(memory_space=pl.ANY)
SM = pl.BlockSpec(memory_space=pltpu.SMEM)


def call(kernel, out_shape, in_specs, out_specs=None, scratch=(), cost=None, aliases=None):
    return pl.pallas_call(
        kernel,
        name=kernel.__name__,
        out_shape=out_shape,
        in_specs=in_specs,
        out_specs=out_specs if out_specs is not None else [VM] * len(out_shape),
        scratch_shapes=scratch,
        compiler_params=PARAMS,
        cost_estimate=cost,
        input_output_aliases=aliases or {},
    )


def tie_kernel(ref, out_ref):
    pass


def hint(values, micros):
    return call(
        tie_kernel,
        [shape(values.shape, values.dtype)],
        [ANY],
        [ANY],
        aliases={0: 0},
        cost=cost(micros),
    )(values)[0]


def cost(micros):
    return pl.CostEstimate(flops=micros * 1_150_000_000, bytes_accessed=0, transcendentals=0)


def shards(pic, cap, log_scale):
    width = pic.shape[1]
    long = width // LANE * OWN + PAD
    [img_out] = call(images_kernel, [shape((NXY, OWN, width), BF16)], [VM])(pic)
    img = hint(exchange(img_out), 10)
    [chip] = call(texts_kernel, [shape((NC, OWN, width), BF16)], [VM] * 2 + [ANY])(cap, swap(cap), img_out)
    own, other = gather(chip, 10)
    txt, rowp, colp = call(
        logits_kernel,
        [
            shape((TILE, width), BF16),
            shape((NXY, 2 * NB, LANE), F32),
            shape((4 * NB, LANE), F32),
        ],
        [SM, VM, VM, VM, VM],
        scratch=[pltpu.VMEM((TILE, TILE), F32)],
    )(log_scale, img, chip, own, other)
    rowg = hint(exchange(rowp), 30)
    chip = jnp.stack([colp, swap(colp)])
    own, other = gather(chip, 10)
    half = (NZ, long, LANE)
    grad, keep, send, columns = call(
        grad_kernel,
        [
            shape((TILE, TILE), BF16),
            shape(half, BF16),
            shape(half, BF16),
            shape((PAD, LANE), BF16),
        ],
        [SM] + [VM] * 6,
        scratch=[
            pltpu.VMEM((TILE, TILE), F32),
            pltpu.VMEM((TILE, TILE), BF16),
            pltpu.VMEM((TILE, TILE), BF16),
            pltpu.VMEM((NC * NZ, 4 * NB, LANE), F32),
        ],
    )(log_scale, txt, img, rowg, chip, own, other)
    [terms] = call(terms_kernel, [shape((NXY, long, LANE), BF16)], [SM] + [VM] * 3, cost=cost(4))(
        log_scale, grad, txt, columns
    )
    one, two, keep, far, terms = call(
        add_kernel,
        [
            shape((NC, long, LANE), BF16),
            shape((2 * NC, long, LANE), BF16),
            shape((long, LANE), BF16),
            shape((long, LANE), BF16),
            shape((NXY, long, LANE), BF16),
        ],
        [VM, VM, ANY],
        [VM] * 4 + [ANY],
        aliases={2: 4},
    )(keep, swap(send), terms)
    terms = exchange(terms)
    two = shift(two, 2)
    far = shift(far, FAR)
    [one] = call(relay_kernel, [shape((NC, long, LANE), BF16)], [VM] * 2, cost=cost(10))(one, two)
    one = shift(one, 1)
    [passed] = call(pass_kernel, [shape((long, LANE), BF16)], [VM] * 2)(one, two)
    return call(
        final_kernel,
        [shape((OWN, width), BF16), shape((OWN, width), BF16), shape((1,), F32), shape((1,), F32)],
        [VM] * 8,
        [VM, VM, SM, SM],
    )(pic, cap, terms, one, two, keep, far, swap(passed))


def solution(mesh):
    grid = Mesh(mesh.devices.reshape(NX, NC, NZ, NY), ("x", "c", "z", "y"))
    rows = P(("x", "c", "z", "y"), None)
    columns = P(("z", "y", "x", "c"), None)
    return jax.shard_map(
        shards,
        mesh=grid,
        in_specs=(rows, columns, P()),
        out_specs=(rows, columns, P(), P()),
        check_vma=False,
    )
```

time: 113 us -> 91.1 us (0.81)
  starting transfers between devices: 63.2 us -> 40.8 us
  local copies, waits for them, and re-layouts: 6.86 us -> 2.85 us
  waiting for transfers between devices: 32.1 us -> 34.8 us
  Pallas kernels: 8.4 us -> 9.65 us
    ppermute x21 -> x9, starting transfers between devices: 40.8 us -> 19.3 us  [shift(): return lax.ppermute(values, ('c', 'z'), pairs)]
    all_to_all x3, waiting for transfers between devices: 0.01 us -> 4.64 us  [exchange(): lax.all_to_all(values, ('x', 'c', 'z', 'y'), 0, 0, axis_index_groups=PLAN...]
    unnamed x27 -> x14, local copies, waits for them, and re-layouts: 6.85 us -> 2.83 us
    all_to_all x3, starting transfers between devices: 22.1 us -> 20.7 us  [exchange(): lax.all_to_all(values, ('x', 'c', 'z', 'y'), 0, 0, axis_index_groups=PLAN...]
    pallas_call x4 -> x12, Pallas kernels: 7.33 us -> 8.62 us  [the longest x1 2.58 us: shards(): call(logits_kernel, [shape((TILE, width), BF16), shape((NXY, 2 * NB, LANE...]
    ppermute x3 -> x6, waiting for transfers between devices: 3.62 us -> 2.57 us  [swap(): return lax.ppermute(values, 'c', [(0, 1), (1, 0)])]
    ppermute x21 -> x9, waiting for transfers between devices: 28.5 us -> 27.6 us  [shift(): return lax.ppermute(values, ('c', 'z'), pairs)]
  transfers between devices with their start and end apart: 27 -> 18, of which waited for: 12 -> 12; matrix products, arithmetic and copies ran while one was open for 0% -> 0% of each run, Pallas kernels for 0% -> 4%
where the time goes in v2:
time: 91.1 us; the launch traced here: 89.8 us
  starting transfers between devices  40.8 us (45%)
  waiting for transfers between devices  34.8 us (38%)
  Pallas kernels  9.65 us (11%)
  local copies, waits for them, and re-layouts  2.85 us (3%)
  between operations  1.59 us (2%)
    ppermute x9, waiting for transfers between devices, shift(): return lax.ppermute(values, ('c', 'z'), pairs)  27.6 us
    all_to_all x3, starting transfers between devices, exchange(): lax.all_to_all(values, ('x', 'c', 'z', 'y'), 0, 0, axis_index_groups=PLAN...  20.7 us
    ppermute x9, starting transfers between devices, shift(): return lax.ppermute(values, ('c', 'z'), pairs)  19.3 us
    all_to_all x3, waiting for transfers between devices, exchange(): lax.all_to_all(values, ('x', 'c', 'z', 'y'), 0, 0, axis_index_groups=PLAN...  4.64 us
    unnamed x14, local copies, waits for them, and re-layouts  2.83 us
    pallas_call x1, Pallas kernels, shards(): call(logits_kernel, [shape((TILE, width), BF16), shape((NXY, 2 * NB, LANE...  2.58 us
    ppermute x6, waiting for transfers between devices, swap(): return lax.ppermute(values, 'c', [(0, 1), (1, 0)])  2.57 us
    pallas_call x1, Pallas kernels, shards(): call(grad_kernel, [shape((TILE, TILE), BF16), shape(half, BF16), shape(ha...  2.45 us
  transfers between devices with their start and end apart: 18, of which 12 were waited for; matrix products, arithmetic and copies ran while one was open for 0% of the time, Pallas kernels for 4%

profile of v2, /device:TPU:2, one launch (start us, length us, event | category | flops | bytes accessed | tf_op | source)
XLA Modules:
  0.0 89.8 jit_solution(9694055687297818592)
XLA Ops:
  0.6 0.0 copy-start.2
  0.6 0.1 collective-permute-start
  0.7 0.0 copy-start.3
  0.8 0.9 copy-done.3
  1.6 1.3 %images_kernel.1.after_ref = bf16[16,32,1280]{2,1,0:T(8,128)(2,1)} custom-call(bf16[32,1280]{1,0:T(8,128)(2,1)S(1)} %copy-done.3), custom_call_target="tpu_custom_call" | custom-call | tf_op jit(solution)/shard_map/images_kernel/pallas_call | solution.py:352
  2.9 0.0 collective-permute-done.other_ref
  2.9 0.1 texts_kernel.1.chip_ref
  3.0 2.0 %collective-permute-start.1 = (bf16[2,32,1280]{2,1,0:T(8,128)(2,1)S(1)}, bf16[2,32,1280]{2,1,0:T(8,128)(2,1)S(1)}, u32[]{:S(2)}, u32[]{:S(2)}) collective-permute-start(bf16[2,32,1280]{2,1,0:T(8,128)(2,1)S(1)} %texts_kernel.1.chip_ref), channel_id=1, source_target_pairs={{0,4},{4,8},{8,12},{12,16},{16,20},{20,24},{24,28},{28,0},{32,60},... | collective-permute-start | bytes 491528 | tf_op jit(solution)/shard_map/ppermute | solution.py:281
  5.0 7.5 %all-to-all-start = ((bf16[16,32,1280]{2,1,0:T(8,128)(2,1)}), bf16[16,32,1280]{2,1,0:T(8,128)(2,1)S(1)}, u32[]{:S(2)}, u32[]{:S(2)}) async-start(bf16[16,32,1280]{2,1,0:T(8,128)(2,1)} %images_kernel.1.after_ref), calls=%async_computation | async-start | bytes 2621440 | tf_op jit(solution)/shard_map/all_to_all | solution.py:308
  12.5 0.0 collective-permute-done.1
  12.6 3.3 %collective-permute-start.2 = (bf16[4,32,1280]{2,1,0:T(8,128)(2,1)S(1)}, bf16[4,32,1280]{2,1,0:T(8,128)(2,1)S(1)}, u32[]{:S(2)}, u32[]{:S(2)}) collective-permute-start(bf16[4,32,1280]{2,1,0:T(8,128)(2,1)S(1)} %tie_kernel.5), channel_id=1, source_target_pairs={{0,8},{4,12},{8,16},{12,20},{16,24},{20,28},{24,0},{28,4},{32,56},... | collective-permute-start | bytes 983048 | tf_op jit(solution)/shard_map/ppermute | solution.py:281
  16.6 4.6 %collective-permute-start.3 = (bf16[1,32,1280]{2,1,0:T(8,128)(2,1)S(1)}, bf16[1,32,1280]{2,1,0:T(8,128)(2,1)S(1)}, u32[]{:S(2)}, u32[]{:S(2)}) collective-permute-start(bf16[1,32,1280]{2,1,0:T(8,128)(2,1)S(1)} %slice.4), channel_id=1, source_target_pairs={{0,16},{4,20},{8,24},{12,28},{16,0},{20,4},{24,8},{28,12},{32,48},... | collective-permute-start | bytes 245768 | tf_op jit(solution)/shard_map/ppermute | solution.py:281
  21.2 6.6 %collective-permute-done.2 = bf16[4,32,1280]{2,1,0:T(8,128)(2,1)S(1)} collective-permute-done((bf16[4,32,1280]{2,1,0:T(8,128)(2,1)S(1)}, bf16[4,32,1280]{2,1,0:T(8,128)(2,1)S(1)}, u32[]{:S(2)}, u32[]{:S(2)}) %collective-permute-start.2) | collective-permute-done | bytes 327712 | tf_op jit(solution)/shard_map/ppermute | solution.py:281
  27.8 3.6 %collective-permute-done.3 = bf16[1,32,1280]{2,1,0:T(8,128)(2,1)S(1)} collective-permute-done((bf16[1,32,1280]{2,1,0:T(8,128)(2,1)S(1)}, bf16[1,32,1280]{2,1,0:T(8,128)(2,1)S(1)}, u32[]{:S(2)}, u32[]{:S(2)}) %collective-permute-start.3) | collective-permute-done | bytes 81952 | tf_op jit(solution)/shard_map/ppermute | solution.py:281
  31.5 0.0 collective-permute-start.4
  31.5 1.6 %all-to-all-done.ref = bf16[16,32,1280]{2,1,0:T(8,128)(2,1)S(1)} async-done(((bf16[16,32,1280]{2,1,0:T(8,128)(2,1)}), bf16[16,32,1280]{2,1,0:T(8,128)(2,1)S(1)}, u32[]{:S(2)}, u32[]{:S(2)}) %all-to-all-start) | async-done | bytes 1310752 | tf_op jit(solution)/shard_map/all_to_all | solution.py:308
  33.1 0.3 collective-permute-done.4.other_ref
  33.4 0.8 copy-done
  34.3 1.1 %copy-done.1 = bf16[7,32,1280]{2,1,0:T(8,128)(2,1)S(1)} copy-done((bf16[7,32,1280]{2,1,0:T(8,128)(2,1)S(1)}, bf16[7,32,1280]{2,1,0:T(8,128)(2,1)}, u32[]{:S(2)}) %copy-start.1) | copy-done | bytes 573464
  35.4 2.6 %logits_kernel.1 = (bf16[512,1280]{1,0:T(8,128)(2,1)S(1)}, f32[16,8,128]{2,1,0:T(8,128)}, f32[16,128]{1,0:T(8,128)S(1)}) custom-call(f32[1]{0:T(128)S(6)} %copy.21.log_ref, bf16[16,32,1280]{2,1,0:T(8,128)(2,1)S(1)} %tie_kernel.4.img_ref, bf16[2,32,1280]{2,1,0:T(8,128)(2,1)S(1)} %texts_kernel.1.chip_ref, ...), custom_call_target="tpu_custom_call" | custom-call | tf_op jit(solution)/shard_map/logits_kernel/pallas_call | solution.py:356
  37.9 0.1 collective-permute-start.5
  38.1 1.0 %collective-permute-done.5 = f32[16,128]{1,0:T(8,128)S(1)} collective-permute-done((f32[16,128]{1,0:T(8,128)S(1)}, f32[16,128]{1,0:T(8,128)S(1)}, u32[]{:S(2)}, u32[]{:S(2)}) %collective-permute-start.5) | collective-permute-done | bytes 8224 | tf_op jit(solution)/shard_map/ppermute | solution.py:292
  39.1 0.0 collective-permute-start.6
  39.1 4.5 %collective-permute-start.8 = (f32[1,16,128]{2,1,0:T(8,128)S(1)}, f32[1,16,128]{2,1,0:T(8,128)S(1)}, u32[]{:S(2)}, u32[]{:S(2)}) collective-permute-start(f32[1,16,128]{2,1,0:T(8,128)S(1)} %bitcast.3), channel_id=1, source_target_pairs={{0,16},{4,20},{8,24},{12,28},{16,0},{20,4},{24,8},{28,12},{32,48},... | collective-permute-start | bytes 24584 | tf_op jit(solution)/shard_map/ppermute | solution.py:281
  43.6 6.3 %all-to-all-start.1 = ((f32[16,8,128]{2,1,0:T(8,128)}), f32[16,8,128]{2,1,0:T(8,128)S(1)}, u32[]{:S(2)}, u32[]{:S(2)}) async-start(f32[16,8,128]{2,1,0:T(8,128)} %get-tuple-element.17), calls=%async_computation.1 | async-start | bytes 131072 | tf_op jit(solution)/shard_map/all_to_all | solution.py:308
  49.9 0.0 collective-permute-done.6
  49.9 0.8 collective-permute-start.7
  50.8 5.3 %collective-permute-done.7 = f32[4,16,128]{2,1,0:T(8,128)S(1)} collective-permute-done((f32[4,16,128]{2,1,0:T(8,128)S(1)}, f32[4,16,128]{2,1,0:T(8,128)S(1)}, u32[]{:S(2)}, u32[]{:S(2)}) %collective-permute-start.7) | collective-permute-done | bytes 32800 | tf_op jit(solution)/shard_map/ppermute | solution.py:281
  56.0 0.0 collective-permute-done.8
  56.1 0.1 collective-permute-start.9
  56.2 0.1 all-to-all-done.1.ref
  56.2 1.2 %collective-permute-done.9.other_ref = f32[7,16,128]{2,1,0:T(8,128)S(1)} collective-permute-done((f32[7,16,128]{2,1,0:T(8,128)S(1)}, f32[7,16,128]{2,1,0:T(8,128)S(1)}, u32[]{:S(2)}, u32[]{:S(2)}) %collective-permute-start.9) | collective-permute-done | bytes 57376 | tf_op jit(solution)/shard_map/ppermute | solution.py:292
  57.4 2.5 %grad_kernel.1 = (bf16[512,512]{1,0:T(8,128)(2,1)S(1)}, bf16[8,336,128]{2,1,0:T(8,128)(2,1)S(1)}, bf16[8,336,128]{2,1,0:T(8,128)(2,1)S(1)}, bf16[16,128]{1,0:T(8,128)(2,1)S(1)}) custom-call(f32[1]{0:T(128)S(6)} %copy.21.log_ref, bf16[512,1280]{1,0:T(8,128)(2,1)S(1)} %get-tuple-element.16.txt_ref, bf16[16,32,1280]{2,1,0:T(8,128)(2,1)S(1)} %tie_kernel.4.img_ref, ...), custom_call_target="tpu_custom_call" | custom-call | tf_op jit(solution)/shard_map/grad_kernel/pallas_call | solution.py:370
  59.8 0.4 collective-permute-start.10
  60.3 2.0 %terms_kernel.1.term_ref = bf16[16,336,128]{2,1,0:T(8,128)(2,1)} custom-call(f32[1]{0:T(128)S(6)} %copy.21.log_ref, bf16[512,512]{1,0:T(8,128)(2,1)S(1)} %get-tuple-element.21.grad_ref, bf16[512,1280]{1,0:T(8,128)(2,1)S(1)} %get-tuple-element.16.txt_ref, bf16[16,128]{1,0:T(8,128)(2,1)S(1)} %get-tuple-element.22.columns_ref), custom_call_target="tpu_custom_call" | custom-call | flops 4600000000 | tf_op jit(solution)/shard_map/terms_kernel/pallas_call | solution.py:386
  62.2 0.0 collective-permute-done.10.other_ref
  62.3 0.2 add_kernel.1
  62.4 0.4 collective-permute-start.11
  62.8 6.9 %all-to-all-start.2 = ((bf16[16,336,128]{2,1,0:T(8,128)(2,1)}), bf16[16,336,128]{2,1,0:T(8,128)(2,1)S(1)}, u32[]{:S(2)}, u32[]{:S(2)}) async-start(bf16[16,336,128]{2,1,0:T(8,128)(2,1)} %get-tuple-element.23), calls=%async_computation.2 | async-start | bytes 2752512 | tf_op jit(solution)/shard_map/all_to_all | solution.py:308
  69.7 5.2 %collective-permute-done.11.two_ref.refs_1_ = bf16[4,336,128]{2,1,0:T(8,128)(2,1)S(1)} collective-permute-done((bf16[4,336,128]{2,1,0:T(8,128)(2,1)S(1)}, bf16[4,336,128]{2,1,0:T(8,128)(2,1)S(1)}, u32[]{:S(2)}, u32[]{:S(2)}) %collective-permute-start.11) | collective-permute-done | bytes 344096 | tf_op jit(solution)/shard_map/ppermute | solution.py:281
  75.0 0.2 collective-permute-start.12
  75.1 3.4 %collective-permute-start.13 = (bf16[336,128]{1,0:T(8,128)(2,1)S(1)}, bf16[336,128]{1,0:T(8,128)(2,1)S(1)}, u32[]{:S(2)}, u32[]{:S(2)}) collective-permute-start(bf16[336,128]{1,0:T(8,128)(2,1)S(1)} %get-tuple-element.27), channel_id=1, source_target_pairs={{0,16},{4,20},{8,24},{12,28},{16,0},{20,4},{24,8},{28,12},{32,48},... | collective-permute-start | bytes 258056 | tf_op jit(solution)/shard_map/ppermute | solution.py:281
  78.6 5.3 %collective-permute-done.12.one_ref.refs_0_ = bf16[2,336,128]{2,1,0:T(8,128)(2,1)S(1)} collective-permute-done((bf16[2,336,128]{2,1,0:T(8,128)(2,1)S(1)}, bf16[2,336,128]{2,1,0:T(8,128)(2,1)S(1)}, u32[]{:S(2)}, u32[]{:S(2)}) %collective-permute-start.12) | collective-permute-done | bytes 172064 | tf_op jit(solution)/shard_map/ppermute | solution.py:281
  83.9 0.1 collective-permute-start.14
  84.0 1.7 %collective-permute-done.13.refs_3_ = bf16[336,128]{1,0:T(8,128)(2,1)S(1)} collective-permute-done((bf16[336,128]{1,0:T(8,128)(2,1)S(1)}, bf16[336,128]{1,0:T(8,128)(2,1)S(1)}, u32[]{:S(2)}, u32[]{:S(2)}) %collective-permute-start.13) | collective-permute-done | bytes 86048 | tf_op jit(solution)/shard_map/ppermute | solution.py:281
  85.6 0.0 collective-permute-done.14.refs_4_
  85.6 2.9 %all-to-all-done.2.term_ref = bf16[16,336,128]{2,1,0:T(8,128)(2,1)S(1)} async-done(((bf16[16,336,128]{2,1,0:T(8,128)(2,1)}), bf16[16,336,128]{2,1,0:T(8,128)(2,1)S(1)}, u32[]{:S(2)}, u32[]{:S(2)}) %all-to-all-start.2) | async-done | bytes 1376288 | tf_op jit(solution)/shard_map/all_to_all | solution.py:308
  88.6 1.0 %final_kernel.1 = (bf16[32,1280]{1,0:T(8,128)(2,1)}, bf16[32,1280]{1,0:T(8,128)(2,1)}, f32[1]{0:T(128)}, f32[1]{0:T(128)}) custom-call(bf16[32,1280]{1,0:T(8,128)(2,1)S(1)} %copy-done.4, bf16[32,1280]{1,0:T(8,128)(2,1)S(1)} %copy-done.2, bf16[16,336,128]{2,1,0:T(8,128)(2,1)S(1)} %all-to-all-done.2.term_ref, ...), custom_call_target="tpu_custom_call" | custom-call | tf_op jit(solution)/shard_map/final_kernel/pallas_call | solution.py:408
  (21 shorter events, 0.2 us)
Async XLA Ops:
  0.6 2.3 %copy-start.2 = (bf16[32,1280]{1,0:T(8,128)(2,1)S(1)}, bf16[32,1280]{1,0:T(8,128)(2,1)}, u32[]{:S(2)}) copy-start(bf16[32,1280]{1,0:T(8,128)(2,1)} %cap_ref.3) | copy-start | bytes 245764
  0.6 2.3 %collective-permute-start = (bf16[32,1280]{1,0:T(8,128)(2,1)}, bf16[32,1280]{1,0:T(8,128)(2,1)S(1)}, u32[]{:S(2)}, u32[]{:S(2)}) collective-permute-start(bf16[32,1280]{1,0:T(8,128)(2,1)} %cap_ref.3), channel_id=1, source_target_pairs={{0,32},{32,0},{1,33},{33,1},{2,34},{34,2},{3,35},{35,3},{4,36},{36... | collective-permute-start | bytes 245768 | tf_op jit(solution)/shard_map/ppermute | solution.py:292
  0.7 0.9 copy-start.3
  3.0 9.5 %collective-permute-start.1 = (bf16[2,32,1280]{2,1,0:T(8,128)(2,1)S(1)}, bf16[2,32,1280]{2,1,0:T(8,128)(2,1)S(1)}, u32[]{:S(2)}, u32[]{:S(2)}) collective-permute-start(bf16[2,32,1280]{2,1,0:T(8,128)(2,1)S(1)} %texts_kernel.1.chip_ref), channel_id=1, source_target_pairs={{0,4},{4,8},{8,12},{12,16},{16,20},{20,24},{24,28},{28,0},{32,60},... | collective-permute-start | bytes 491528 | tf_op jit(solution)/shard_map/ppermute | solution.py:281
  5.0 28.1 %all-to-all-start = ((bf16[16,32,1280]{2,1,0:T(8,128)(2,1)}), bf16[16,32,1280]{2,1,0:T(8,128)(2,1)S(1)}, u32[]{:S(2)}, u32[]{:S(2)}) async-start(bf16[16,32,1280]{2,1,0:T(8,128)(2,1)} %images_kernel.1.after_ref), calls=%async_computation | async-start | bytes 2621440 | tf_op jit(solution)/shard_map/all_to_all | solution.py:308
  12.6 15.2 %collective-permute-start.2 = (bf16[4,32,1280]{2,1,0:T(8,128)(2,1)S(1)}, bf16[4,32,1280]{2,1,0:T(8,128)(2,1)S(1)}, u32[]{:S(2)}, u32[]{:S(2)}) collective-permute-start(bf16[4,32,1280]{2,1,0:T(8,128)(2,1)S(1)} %tie_kernel.5), channel_id=1, source_target_pairs={{0,8},{4,12},{8,16},{12,20},{16,24},{20,28},{24,0},{28,4},{32,56},... | collective-permute-start | bytes 983048 | tf_op jit(solution)/shard_map/ppermute | solution.py:281
  16.6 14.9 %collective-permute-start.3 = (bf16[1,32,1280]{2,1,0:T(8,128)(2,1)S(1)}, bf16[1,32,1280]{2,1,0:T(8,128)(2,1)S(1)}, u32[]{:S(2)}, u32[]{:S(2)}) collective-permute-start(bf16[1,32,1280]{2,1,0:T(8,128)(2,1)S(1)} %slice.4), channel_id=1, source_target_pairs={{0,16},{4,20},{8,24},{12,28},{16,0},{20,4},{24,8},{28,12},{32,48},... | collective-permute-start | bytes 245768 | tf_op jit(solution)/shard_map/ppermute | solution.py:281
  31.5 2.0 %collective-permute-start.4 = (bf16[7,32,1280]{2,1,0:T(8,128)(2,1)S(1)}, bf16[7,32,1280]{2,1,0:T(8,128)(2,1)S(1)}, u32[]{:S(2)}, u32[]{:S(2)}) collective-permute-start(bf16[7,32,1280]{2,1,0:T(8,128)(2,1)S(1)} %constant_dynamic-update-slice_fusion.own_ref), channel_id=1, source_target_pairs={{0,32},{32,0},{1,33},{33,1},{2,34},{34,2},{3,35},{35,3},{4,36},{36... | collective-permute-start | bytes 1720328 | tf_op jit(solution)/shard_map/ppermute | solution.py:292
  33.4 0.8 copy-start
  34.3 1.1 %copy-start.1 = (bf16[7,32,1280]{2,1,0:T(8,128)(2,1)S(1)}, bf16[7,32,1280]{2,1,0:T(8,128)(2,1)}, u32[]{:S(2)}) copy-start(bf16[7,32,1280]{2,1,0:T(8,128)(2,1)} %copy-done) | copy-start | bytes 1720324
  37.9 1.2 %collective-permute-start.5 = (f32[16,128]{1,0:T(8,128)S(1)}, f32[16,128]{1,0:T(8,128)S(1)}, u32[]{:S(2)}, u32[]{:S(2)}) collective-permute-start(f32[16,128]{1,0:T(8,128)S(1)} %get-tuple-element.18), channel_id=1, source_target_pairs={{0,32},{32,0},{1,33},{33,1},{2,34},{34,2},{3,35},{35,3},{4,36},{36... | collective-permute-start | bytes 24584 | tf_op jit(solution)/shard_map/ppermute | solution.py:292
  39.1 10.8 %collective-permute-start.6 = (f32[2,16,128]{2,1,0:T(8,128)S(1)}, f32[2,16,128]{2,1,0:T(8,128)S(1)}, u32[]{:S(2)}, u32[]{:S(2)}) collective-permute-start(f32[2,16,128]{2,1,0:T(8,128)S(1)} %pad_maximum_fusion.2.chip_ref), channel_id=1, source_target_pairs={{0,4},{4,8},{8,12},{12,16},{16,20},{20,24},{24,28},{28,0},{32,60},... | collective-permute-start | bytes 49160 | tf_op jit(solution)/shard_map/ppermute | solution.py:281
  39.1 16.9 %collective-permute-start.8 = (f32[1,16,128]{2,1,0:T(8,128)S(1)}, f32[1,16,128]{2,1,0:T(8,128)S(1)}, u32[]{:S(2)}, u32[]{:S(2)}) collective-permute-start(f32[1,16,128]{2,1,0:T(8,128)S(1)} %bitcast.3), channel_id=1, source_target_pairs={{0,16},{4,20},{8,24},{12,28},{16,0},{20,4},{24,8},{28,12},{32,48},... | collective-permute-start | bytes 24584 | tf_op jit(solution)/shard_map/ppermute | solution.py:281
  43.6 12.6 %all-to-all-start.1 = ((f32[16,8,128]{2,1,0:T(8,128)}), f32[16,8,128]{2,1,0:T(8,128)S(1)}, u32[]{:S(2)}, u32[]{:S(2)}) async-start(f32[16,8,128]{2,1,0:T(8,128)} %get-tuple-element.17), calls=%async_computation.1 | async-start | bytes 131072 | tf_op jit(solution)/shard_map/all_to_all | solution.py:308
  49.9 6.1 %collective-permute-start.7 = (f32[4,16,128]{2,1,0:T(8,128)S(1)}, f32[4,16,128]{2,1,0:T(8,128)S(1)}, u32[]{:S(2)}, u32[]{:S(2)}) collective-permute-start(f32[4,16,128]{2,1,0:T(8,128)S(1)} %tie_kernel.7), channel_id=1, source_target_pairs={{0,8},{4,12},{8,16},{12,20},{16,24},{20,28},{24,0},{28,4},{32,56},... | collective-permute-start | bytes 98312 | tf_op jit(solution)/shard_map/ppermute | solution.py:281
  56.1 1.3 %collective-permute-start.9 = (f32[7,16,128]{2,1,0:T(8,128)S(1)}, f32[7,16,128]{2,1,0:T(8,128)S(1)}, u32[]{:S(2)}, u32[]{:S(2)}) collective-permute-start(f32[7,16,128]{2,1,0:T(8,128)S(1)} %constant_dynamic-update-slice_fusion.3.own_ref), channel_id=1, source_target_pairs={{0,32},{32,0},{1,33},{33,1},{2,34},{34,2},{3,35},{35,3},{4,36},{36... | collective-permute-start | bytes 172040 | tf_op jit(solution)/shard_map/ppermute | solution.py:292
  59.8 2.4 %collective-permute-start.10 = (bf16[8,336,128]{2,1,0:T(8,128)(2,1)S(1)}, bf16[8,336,128]{2,1,0:T(8,128)(2,1)S(1)}, u32[]{:S(2)}, u32[]{:S(2)}) collective-permute-start(bf16[8,336,128]{2,1,0:T(8,128)(2,1)S(1)} %get-tuple-element.20), channel_id=1, source_target_pairs={{0,32},{32,0},{1,33},{33,1},{2,34},{34,2},{3,35},{35,3},{4,36},{36... | collective-permute-start | bytes 2064392 | tf_op jit(solution)/shard_map/ppermute | solution.py:292
  62.4 12.5 %collective-permute-start.11 = (bf16[4,336,128]{2,1,0:T(8,128)(2,1)S(1)}, bf16[4,336,128]{2,1,0:T(8,128)(2,1)S(1)}, u32[]{:S(2)}, u32[]{:S(2)}) collective-permute-start(bf16[4,336,128]{2,1,0:T(8,128)(2,1)S(1)} %get-tuple-element.25), channel_id=1, source_target_pairs={{0,8},{4,12},{8,16},{12,20},{16,24},{20,28},{24,0},{28,4},{32,56},... | collective-permute-start | bytes 1032200 | tf_op jit(solution)/shard_map/ppermute | solution.py:281
  62.8 25.7 %all-to-all-start.2 = ((bf16[16,336,128]{2,1,0:T(8,128)(2,1)}), bf16[16,336,128]{2,1,0:T(8,128)(2,1)S(1)}, u32[]{:S(2)}, u32[]{:S(2)}) async-start(bf16[16,336,128]{2,1,0:T(8,128)(2,1)} %get-tuple-element.23), calls=%async_computation.2 | async-start | bytes 2752512 | tf_op jit(solution)/shard_map/all_to_all | solution.py:308
  74.9 13.7 %copy-start.4 = (bf16[32,1280]{1,0:T(8,128)(2,1)S(1)}, bf16[32,1280]{1,0:T(8,128)(2,1)}, u32[]{:S(2)}) copy-start(bf16[32,1280]{1,0:T(8,128)(2,1)} %pic_ref.3) | copy-start | bytes 245764
  75.0 8.9 %collective-permute-start.12 = (bf16[2,336,128]{2,1,0:T(8,128)(2,1)S(1)}, bf16[2,336,128]{2,1,0:T(8,128)(2,1)S(1)}, u32[]{:S(2)}, u32[]{:S(2)}) collective-permute-start(bf16[2,336,128]{2,1,0:T(8,128)(2,1)S(1)} %relay_kernel.1), channel_id=1, source_target_pairs={{0,4},{4,8},{8,12},{12,16},{16,20},{20,24},{24,28},{28,0},{32,60},... | collective-permute-start | bytes 516104 | tf_op jit(solution)/shard_map/ppermute | solution.py:281
  75.1 10.5 %collective-permute-start.13 = (bf16[336,128]{1,0:T(8,128)(2,1)S(1)}, bf16[336,128]{1,0:T(8,128)(2,1)S(1)}, u32[]{:S(2)}, u32[]{:S(2)}) collective-permute-start(bf16[336,128]{1,0:T(8,128)(2,1)S(1)} %get-tuple-element.27), channel_id=1, source_target_pairs={{0,16},{4,20},{8,24},{12,28},{16,0},{20,4},{24,8},{28,12},{32,48},... | collective-permute-start | bytes 258056 | tf_op jit(solution)/shard_map/ppermute | solution.py:281
  83.9 1.8 %collective-permute-start.14 = (bf16[336,128]{1,0:T(8,128)(2,1)S(1)}, bf16[336,128]{1,0:T(8,128)(2,1)S(1)}, u32[]{:S(2)}, u32[]{:S(2)}) collective-permute-start(bf16[336,128]{1,0:T(8,128)(2,1)S(1)} %pass_kernel.1), channel_id=1, source_target_pairs={{0,32},{32,0},{1,33},{33,1},{2,34},{34,2},{3,35},{35,3},{4,36},{36... | collective-permute-start | bytes 258056 | tf_op jit(solution)/shard_map/ppermute | solution.py:292

commit v3 on v2

--- a/solution.py
+++ b/solution.py
@@ -81,15 +81,24 @@
     return jnp.transpose(jnp.broadcast_to(column, (LANE, LANE)))[0:1, :]
 
 
-def logits_kernel(log_ref, img_ref, chip_ref, own_ref, other_ref, txt_ref, rowp_ref, colp_ref, logit_ref):
-    x, c, z, y = position()
+def ring_blocks(chip_ref, own_ref, other_ref, c, z):
     for ref, order in (
         (chip_ref, [(c, z), (1 - c, z)]),
         (own_ref, arrivals(c, z)),
         (other_ref, arrivals(1 - c, z)),
     ):
         for k, (core, at) in enumerate(order):
-            txt_ref[rows_at((core * NZ + at) * OWN, OWN), :] = ref[k]
+            yield ref[k], core * NZ + at
+
+
+def place_texts(chip_ref, own_ref, other_ref, txt_ref, c, z):
+    for block, place in ring_blocks(chip_ref, own_ref, other_ref, c, z):
+        txt_ref[rows_at(place * OWN, OWN), :] = block
+
+
+def logits_kernel(log_ref, img_ref, chip_ref, own_ref, other_ref, rowp_ref, colp_ref, txt_ref, logit_ref):
+    x, c, z, y = position()
+    place_texts(chip_ref, own_ref, other_ref, txt_ref, c, z)
     img = img_ref[...].reshape(TILE, img_ref.shape[2])
     scale = jnp.tile(scale_row(log_ref), (1, NB))
     logit_ref[...] = scale * similarity(img, txt_ref[...])
@@ -152,23 +161,23 @@
     return jnp.where(row == 0, high, jnp.where(row == 1, middle, jnp.where(row == 2, low, 0.0))).astype(BF16)
 
 
+def again_kernel(log_ref, img_ref, chip_ref, own_ref, other_ref, row_ref, logit_ref, txt_ref):
+    x, c, z, y = position()
+    place_texts(chip_ref, own_ref, other_ref, txt_ref, c, z)
+    logit_ref[...] = jnp.tile(scale_row(log_ref), (1, NB)) * similarity(
+        img_ref[...].reshape(TILE, img_ref.shape[2]), txt_ref[...]
+    )
+
+
 def grad_kernel(
-    log_ref, txt_ref, img_ref, rowg_ref, chip_ref, own_ref, other_ref,
-    grad_ref, keep_ref, send_ref, columns_ref, logit_ref, gradt, order_gradt, colg,
+    log_ref, logit_ref, img_ref, row_ref, chip_ref, own_ref, other_ref,
+    grad_ref, keep_ref, send_ref, columns_ref, gradt, order_gradt, colg,
 ):
     x, c, z, y = position()
     width = img_ref.shape[2]
-    for ref, order in (
-        (chip_ref, [(c, z), (1 - c, z)]),
-        (own_ref, arrivals(c, z)),
-        (other_ref, arrivals(1 - c, z)),
-    ):
-        for k, (core, at) in enumerate(order):
-            colg[core * NZ + at] = ref[k]
-    logit_ref[...] = jnp.tile(scale_row(log_ref), (1, NB)) * similarity(
-        img_ref[...].reshape(TILE, width), txt_ref[...]
-    )
-    row_lse, row_mean = combine(rowg_ref[:, :NB, :], rowg_ref[:, NB:, :])
+    for block, place in ring_blocks(chip_ref, own_ref, other_ref, c, z):
+        colg[place] = block
+    row_lse, row_mean = combine(row_ref[:, :NB, :], row_ref[:, NB:, :])
     col_lse, col_mean = combine(colg[:, :NB, :], colg[:, NB : 2 * NB, :])
     pos = all_sum(jnp.sum(colg[:, 2 * NB :, :], axis=0))
     rows_block = scalar_block(z * NC + c, all_sum(row_lse), 0.5 * all_sum(row_mean))
@@ -293,7 +302,7 @@
 
 
 def plane_member(slot, c):
-    return (slot + TURN_X * c) % NX, (slot // NX + TURN_Y * c) % NY
+    return (slot * (1 - c) + (slot // NY + 2) * c) % NX, (slot // NX * (1 - c) + (slot + 2) * c) % NY
 
 
 def plane(c, z):
@@ -353,21 +362,26 @@
     img = hint(exchange(img_out), 10)
     [chip] = call(texts_kernel, [shape((NC, OWN, width), BF16)], [VM] * 2 + [ANY])(cap, swap(cap), img_out)
     own, other = gather(chip, 10)
-    txt, rowp, colp = call(
+    rowp, colp = call(
         logits_kernel,
         [
-            shape((TILE, width), BF16),
             shape((NXY, 2 * NB, LANE), F32),
             shape((4 * NB, LANE), F32),
         ],
         [SM, VM, VM, VM, VM],
-        scratch=[pltpu.VMEM((TILE, TILE), F32)],
+        scratch=[pltpu.VMEM((TILE, width), BF16), pltpu.VMEM((TILE, TILE), F32)],
     )(log_scale, img, chip, own, other)
-    rowg = hint(exchange(rowp), 30)
-    chip = jnp.stack([colp, swap(colp)])
-    own, other = gather(chip, 10)
+    rows = exchange(rowp)
+    near = jnp.stack([colp, swap(colp)])
+    columns = gather(near, 10)
+    logits, txt = call(
+        again_kernel,
+        [shape((TILE, TILE), F32), shape((TILE, width), BF16)],
+        [SM] + [VM] * 4 + [ANY],
+        cost=cost(30),
+    )(log_scale, img, chip, own, other, rows)
     half = (NZ, long, LANE)
-    grad, keep, send, columns = call(
+    grad, keep, send, scalars = call(
         grad_kernel,
         [
             shape((TILE, TILE), BF16),
@@ -377,14 +391,13 @@
         ],
         [SM] + [VM] * 6,
         scratch=[
-            pltpu.VMEM((TILE, TILE), F32),
             pltpu.VMEM((TILE, TILE), BF16),
             pltpu.VMEM((TILE, TILE), BF16),
             pltpu.VMEM((NC * NZ, 4 * NB, LANE), F32),
         ],
-    )(log_scale, txt, img, rowg, chip, own, other)
+    )(log_scale, logits, img, rows, near, *columns)
     [terms] = call(terms_kernel, [shape((NXY, long, LANE), BF16)], [SM] + [VM] * 3, cost=cost(4))(
-        log_scale, grad, txt, columns
+        log_scale, grad, txt, scalars
     )
     one, two, keep, far, terms = call(
         add_kernel,

time: 91.1 us -> 87.8 us (0.964)
  local copies, waits for them, and re-layouts: 2.85 us -> 0.94 us
    unnamed x14 -> x10, local copies, waits for them, and re-layouts: 2.83 us -> 0.93 us
    all_to_all x3, waiting for transfers between devices: 4.64 us -> 3.59 us  [exchange(): lax.all_to_all(values, ('x', 'c', 'z', 'y'), 0, 0, axis_index_groups=PLAN...]
    pallas_call x1 -> x2, Pallas kernels: 2.58 us -> 3.61 us  [the longest x1 2.63 us: shards(): call(logits_kernel, [shape((NXY, 2 * NB, LANE), F32), shape((4 * NB, LANE...]
  transfers between devices with their start and end apart: 18 -> 18, of which waited for: 12 -> 12; matrix products, arithmetic and copies ran while one was open for 0% -> 0% of each run, Pallas kernels for 4% -> 5%
where the time goes in v3:
time: 87.8 us; the launch traced here: 87.3 us
  starting transfers between devices  40.5 us (46%)
  waiting for transfers between devices  34.2 us (39%)
  Pallas kernels  10 us (11%)
  between operations  1.6 us (2%)
  local copies, waits for them, and re-layouts  0.94 us (1%)
    ppermute x9, waiting for transfers between devices, shift(): return lax.ppermute(values, ('c', 'z'), pairs)  28.1 us
    all_to_all x3, starting transfers between devices, exchange(): lax.all_to_all(values, ('x', 'c', 'z', 'y'), 0, 0, axis_index_groups=PLAN...  20.7 us
    ppermute x9, starting transfers between devices, shift(): return lax.ppermute(values, ('c', 'z'), pairs)  18.8 us
    all_to_all x3, waiting for transfers between devices, exchange(): lax.all_to_all(values, ('x', 'c', 'z', 'y'), 0, 0, axis_index_groups=PLAN...  3.59 us
    pallas_call x1, Pallas kernels, shards(): call(logits_kernel, [shape((NXY, 2 * NB, LANE), F32), shape((4 * NB, LANE...  2.63 us
    ppermute x6, waiting for transfers between devices, swap(): return lax.ppermute(values, 'c', [(0, 1), (1, 0)])  2.52 us
    pallas_call x1, Pallas kernels, shards(): call(terms_kernel, [shape((NXY, long, LANE), BF16)], [SM] + [VM] * 3, cos...  1.96 us
    pallas_call x1, Pallas kernels, shards(): call(grad_kernel, [shape((TILE, TILE), BF16), shape(half, BF16), shape(ha...  1.8 us
  transfers between devices with their start and end apart: 18, of which 12 were waited for; matrix products, arithmetic and copies ran while one was open for 0% of the time, Pallas kernels for 5%

profile of v3, /device:TPU:2, one launch (start us, length us, event | category | flops | bytes accessed | tf_op | source)
XLA Modules:
  0.0 87.3 jit_solution(14493147329935685554)
XLA Ops:
  0.6 0.0 copy-start
  0.6 0.1 collective-permute-start
  0.7 0.0 copy-start.1
  0.8 0.9 %copy-done.1 = bf16[32,1280]{1,0:T(8,128)(2,1)S(1)} copy-done((bf16[32,1280]{1,0:T(8,128)(2,1)S(1)}, bf16[32,1280]{1,0:T(8,128)(2,1)}, u32[]{:S(2)}) %copy-start.1) | copy-done | bytes 81944
  1.6 1.3 %images_kernel.1.after_ref = bf16[16,32,1280]{2,1,0:T(8,128)(2,1)} custom-call(bf16[32,1280]{1,0:T(8,128)(2,1)S(1)} %copy-done.1), custom_call_target="tpu_custom_call" | custom-call | tf_op jit(solution)/shard_map/images_kernel/pallas_call | solution.py:361
  2.9 0.0 collective-permute-done.other_ref
  2.9 0.0 copy-done
  2.9 0.1 texts_kernel.1.chip_ref
  3.0 2.0 %collective-permute-start.1 = (bf16[2,32,1280]{2,1,0:T(8,128)(2,1)S(1)}, bf16[2,32,1280]{2,1,0:T(8,128)(2,1)S(1)}, u32[]{:S(2)}, u32[]{:S(2)}) collective-permute-start(bf16[2,32,1280]{2,1,0:T(8,128)(2,1)S(1)} %texts_kernel.1.chip_ref), channel_id=1, source_target_pairs={{0,4},{4,8},{8,12},{12,16},{16,20},{20,24},{24,28},{28,0},{32,60},... | collective-permute-start | bytes 491528 | tf_op jit(solution)/shard_map/ppermute | solution.py:290
  5.0 7.5 %all-to-all-start = ((bf16[16,32,1280]{2,1,0:T(8,128)(2,1)}), bf16[16,32,1280]{2,1,0:T(8,128)(2,1)S(1)}, u32[]{:S(2)}, u32[]{:S(2)}) async-start(bf16[16,32,1280]{2,1,0:T(8,128)(2,1)} %images_kernel.1.after_ref), calls=%async_computation | async-start | bytes 2621440 | tf_op jit(solution)/shard_map/all_to_all | solution.py:317
  12.5 0.0 collective-permute-done.1
  12.6 3.3 %collective-permute-start.2 = (bf16[4,32,1280]{2,1,0:T(8,128)(2,1)S(1)}, bf16[4,32,1280]{2,1,0:T(8,128)(2,1)S(1)}, u32[]{:S(2)}, u32[]{:S(2)}) collective-permute-start(bf16[4,32,1280]{2,1,0:T(8,128)(2,1)S(1)} %tie_kernel.4), channel_id=1, source_target_pairs={{0,8},{4,12},{8,16},{12,20},{16,24},{20,28},{24,0},{28,4},{32,56},... | collective-permute-start | bytes 983048 | tf_op jit(solution)/shard_map/ppermute | solution.py:290
  16.6 4.6 %collective-permute-start.3 = (bf16[1,32,1280]{2,1,0:T(8,128)(2,1)S(1)}, bf16[1,32,1280]{2,1,0:T(8,128)(2,1)S(1)}, u32[]{:S(2)}, u32[]{:S(2)}) collective-permute-start(bf16[1,32,1280]{2,1,0:T(8,128)(2,1)S(1)} %slice.4), channel_id=1, source_target_pairs={{0,16},{4,20},{8,24},{12,28},{16,0},{20,4},{24,8},{28,12},{32,48},... | collective-permute-start | bytes 245768 | tf_op jit(solution)/shard_map/ppermute | solution.py:290
  21.2 6.6 %collective-permute-done.2 = bf16[4,32,1280]{2,1,0:T(8,128)(2,1)S(1)} collective-permute-done((bf16[4,32,1280]{2,1,0:T(8,128)(2,1)S(1)}, bf16[4,32,1280]{2,1,0:T(8,128)(2,1)S(1)}, u32[]{:S(2)}, u32[]{:S(2)}) %collective-permute-start.2) | collective-permute-done | bytes 327712 | tf_op jit(solution)/shard_map/ppermute | solution.py:290
  27.8 3.7 %collective-permute-done.3 = bf16[1,32,1280]{2,1,0:T(8,128)(2,1)S(1)} collective-permute-done((bf16[1,32,1280]{2,1,0:T(8,128)(2,1)S(1)}, bf16[1,32,1280]{2,1,0:T(8,128)(2,1)S(1)}, u32[]{:S(2)}, u32[]{:S(2)}) %collective-permute-start.3) | collective-permute-done | bytes 81952 | tf_op jit(solution)/shard_map/ppermute | solution.py:290
  31.5 0.0 collective-permute-start.4
  31.5 0.7 all-to-all-done.ref
  32.1 1.3 %collective-permute-done.4.other_ref = bf16[7,32,1280]{2,1,0:T(8,128)(2,1)S(1)} collective-permute-done((bf16[7,32,1280]{2,1,0:T(8,128)(2,1)S(1)}, bf16[7,32,1280]{2,1,0:T(8,128)(2,1)S(1)}, u32[]{:S(2)}, u32[]{:S(2)}) %collective-permute-start.4) | collective-permute-done | bytes 573472 | tf_op jit(solution)/shard_map/ppermute | solution.py:301
  33.4 2.6 %logits_kernel.1 = (f32[16,8,128]{2,1,0:T(8,128)}, f32[16,128]{1,0:T(8,128)S(1)}) custom-call(f32[1]{0:T(128)S(6)} %copy.19.log_ref, bf16[16,32,1280]{2,1,0:T(8,128)(2,1)S(1)} %tie_kernel.3.img_ref, bf16[2,32,1280]{2,1,0:T(8,128)(2,1)S(1)} %texts_kernel.1.chip_ref, bf16[7,32,1280]{2,1,0:T(8,128)(2,1)S(1)} %constant_dynamic-update-slice_fusion.own_ref, ...), custom_call_target="tpu_custom_call" | custom-call | tf_op jit(solution)/shard_map/logits_kernel/pallas_call | solution.py:365
  36.1 0.1 collective-permute-start.5
  36.2 1.0 %collective-permute-done.5 = f32[16,128]{1,0:T(8,128)S(1)} collective-permute-done((f32[16,128]{1,0:T(8,128)S(1)}, f32[16,128]{1,0:T(8,128)S(1)}, u32[]{:S(2)}, u32[]{:S(2)}) %collective-permute-start.5) | collective-permute-done | bytes 8224 | tf_op jit(solution)/shard_map/ppermute | solution.py:301
  37.2 0.0 collective-permute-start.6
  37.2 4.3 %collective-permute-start.8 = (f32[1,16,128]{2,1,0:T(8,128)S(1)}, f32[1,16,128]{2,1,0:T(8,128)S(1)}, u32[]{:S(2)}, u32[]{:S(2)}) collective-permute-start(f32[1,16,128]{2,1,0:T(8,128)S(1)} %bitcast.3), channel_id=1, source_target_pairs={{0,16},{4,20},{8,24},{12,28},{16,0},{20,4},{24,8},{28,12},{32,48},... | collective-permute-start | bytes 24584 | tf_op jit(solution)/shard_map/ppermute | solution.py:290
  41.5 6.5 %all-to-all-start.1 = ((f32[16,8,128]{2,1,0:T(8,128)}), f32[16,8,128]{2,1,0:T(8,128)S(1)}, u32[]{:S(2)}, u32[]{:S(2)}) async-start(f32[16,8,128]{2,1,0:T(8,128)} %get-tuple-element.17), calls=%async_computation.1 | async-start | bytes 131072 | tf_op jit(solution)/shard_map/all_to_all | solution.py:317
  48.0 0.0 collective-permute-done.6
  48.1 0.6 collective-permute-start.7
  48.7 5.5 %collective-permute-done.7 = f32[4,16,128]{2,1,0:T(8,128)S(1)} collective-permute-done((f32[4,16,128]{2,1,0:T(8,128)S(1)}, f32[4,16,128]{2,1,0:T(8,128)S(1)}, u32[]{:S(2)}, u32[]{:S(2)}) %collective-permute-start.7) | collective-permute-done | bytes 32800 | tf_op jit(solution)/shard_map/ppermute | solution.py:290
  54.2 0.0 collective-permute-done.8
  54.2 0.1 collective-permute-start.9
  54.3 0.1 all-to-all-done.1.row_ref
  54.3 1.0 %again_kernel.1 = (f32[512,512]{1,0:T(8,128)S(1)}, bf16[512,1280]{1,0:T(8,128)(2,1)S(1)}) custom-call(f32[1]{0:T(128)S(6)} %copy.19.log_ref, bf16[16,32,1280]{2,1,0:T(8,128)(2,1)S(1)} %tie_kernel.3.img_ref, bf16[2,32,1280]{2,1,0:T(8,128)(2,1)S(1)} %texts_kernel.1.chip_ref, bf16[7,32,1280]{2,1,0:T(8,128)(2,1)S(1)} %constant_dynamic-update-slice_fusion.own_ref, ...), custom_call_target="tpu_custom_call" | custom-call | flops 34500001792 | tf_op jit(solution)/shard_map/again_kernel/pallas_call | solution.py:377
  55.3 0.2 collective-permute-done.9.other_ref
  55.5 1.8 %grad_kernel.1 = (bf16[512,512]{1,0:T(8,128)(2,1)S(1)}, bf16[8,336,128]{2,1,0:T(8,128)(2,1)S(1)}, bf16[8,336,128]{2,1,0:T(8,128)(2,1)S(1)}, bf16[16,128]{1,0:T(8,128)(2,1)S(1)}) custom-call(f32[1]{0:T(128)S(6)} %copy.19.log_ref, f32[512,512]{1,0:T(8,128)S(1)} %get-tuple-element.18.logit_ref, bf16[16,32,1280]{2,1,0:T(8,128)(2,1)S(1)} %tie_kernel.3.img_ref, ...), custom_call_target="tpu_custom_call" | custom-call | tf_op jit(solution)/shard_map/grad_kernel/pallas_call | solution.py:384
  57.3 0.5 collective-permute-start.10
  57.9 2.0 %terms_kernel.1.term_ref = bf16[16,336,128]{2,1,0:T(8,128)(2,1)} custom-call(f32[1]{0:T(128)S(6)} %copy.19.log_ref, bf16[512,512]{1,0:T(8,128)(2,1)S(1)} %get-tuple-element.22.grad_ref, bf16[512,1280]{1,0:T(8,128)(2,1)S(1)} %get-tuple-element.23.txt_ref, bf16[16,128]{1,0:T(8,128)(2,1)S(1)} %get-tuple-element.24.columns_ref), custom_call_target="tpu_custom_call" | custom-call | flops 4600000000 | tf_op jit(solution)/shard_map/terms_kernel/pallas_call | solution.py:399
  59.8 0.0 collective-permute-done.10.other_ref
  59.8 0.2 add_kernel.1
  60.0 0.6 collective-permute-start.11
  60.6 6.8 %all-to-all-start.2 = ((bf16[16,336,128]{2,1,0:T(8,128)(2,1)}), bf16[16,336,128]{2,1,0:T(8,128)(2,1)S(1)}, u32[]{:S(2)}, u32[]{:S(2)}) async-start(bf16[16,336,128]{2,1,0:T(8,128)(2,1)} %get-tuple-element.25), calls=%async_computation.2 | async-start | bytes 2752512 | tf_op jit(solution)/shard_map/all_to_all | solution.py:317
  67.3 5.3 %collective-permute-done.11.two_ref.refs_1_ = bf16[4,336,128]{2,1,0:T(8,128)(2,1)S(1)} collective-permute-done((bf16[4,336,128]{2,1,0:T(8,128)(2,1)S(1)}, bf16[4,336,128]{2,1,0:T(8,128)(2,1)S(1)}, u32[]{:S(2)}, u32[]{:S(2)}) %collective-permute-start.11) | collective-permute-done | bytes 344096 | tf_op jit(solution)/shard_map/ppermute | solution.py:290
  72.7 0.9 %collective-permute-start.12 = (bf16[2,336,128]{2,1,0:T(8,128)(2,1)S(1)}, bf16[2,336,128]{2,1,0:T(8,128)(2,1)S(1)}, u32[]{:S(2)}, u32[]{:S(2)}) collective-permute-start(bf16[2,336,128]{2,1,0:T(8,128)(2,1)S(1)} %relay_kernel.1), channel_id=1, source_target_pairs={{0,4},{4,8},{8,12},{12,16},{16,20},{20,24},{24,28},{28,0},{32,60},... | collective-permute-start | bytes 516104 | tf_op jit(solution)/shard_map/ppermute | solution.py:290
  73.6 2.5 %collective-permute-start.13 = (bf16[336,128]{1,0:T(8,128)(2,1)S(1)}, bf16[336,128]{1,0:T(8,128)(2,1)S(1)}, u32[]{:S(2)}, u32[]{:S(2)}) collective-permute-start(bf16[336,128]{1,0:T(8,128)(2,1)S(1)} %get-tuple-element.29), channel_id=1, source_target_pairs={{0,16},{4,20},{8,24},{12,28},{16,0},{20,4},{24,8},{28,12},{32,48},... | collective-permute-start | bytes 258056 | tf_op jit(solution)/shard_map/ppermute | solution.py:290
  76.1 5.5 %collective-permute-done.12.one_ref.refs_0_ = bf16[2,336,128]{2,1,0:T(8,128)(2,1)S(1)} collective-permute-done((bf16[2,336,128]{2,1,0:T(8,128)(2,1)S(1)}, bf16[2,336,128]{2,1,0:T(8,128)(2,1)S(1)}, u32[]{:S(2)}, u32[]{:S(2)}) %collective-permute-start.12) | collective-permute-done | bytes 172064 | tf_op jit(solution)/shard_map/ppermute | solution.py:290
  81.7 0.1 collective-permute-start.14
  81.8 1.4 %collective-permute-done.13.refs_3_ = bf16[336,128]{1,0:T(8,128)(2,1)S(1)} collective-permute-done((bf16[336,128]{1,0:T(8,128)(2,1)S(1)}, bf16[336,128]{1,0:T(8,128)(2,1)S(1)}, u32[]{:S(2)}, u32[]{:S(2)}) %collective-permute-start.13) | collective-permute-done | bytes 86048 | tf_op jit(solution)/shard_map/ppermute | solution.py:290
  83.2 0.0 collective-permute-done.14.refs_4_
  83.2 2.9 %all-to-all-done.2.term_ref = bf16[16,336,128]{2,1,0:T(8,128)(2,1)S(1)} async-done(((bf16[16,336,128]{2,1,0:T(8,128)(2,1)}), bf16[16,336,128]{2,1,0:T(8,128)(2,1)S(1)}, u32[]{:S(2)}, u32[]{:S(2)}) %all-to-all-start.2) | async-done | bytes 1376288 | tf_op jit(solution)/shard_map/all_to_all | solution.py:317
  86.1 1.0 %final_kernel.1 = (bf16[32,1280]{1,0:T(8,128)(2,1)}, bf16[32,1280]{1,0:T(8,128)(2,1)}, f32[1]{0:T(128)}, f32[1]{0:T(128)}) custom-call(bf16[32,1280]{1,0:T(8,128)(2,1)S(1)} %copy-done.2, bf16[32,1280]{1,0:T(8,128)(2,1)S(1)} %copy-done, bf16[16,336,128]{2,1,0:T(8,128)(2,1)S(1)} %all-to-all-done.2.term_ref, ...), custom_call_target="tpu_custom_call" | custom-call | tf_op jit(solution)/shard_map/final_kernel/pallas_call | solution.py:421
  (17 shorter events, 0.2 us)
Async XLA Ops:
  0.6 2.3 %copy-start = (bf16[32,1280]{1,0:T(8,128)(2,1)S(1)}, bf16[32,1280]{1,0:T(8,128)(2,1)}, u32[]{:S(2)}) copy-start(bf16[32,1280]{1,0:T(8,128)(2,1)} %cap_ref.3) | copy-start | bytes 245764
  0.6 2.3 %collective-permute-start = (bf16[32,1280]{1,0:T(8,128)(2,1)}, bf16[32,1280]{1,0:T(8,128)(2,1)S(1)}, u32[]{:S(2)}, u32[]{:S(2)}) collective-permute-start(bf16[32,1280]{1,0:T(8,128)(2,1)} %cap_ref.3), channel_id=1, source_target_pairs={{0,32},{32,0},{1,33},{33,1},{2,34},{34,2},{3,35},{35,3},{4,36},{36... | collective-permute-start | bytes 245768 | tf_op jit(solution)/shard_map/ppermute | solution.py:301
  0.7 0.9 %copy-start.1 = (bf16[32,1280]{1,0:T(8,128)(2,1)S(1)}, bf16[32,1280]{1,0:T(8,128)(2,1)}, u32[]{:S(2)}) copy-start(bf16[32,1280]{1,0:T(8,128)(2,1)} %pic_ref.3) | copy-start | bytes 245764
  3.0 9.5 %collective-permute-start.1 = (bf16[2,32,1280]{2,1,0:T(8,128)(2,1)S(1)}, bf16[2,32,1280]{2,1,0:T(8,128)(2,1)S(1)}, u32[]{:S(2)}, u32[]{:S(2)}) collective-permute-start(bf16[2,32,1280]{2,1,0:T(8,128)(2,1)S(1)} %texts_kernel.1.chip_ref), channel_id=1, source_target_pairs={{0,4},{4,8},{8,12},{12,16},{16,20},{20,24},{24,28},{28,0},{32,60},... | collective-permute-start | bytes 491528 | tf_op jit(solution)/shard_map/ppermute | solution.py:290
  5.0 27.1 %all-to-all-start = ((bf16[16,32,1280]{2,1,0:T(8,128)(2,1)}), bf16[16,32,1280]{2,1,0:T(8,128)(2,1)S(1)}, u32[]{:S(2)}, u32[]{:S(2)}) async-start(bf16[16,32,1280]{2,1,0:T(8,128)(2,1)} %images_kernel.1.after_ref), calls=%async_computation | async-start | bytes 2621440 | tf_op jit(solution)/shard_map/all_to_all | solution.py:317
  12.6 15.2 %collective-permute-start.2 = (bf16[4,32,1280]{2,1,0:T(8,128)(2,1)S(1)}, bf16[4,32,1280]{2,1,0:T(8,128)(2,1)S(1)}, u32[]{:S(2)}, u32[]{:S(2)}) collective-permute-start(bf16[4,32,1280]{2,1,0:T(8,128)(2,1)S(1)} %tie_kernel.4), channel_id=1, source_target_pairs={{0,8},{4,12},{8,16},{12,20},{16,24},{20,28},{24,0},{28,4},{32,56},... | collective-permute-start | bytes 983048 | tf_op jit(solution)/shard_map/ppermute | solution.py:290
  16.6 14.9 %collective-permute-start.3 = (bf16[1,32,1280]{2,1,0:T(8,128)(2,1)S(1)}, bf16[1,32,1280]{2,1,0:T(8,128)(2,1)S(1)}, u32[]{:S(2)}, u32[]{:S(2)}) collective-permute-start(bf16[1,32,1280]{2,1,0:T(8,128)(2,1)S(1)} %slice.4), channel_id=1, source_target_pairs={{0,16},{4,20},{8,24},{12,28},{16,0},{20,4},{24,8},{28,12},{32,48},... | collective-permute-start | bytes 245768 | tf_op jit(solution)/shard_map/ppermute | solution.py:290
  31.5 2.0 %collective-permute-start.4 = (bf16[7,32,1280]{2,1,0:T(8,128)(2,1)S(1)}, bf16[7,32,1280]{2,1,0:T(8,128)(2,1)S(1)}, u32[]{:S(2)}, u32[]{:S(2)}) collective-permute-start(bf16[7,32,1280]{2,1,0:T(8,128)(2,1)S(1)} %constant_dynamic-update-slice_fusion.own_ref), channel_id=1, source_target_pairs={{0,32},{32,0},{1,33},{33,1},{2,34},{34,2},{3,35},{35,3},{4,36},{36... | collective-permute-start | bytes 1720328 | tf_op jit(solution)/shard_map/ppermute | solution.py:301
  36.1 1.2 %collective-permute-start.5 = (f32[16,128]{1,0:T(8,128)S(1)}, f32[16,128]{1,0:T(8,128)S(1)}, u32[]{:S(2)}, u32[]{:S(2)}) collective-permute-start(f32[16,128]{1,0:T(8,128)S(1)} %get-tuple-element.19), channel_id=1, source_target_pairs={{0,32},{32,0},{1,33},{33,1},{2,34},{34,2},{3,35},{35,3},{4,36},{36... | collective-permute-start | bytes 24584 | tf_op jit(solution)/shard_map/ppermute | solution.py:301
  37.2 10.8 %collective-permute-start.6 = (f32[2,16,128]{2,1,0:T(8,128)S(1)}, f32[2,16,128]{2,1,0:T(8,128)S(1)}, u32[]{:S(2)}, u32[]{:S(2)}) collective-permute-start(f32[2,16,128]{2,1,0:T(8,128)S(1)} %pad_maximum_fusion.2.chip_ref), channel_id=1, source_target_pairs={{0,4},{4,8},{8,12},{12,16},{16,20},{20,24},{24,28},{28,0},{32,60},... | collective-permute-start | bytes 49160 | tf_op jit(solution)/shard_map/ppermute | solution.py:290
  37.2 16.9 %collective-permute-start.8 = (f32[1,16,128]{2,1,0:T(8,128)S(1)}, f32[1,16,128]{2,1,0:T(8,128)S(1)}, u32[]{:S(2)}, u32[]{:S(2)}) collective-permute-start(f32[1,16,128]{2,1,0:T(8,128)S(1)} %bitcast.3), channel_id=1, source_target_pairs={{0,16},{4,20},{8,24},{12,28},{16,0},{20,4},{24,8},{28,12},{32,48},... | collective-permute-start | bytes 24584 | tf_op jit(solution)/shard_map/ppermute | solution.py:290
  41.5 12.8 %all-to-all-start.1 = ((f32[16,8,128]{2,1,0:T(8,128)}), f32[16,8,128]{2,1,0:T(8,128)S(1)}, u32[]{:S(2)}, u32[]{:S(2)}) async-start(f32[16,8,128]{2,1,0:T(8,128)} %get-tuple-element.17), calls=%async_computation.1 | async-start | bytes 131072 | tf_op jit(solution)/shard_map/all_to_all | solution.py:317
  48.1 6.1 %collective-permute-start.7 = (f32[4,16,128]{2,1,0:T(8,128)S(1)}, f32[4,16,128]{2,1,0:T(8,128)S(1)}, u32[]{:S(2)}, u32[]{:S(2)}) collective-permute-start(f32[4,16,128]{2,1,0:T(8,128)S(1)} %tie_kernel.5), channel_id=1, source_target_pairs={{0,8},{4,12},{8,16},{12,20},{16,24},{20,28},{24,0},{28,4},{32,56},... | collective-permute-start | bytes 98312 | tf_op jit(solution)/shard_map/ppermute | solution.py:290
  54.2 1.3 %collective-permute-start.9 = (f32[7,16,128]{2,1,0:T(8,128)S(1)}, f32[7,16,128]{2,1,0:T(8,128)S(1)}, u32[]{:S(2)}, u32[]{:S(2)}) collective-permute-start(f32[7,16,128]{2,1,0:T(8,128)S(1)} %constant_dynamic-update-slice_fusion.3.own_ref), channel_id=1, source_target_pairs={{0,32},{32,0},{1,33},{33,1},{2,34},{34,2},{3,35},{35,3},{4,36},{36... | collective-permute-start | bytes 172040 | tf_op jit(solution)/shard_map/ppermute | solution.py:301
  57.3 2.5 %collective-permute-start.10 = (bf16[8,336,128]{2,1,0:T(8,128)(2,1)S(1)}, bf16[8,336,128]{2,1,0:T(8,128)(2,1)S(1)}, u32[]{:S(2)}, u32[]{:S(2)}) collective-permute-start(bf16[8,336,128]{2,1,0:T(8,128)(2,1)S(1)} %get-tuple-element.21), channel_id=1, source_target_pairs={{0,32},{32,0},{1,33},{33,1},{2,34},{34,2},{3,35},{35,3},{4,36},{36... | collective-permute-start | bytes 2064392 | tf_op jit(solution)/shard_map/ppermute | solution.py:301
  60.0 12.7 %collective-permute-start.11 = (bf16[4,336,128]{2,1,0:T(8,128)(2,1)S(1)}, bf16[4,336,128]{2,1,0:T(8,128)(2,1)S(1)}, u32[]{:S(2)}, u32[]{:S(2)}) collective-permute-start(bf16[4,336,128]{2,1,0:T(8,128)(2,1)S(1)} %get-tuple-element.27), channel_id=1, source_target_pairs={{0,8},{4,12},{8,16},{12,20},{16,24},{20,28},{24,0},{28,4},{32,56},... | collective-permute-start | bytes 1032200 | tf_op jit(solution)/shard_map/ppermute | solution.py:290
  60.6 25.5 %all-to-all-start.2 = ((bf16[16,336,128]{2,1,0:T(8,128)(2,1)}), bf16[16,336,128]{2,1,0:T(8,128)(2,1)S(1)}, u32[]{:S(2)}, u32[]{:S(2)}) async-start(bf16[16,336,128]{2,1,0:T(8,128)(2,1)} %get-tuple-element.25), calls=%async_computation.2 | async-start | bytes 2752512 | tf_op jit(solution)/shard_map/all_to_all | solution.py:317
  72.6 13.4 %copy-start.2 = (bf16[32,1280]{1,0:T(8,128)(2,1)S(1)}, bf16[32,1280]{1,0:T(8,128)(2,1)}, u32[]{:S(2)}) copy-start(bf16[32,1280]{1,0:T(8,128)(2,1)} %pic_ref.3) | copy-start | bytes 245764
  72.7 9.0 %collective-permute-start.12 = (bf16[2,336,128]{2,1,0:T(8,128)(2,1)S(1)}, bf16[2,336,128]{2,1,0:T(8,128)(2,1)S(1)}, u32[]{:S(2)}, u32[]{:S(2)}) collective-permute-start(bf16[2,336,128]{2,1,0:T(8,128)(2,1)S(1)} %relay_kernel.1), channel_id=1, source_target_pairs={{0,4},{4,8},{8,12},{12,16},{16,20},{20,24},{24,28},{28,0},{32,60},... | collective-permute-start | bytes 516104 | tf_op jit(solution)/shard_map/ppermute | solution.py:290
  73.6 9.6 %collective-permute-start.13 = (bf16[336,128]{1,0:T(8,128)(2,1)S(1)}, bf16[336,128]{1,0:T(8,128)(2,1)S(1)}, u32[]{:S(2)}, u32[]{:S(2)}) collective-permute-start(bf16[336,128]{1,0:T(8,128)(2,1)S(1)} %get-tuple-element.29), channel_id=1, source_target_pairs={{0,16},{4,20},{8,24},{12,28},{16,0},{20,4},{24,8},{28,12},{32,48},... | collective-permute-start | bytes 258056 | tf_op jit(solution)/shard_map/ppermute | solution.py:290
  81.7 1.5 %collective-permute-start.14 = (bf16[336,128]{1,0:T(8,128)(2,1)S(1)}, bf16[336,128]{1,0:T(8,128)(2,1)S(1)}, u32[]{:S(2)}, u32[]{:S(2)}) collective-permute-start(bf16[336,128]{1,0:T(8,128)(2,1)S(1)} %pass_kernel.1), channel_id=1, source_target_pairs={{0,32},{32,0},{1,33},{33,1},{2,34},{34,2},{3,35},{35,3},{4,36},{36... | collective-permute-start | bytes 258056 | tf_op jit(solution)/shard_map/ppermute | solution.py:301

commit v4 on v3

--- a/solution.py
+++ b/solution.py
@@ -62,14 +62,15 @@
     return jnp.exp(jnp.full((1, LANE), log_ref[0], F32))
 
 
-def pair_mask(j, q, x, c, z, y):
+def pair_mask(j, q, x, c, z, y, turned=False):
     row = lax.broadcasted_iota(jnp.int32, (LANE, 1), 0) + j * LANE
     col = lax.broadcasted_iota(jnp.int32, (1, LANE), 1) + q * LANE
-    slot = row // OWN
+    image_at, text_at = (col, row) if turned else (row, col)
+    slot = image_at // OWN
     at_x, at_y = plane_member(slot, c)
-    image = ((at_x * NC + c) * (NZ * NY) + z * NY + at_y) * OWN + row % OWN
-    part = col // OWN
-    text = (((part % NZ) * NY + y) * (NX * NC) + x * NC + part // NZ) * OWN + col % OWN
+    image = ((at_x * NC + c) * (NZ * NY) + z * NY + at_y) * OWN + image_at % OWN
+    part = text_at // OWN
+    text = (((part % NZ) * NY + y) * (NX * NC) + x * NC + part // NZ) * OWN + text_at % OWN
     return image == text
 
 
@@ -96,32 +97,47 @@
         txt_ref[rows_at(place * OWN, OWN), :] = block
 
 
-def logits_kernel(log_ref, img_ref, chip_ref, own_ref, other_ref, rowp_ref, colp_ref, txt_ref, logit_ref):
+def early_kernel(log_ref, img_ref, chip_ref, own_ref, part_ref, txt_ref):
+    width = img_ref.shape[2]
+    here = NC * OWN
+    txt_ref[:here, :] = chip_ref[...].reshape(here, width)
+    txt_ref[here:, :] = own_ref[...].reshape(own_ref.shape[0] * OWN, width)
+    scale = jnp.tile(scale_row(log_ref), (1, NB))
+    part_ref[...] = scale * similarity(txt_ref[...], img_ref[...].reshape(TILE, width))
+
+
+def logits_kernel(log_ref, img_ref, part_ref, other_ref, rowp_ref, colp_ref, logit_ref):
     x, c, z, y = position()
-    place_texts(chip_ref, own_ref, other_ref, txt_ref, c, z)
-    img = img_ref[...].reshape(TILE, img_ref.shape[2])
+    width = img_ref.shape[2]
+    places = [core * NZ + at for core, at in [(c, z), (1 - c, z), *arrivals(c, z), *arrivals(1 - c, z)]]
+    here = part_ref.shape[0]
     scale = jnp.tile(scale_row(log_ref), (1, NB))
-    logit_ref[...] = scale * similarity(img, txt_ref[...])
+    rest = scale * similarity(other_ref[...].reshape(TILE - here, width), img_ref[...].reshape(TILE, width))
+    for k, place in enumerate(places):
+        start = k * OWN
+        block = part_ref[start : start + OWN, :] if start < here else rest[start - here : start - here + OWN, :]
+        logit_ref[rows_at(place * OWN, OWN), :] = block
     pos = jnp.zeros((LANE, LANE), F32)
     for j in range(NB):
         piece = logit_ref[j * LANE : (j + 1) * LANE, :]
         peak = jnp.max(piece, axis=1, keepdims=True)
         shifted = jnp.exp(piece - peak)
         total = jnp.sum(shifted, axis=1, keepdims=True)
-        mean = to_lanes(jnp.sum(shifted * piece, axis=1, keepdims=True) / total)
-        lse = to_lanes(peak + jnp.log(total))
-        for slot in range(NXY):
-            rowp_ref[slot, j : j + 1, :] = lse
-            rowp_ref[slot, NB + j : NB + j + 1, :] = mean
+        colp_ref[j : j + 1, :] = to_lanes(peak + jnp.log(total))
+        colp_ref[NB + j : NB + j + 1, :] = to_lanes(jnp.sum(shifted * piece, axis=1, keepdims=True) / total)
         for q in range(NB):
-            pos += jnp.where(pair_mask(j, q, x, c, z, y), piece[:, q * LANE : (q + 1) * LANE], 0.0)
+            pair = pair_mask(j, q, x, c, z, y, turned=True)
+            pos += jnp.where(pair, piece[:, q * LANE : (q + 1) * LANE], 0.0)
     for q in range(NB):
         piece = logit_ref[:, q * LANE : (q + 1) * LANE]
         peak = jnp.max(piece, axis=0, keepdims=True)
         shifted = jnp.exp(piece - peak)
         total = jnp.sum(shifted, axis=0, keepdims=True)
-        colp_ref[q : q + 1, :] = peak + jnp.log(total)
-        colp_ref[NB + q : NB + q + 1, :] = jnp.sum(shifted * piece, axis=0, keepdims=True) / total
+        lse = peak + jnp.log(total)
+        mean = jnp.sum(shifted * piece, axis=0, keepdims=True) / total
+        for slot in range(NXY):
+            rowp_ref[slot, q : q + 1, :] = lse
+            rowp_ref[slot, NB + q : NB + q + 1, :] = mean
     pos = jnp.sum(pos, axis=0, keepdims=True)
     first = lax.broadcasted_iota(jnp.int32, (2 * NB, LANE), 0) == 0
     colp_ref[2 * NB :, :] = jnp.where(first, pos, 0.0)
@@ -215,18 +231,26 @@
         send_ref[k, last:, :] = rows_block
 
 
-def terms_kernel(log_ref, grad_ref, txt_ref, columns_ref, term_ref):
+def terms_kernel(log_ref, grad_ref, txt_ref, columns_ref, term_out, term_ref, sems):
     width = txt_ref.shape[1]
     step = 2 * LANE
     scale = jnp.tile(scale_row(log_ref), (1, 2))
+    for slot in range(NXY):
+        term_ref[slot, width // LANE * OWN :, :] = columns_ref[...]
+    copies = []
     for start in range(0, width, step):
         term = scale * jnp.dot(grad_ref[...], txt_ref[:, start : start + step], preferred_element_type=F32)
         term = term.astype(BF16)
         for k in range(2):
             lanes = slice(k * LANE, (k + 1) * LANE)
             term_ref[:, group_at(start // LANE + k), :] = term[:, lanes].reshape(NXY, OWN, LANE)
-    for slot in range(NXY):
-        term_ref[slot, width // LANE * OWN :, :] = columns_ref[...]
+        rows = pl.ds(start // LANE * OWN, 2 * OWN + (PAD if start + step == width else 0))
+        copies.append(
+            pltpu.make_async_copy(term_ref.at[:, rows, :], term_out.at[:, rows, :], sems.at[start // step])
+        )
+        copies[-1].start()
+    for copy in copies:
+        copy.wait()
 
 
 def add_kernel(keep_ref, other_ref, term_ref, *out_refs):
@@ -362,15 +386,20 @@
     img = hint(exchange(img_out), 10)
     [chip] = call(texts_kernel, [shape((NC, OWN, width), BF16)], [VM] * 2 + [ANY])(cap, swap(cap), img_out)
     own, other = gather(chip, 10)
+    here = (NC + own.shape[0]) * OWN
+    [part] = call(
+        early_kernel,
+        [shape((here, TILE), F32)],
+        [SM] + [VM] * 3,
+        scratch=[pltpu.VMEM((here, width), BF16)],
+        cost=cost(3),
+    )(log_scale, img, chip, own)
     rowp, colp = call(
         logits_kernel,
-        [
-            shape((NXY, 2 * NB, LANE), F32),
-            shape((4 * NB, LANE), F32),
-        ],
-        [SM, VM, VM, VM, VM],
-        scratch=[pltpu.VMEM((TILE, width), BF16), pltpu.VMEM((TILE, TILE), F32)],
-    )(log_scale, img, chip, own, other)
+        [shape((NXY, 2 * NB, LANE), F32), shape((4 * NB, LANE), F32)],
+        [SM, VM, VM, VM],
+        scratch=[pltpu.VMEM((TILE, TILE), F32)],
+    )(log_scale, img, part, other)
     rows = exchange(rowp)
     near = jnp.stack([colp, swap(colp)])
     columns = gather(near, 10)
@@ -396,9 +425,14 @@
             pltpu.VMEM((NC * NZ, 4 * NB, LANE), F32),
         ],
     )(log_scale, logits, img, rows, near, *columns)
-    [terms] = call(terms_kernel, [shape((NXY, long, LANE), BF16)], [SM] + [VM] * 3, cost=cost(4))(
-        log_scale, grad, txt, scalars
-    )
+    [terms] = call(
+        terms_kernel,
+        [shape((NXY, long, LANE), BF16)],
+        [SM] + [VM] * 3,
+        [ANY],
+        scratch=[pltpu.VMEM((NXY, long, LANE), BF16), pltpu.SemaphoreType.DMA((width // (2 * LANE),))],
+        cost=cost(4),
+    )(log_scale, grad, txt, scalars)
     one, two, keep, far, terms = call(
         add_kernel,
         [

time: 87.8 us -> 87.7 us (level)
    pallas_call x1 -> x2, Pallas kernels: 1.96 us -> 2.37 us  [the longest x1 1.8 us: shards(): call(terms_kernel, [shape((NXY, long, LANE), BF16)], [SM] + [VM] * 3, [AN...]
  transfers between devices with their start and end apart: 18 -> 18, of which waited for: 12 -> 13; matrix products, arithmetic and copies ran while one was open for 0% -> 0% of each run, Pallas kernels for 5% -> 5%
where the time goes in v4:
time: 87.7 us; the launch traced here: 86.9 us
  starting transfers between devices  39.9 us (45%)
  waiting for transfers between devices  34.6 us (39%)
  Pallas kernels  9.81 us (11%)
  between operations  1.63 us (2%)
  local copies, waits for them, and re-layouts  0.94 us (1%)
    ppermute x9, waiting for transfers between devices, shift(): return lax.ppermute(values, ('c', 'z'), pairs)  28.6 us
    all_to_all x3, starting transfers between devices, exchange(): lax.all_to_all(values, ('x', 'c', 'z', 'y'), 0, 0, axis_index_groups=PLAN...  20.4 us
    ppermute x9, starting transfers between devices, shift(): return lax.ppermute(values, ('c', 'z'), pairs)  18.6 us
    all_to_all x3, waiting for transfers between devices, exchange(): lax.all_to_all(values, ('x', 'c', 'z', 'y'), 0, 0, axis_index_groups=PLAN...  3.13 us
    ppermute x6, waiting for transfers between devices, swap(): return lax.ppermute(values, 'c', [(0, 1), (1, 0)])  2.81 us
    pallas_call x1, Pallas kernels, shards(): call(logits_kernel, [shape((NXY, 2 * NB, LANE), F32), shape((4 * NB, LANE...  2.01 us
    pallas_call x1, Pallas kernels, shards(): call(terms_kernel, [shape((NXY, long, LANE), BF16)], [SM] + [VM] * 3, [AN...  1.8 us
    pallas_call x1, Pallas kernels, shards(): call(grad_kernel, [shape((TILE, TILE), BF16), shape(half, BF16), shape(ha...  1.8 us
  transfers between devices with their start and end apart: 18, of which 13 were waited for; matrix products, arithmetic and copies ran while one was open for 0% of the time, Pallas kernels for 5%

profile of v4, /device:TPU:2, one launch (start us, length us, event | category | flops | bytes accessed | tf_op | source)
XLA Modules:
  0.0 86.9 jit_solution(8765695951243777659)
XLA Ops:
  0.6 0.0 copy-start
  0.6 0.1 collective-permute-start
  0.7 0.0 copy-start.1
  0.8 0.9 %copy-done.1 = bf16[32,1280]{1,0:T(8,128)(2,1)S(1)} copy-done((bf16[32,1280]{1,0:T(8,128)(2,1)S(1)}, bf16[32,1280]{1,0:T(8,128)(2,1)}, u32[]{:S(2)}) %copy-start.1) | copy-done | bytes 81944
  1.6 1.3 %images_kernel.1.after_ref = bf16[16,32,1280]{2,1,0:T(8,128)(2,1)} custom-call(bf16[32,1280]{1,0:T(8,128)(2,1)S(1)} %copy-done.1), custom_call_target="tpu_custom_call" | custom-call | tf_op jit(solution)/shard_map/images_kernel/pallas_call | solution.py:385
  2.9 0.0 collective-permute-done.other_ref
  2.9 0.1 texts_kernel.1.chip_ref
  3.0 2.0 %collective-permute-start.1 = (bf16[2,32,1280]{2,1,0:T(8,128)(2,1)S(1)}, bf16[2,32,1280]{2,1,0:T(8,128)(2,1)S(1)}, u32[]{:S(2)}, u32[]{:S(2)}) collective-permute-start(bf16[2,32,1280]{2,1,0:T(8,128)(2,1)S(1)} %texts_kernel.1.chip_ref), channel_id=1, source_target_pairs={{0,4},{4,8},{8,12},{12,16},{16,20},{20,24},{24,28},{28,0},{32,60},... | collective-permute-start | bytes 491528 | tf_op jit(solution)/shard_map/ppermute | solution.py:314
  5.0 7.5 %all-to-all-start = ((bf16[16,32,1280]{2,1,0:T(8,128)(2,1)}), bf16[16,32,1280]{2,1,0:T(8,128)(2,1)S(1)}, u32[]{:S(2)}, u32[]{:S(2)}) async-start(bf16[16,32,1280]{2,1,0:T(8,128)(2,1)} %images_kernel.1.after_ref), calls=%async_computation | async-start | bytes 2621440 | tf_op jit(solution)/shard_map/all_to_all | solution.py:341
  12.5 0.0 collective-permute-done.1
  12.6 3.3 %collective-permute-start.2 = (bf16[4,32,1280]{2,1,0:T(8,128)(2,1)S(1)}, bf16[4,32,1280]{2,1,0:T(8,128)(2,1)S(1)}, u32[]{:S(2)}, u32[]{:S(2)}) collective-permute-start(bf16[4,32,1280]{2,1,0:T(8,128)(2,1)S(1)} %tie_kernel.4), channel_id=1, source_target_pairs={{0,8},{4,12},{8,16},{12,20},{16,24},{20,28},{24,0},{28,4},{32,56},... | collective-permute-start | bytes 983048 | tf_op jit(solution)/shard_map/ppermute | solution.py:314
  16.6 4.6 %collective-permute-start.3 = (bf16[1,32,1280]{2,1,0:T(8,128)(2,1)S(1)}, bf16[1,32,1280]{2,1,0:T(8,128)(2,1)S(1)}, u32[]{:S(2)}, u32[]{:S(2)}) collective-permute-start(bf16[1,32,1280]{2,1,0:T(8,128)(2,1)S(1)} %slice.4), channel_id=1, source_target_pairs={{0,16},{4,20},{8,24},{12,28},{16,0},{20,4},{24,8},{28,12},{32,48},... | collective-permute-start | bytes 245768 | tf_op jit(solution)/shard_map/ppermute | solution.py:314
  21.2 6.6 %collective-permute-done.2 = bf16[4,32,1280]{2,1,0:T(8,128)(2,1)S(1)} collective-permute-done((bf16[4,32,1280]{2,1,0:T(8,128)(2,1)S(1)}, bf16[4,32,1280]{2,1,0:T(8,128)(2,1)S(1)}, u32[]{:S(2)}, u32[]{:S(2)}) %collective-permute-start.2) | collective-permute-done | bytes 327712 | tf_op jit(solution)/shard_map/ppermute | solution.py:314
  27.8 3.7 %collective-permute-done.3 = bf16[1,32,1280]{2,1,0:T(8,128)(2,1)S(1)} collective-permute-done((bf16[1,32,1280]{2,1,0:T(8,128)(2,1)S(1)}, bf16[1,32,1280]{2,1,0:T(8,128)(2,1)S(1)}, u32[]{:S(2)}, u32[]{:S(2)}) %collective-permute-start.3) | collective-permute-done | bytes 81952 | tf_op jit(solution)/shard_map/ppermute | solution.py:314
  31.5 0.0 collective-permute-start.4
  31.5 0.7 all-to-all-done.ref
  32.1 0.6 early_kernel.1.part_ref
  32.7 0.7 collective-permute-done.4.other_ref
  33.4 2.0 %logits_kernel.1 = (f32[16,8,128]{2,1,0:T(8,128)}, f32[16,128]{1,0:T(8,128)S(1)}) custom-call(f32[1]{0:T(128)S(6)} %copy.19.log_ref, bf16[16,32,1280]{2,1,0:T(8,128)(2,1)S(1)} %tie_kernel.3.img_ref, f32[288,512]{1,0:T(8,128)S(1)} %early_kernel.1.part_ref, bf16[7,32,1280]{2,1,0:T(8,128)(2,1)S(1)} %collective-permute-done.4.other_ref), custom_call_target="tpu_custom_call" | custom-call | tf_op jit(solution)/shard_map/logits_kernel/pallas_call | solution.py:397
  35.4 0.1 collective-permute-start.5
  35.6 1.0 %collective-permute-done.5 = f32[16,128]{1,0:T(8,128)S(1)} collective-permute-done((f32[16,128]{1,0:T(8,128)S(1)}, f32[16,128]{1,0:T(8,128)S(1)}, u32[]{:S(2)}, u32[]{:S(2)}) %collective-permute-start.5) | collective-permute-done | bytes 8224 | tf_op jit(solution)/shard_map/ppermute | solution.py:325
  36.6 0.0 collective-permute-start.6
  36.6 4.9 %collective-permute-start.8 = (f32[1,16,128]{2,1,0:T(8,128)S(1)}, f32[1,16,128]{2,1,0:T(8,128)S(1)}, u32[]{:S(2)}, u32[]{:S(2)}) collective-permute-start(f32[1,16,128]{2,1,0:T(8,128)S(1)} %bitcast.3), channel_id=1, source_target_pairs={{0,16},{4,20},{8,24},{12,28},{16,0},{20,4},{24,8},{28,12},{32,48},... | collective-permute-start | bytes 24584 | tf_op jit(solution)/shard_map/ppermute | solution.py:314
  41.5 5.9 %all-to-all-start.1 = ((f32[16,8,128]{2,1,0:T(8,128)}), f32[16,8,128]{2,1,0:T(8,128)S(1)}, u32[]{:S(2)}, u32[]{:S(2)}) async-start(f32[16,8,128]{2,1,0:T(8,128)} %get-tuple-element.17), calls=%async_computation.1 | async-start | bytes 131072 | tf_op jit(solution)/shard_map/all_to_all | solution.py:341
  47.4 0.0 collective-permute-done.6
  47.4 0.8 collective-permute-start.7
  48.2 5.7 %collective-permute-done.7 = f32[4,16,128]{2,1,0:T(8,128)S(1)} collective-permute-done((f32[4,16,128]{2,1,0:T(8,128)S(1)}, f32[4,16,128]{2,1,0:T(8,128)S(1)}, u32[]{:S(2)}, u32[]{:S(2)}) %collective-permute-start.7) | collective-permute-done | bytes 32800 | tf_op jit(solution)/shard_map/ppermute | solution.py:314
  53.9 0.0 collective-permute-done.8
  53.9 0.1 collective-permute-start.9
  54.0 0.0 all-to-all-done.1.row_ref
  54.0 1.0 %again_kernel.1 = (f32[512,512]{1,0:T(8,128)S(1)}, bf16[512,1280]{1,0:T(8,128)(2,1)S(1)}) custom-call(f32[1]{0:T(128)S(6)} %copy.19.log_ref, bf16[16,32,1280]{2,1,0:T(8,128)(2,1)S(1)} %tie_kernel.3.img_ref, bf16[2,32,1280]{2,1,0:T(8,128)(2,1)S(1)} %texts_kernel.1.chip_ref, bf16[7,32,1280]{2,1,0:T(8,128)(2,1)S(1)} %constant_dynamic-update-slice_fusion.own_ref, ...), custom_call_target="tpu_custom_call" | custom-call | flops 34500001792 | tf_op jit(solution)/shard_map/again_kernel/pallas_call | solution.py:406
  55.0 0.2 collective-permute-done.9.other_ref
  55.2 1.8 %grad_kernel.1 = (bf16[512,512]{1,0:T(8,128)(2,1)S(1)}, bf16[8,336,128]{2,1,0:T(8,128)(2,1)S(1)}, bf16[8,336,128]{2,1,0:T(8,128)(2,1)S(1)}, bf16[16,128]{1,0:T(8,128)(2,1)S(1)}) custom-call(f32[1]{0:T(128)S(6)} %copy.19.log_ref, f32[512,512]{1,0:T(8,128)S(1)} %get-tuple-element.18.logit_ref, bf16[16,32,1280]{2,1,0:T(8,128)(2,1)S(1)} %tie_kernel.3.img_ref, ...), custom_call_target="tpu_custom_call" | custom-call | tf_op jit(solution)/shard_map/grad_kernel/pallas_call | solution.py:413
  57.0 0.5 collective-permute-start.10
  57.6 1.8 %terms_kernel.1.term_ref = bf16[16,336,128]{2,1,0:T(8,128)(2,1)} custom-call(f32[1]{0:T(128)S(6)} %copy.19.log_ref, bf16[512,512]{1,0:T(8,128)(2,1)S(1)} %get-tuple-element.22.grad_ref, bf16[512,1280]{1,0:T(8,128)(2,1)S(1)} %get-tuple-element.23.txt_ref, bf16[16,128]{1,0:T(8,128)(2,1)S(1)} %get-tuple-element.24.columns_ref), custom_call_target="tpu_custom_call" | custom-call | flops 4600000000 | tf_op jit(solution)/shard_map/terms_kernel/pallas_call | solution.py:428
  59.4 0.1 collective-permute-done.10.other_ref
  59.5 0.2 add_kernel.1
  59.6 0.3 collective-permute-start.11
  59.9 7.0 %all-to-all-start.2 = ((bf16[16,336,128]{2,1,0:T(8,128)(2,1)}), bf16[16,336,128]{2,1,0:T(8,128)(2,1)S(1)}, u32[]{:S(2)}, u32[]{:S(2)}) async-start(bf16[16,336,128]{2,1,0:T(8,128)(2,1)} %get-tuple-element.25), calls=%async_computation.2 | async-start | bytes 2752512 | tf_op jit(solution)/shard_map/all_to_all | solution.py:341
  66.9 5.7 %collective-permute-done.11.two_ref.refs_1_ = bf16[4,336,128]{2,1,0:T(8,128)(2,1)S(1)} collective-permute-done((bf16[4,336,128]{2,1,0:T(8,128)(2,1)S(1)}, bf16[4,336,128]{2,1,0:T(8,128)(2,1)S(1)}, u32[]{:S(2)}, u32[]{:S(2)}) %collective-permute-start.11) | collective-permute-done | bytes 344096 | tf_op jit(solution)/shard_map/ppermute | solution.py:314
  72.7 0.1 collective-permute-start.12
  72.8 2.6 %collective-permute-start.13 = (bf16[336,128]{1,0:T(8,128)(2,1)S(1)}, bf16[336,128]{1,0:T(8,128)(2,1)S(1)}, u32[]{:S(2)}, u32[]{:S(2)}) collective-permute-start(bf16[336,128]{1,0:T(8,128)(2,1)S(1)} %get-tuple-element.29), channel_id=1, source_target_pairs={{0,16},{4,20},{8,24},{12,28},{16,0},{20,4},{24,8},{28,12},{32,48},... | collective-permute-start | bytes 258056 | tf_op jit(solution)/shard_map/ppermute | solution.py:314
  75.4 6.4 %collective-permute-done.12.one_ref.refs_0_ = bf16[2,336,128]{2,1,0:T(8,128)(2,1)S(1)} collective-permute-done((bf16[2,336,128]{2,1,0:T(8,128)(2,1)S(1)}, bf16[2,336,128]{2,1,0:T(8,128)(2,1)S(1)}, u32[]{:S(2)}, u32[]{:S(2)}) %collective-permute-start.12) | collective-permute-done | bytes 172064 | tf_op jit(solution)/shard_map/ppermute | solution.py:314
  81.9 0.1 collective-permute-start.14
  82.0 0.5 collective-permute-done.13.refs_3_
  82.5 0.8 collective-permute-done.14.refs_4_
  83.3 2.5 %all-to-all-done.2.term_ref = bf16[16,336,128]{2,1,0:T(8,128)(2,1)S(1)} async-done(((bf16[16,336,128]{2,1,0:T(8,128)(2,1)}), bf16[16,336,128]{2,1,0:T(8,128)(2,1)S(1)}, u32[]{:S(2)}, u32[]{:S(2)}) %all-to-all-start.2) | async-done | bytes 1376288 | tf_op jit(solution)/shard_map/all_to_all | solution.py:341
  85.7 1.0 %final_kernel.1 = (bf16[32,1280]{1,0:T(8,128)(2,1)}, bf16[32,1280]{1,0:T(8,128)(2,1)}, f32[1]{0:T(128)}, f32[1]{0:T(128)}) custom-call(bf16[32,1280]{1,0:T(8,128)(2,1)S(1)} %copy-done.2, bf16[32,1280]{1,0:T(8,128)(2,1)S(1)} %copy-done, bf16[16,336,128]{2,1,0:T(8,128)(2,1)S(1)} %all-to-all-done.2.term_ref, ...), custom_call_target="tpu_custom_call" | custom-call | tf_op jit(solution)/shard_map/final_kernel/pallas_call | solution.py:455
  (18 shorter events, 0.2 us)
Async XLA Ops:
  0.6 2.3 %copy-start = (bf16[32,1280]{1,0:T(8,128)(2,1)S(1)}, bf16[32,1280]{1,0:T(8,128)(2,1)}, u32[]{:S(2)}) copy-start(bf16[32,1280]{1,0:T(8,128)(2,1)} %cap_ref.3) | copy-start | bytes 245764
  0.6 2.3 %collective-permute-start = (bf16[32,1280]{1,0:T(8,128)(2,1)}, bf16[32,1280]{1,0:T(8,128)(2,1)S(1)}, u32[]{:S(2)}, u32[]{:S(2)}) collective-permute-start(bf16[32,1280]{1,0:T(8,128)(2,1)} %cap_ref.3), channel_id=1, source_target_pairs={{0,32},{32,0},{1,33},{33,1},{2,34},{34,2},{3,35},{35,3},{4,36},{36... | collective-permute-start | bytes 245768 | tf_op jit(solution)/shard_map/ppermute | solution.py:325
  0.7 0.9 %copy-start.1 = (bf16[32,1280]{1,0:T(8,128)(2,1)S(1)}, bf16[32,1280]{1,0:T(8,128)(2,1)}, u32[]{:S(2)}) copy-start(bf16[32,1280]{1,0:T(8,128)(2,1)} %pic_ref.3) | copy-start | bytes 245764
  3.0 9.5 %collective-permute-start.1 = (bf16[2,32,1280]{2,1,0:T(8,128)(2,1)S(1)}, bf16[2,32,1280]{2,1,0:T(8,128)(2,1)S(1)}, u32[]{:S(2)}, u32[]{:S(2)}) collective-permute-start(bf16[2,32,1280]{2,1,0:T(8,128)(2,1)S(1)} %texts_kernel.1.chip_ref), channel_id=1, source_target_pairs={{0,4},{4,8},{8,12},{12,16},{16,20},{20,24},{24,28},{28,0},{32,60},... | collective-permute-start | bytes 491528 | tf_op jit(solution)/shard_map/ppermute | solution.py:314
  5.0 27.1 %all-to-all-start = ((bf16[16,32,1280]{2,1,0:T(8,128)(2,1)}), bf16[16,32,1280]{2,1,0:T(8,128)(2,1)S(1)}, u32[]{:S(2)}, u32[]{:S(2)}) async-start(bf16[16,32,1280]{2,1,0:T(8,128)(2,1)} %images_kernel.1.after_ref), calls=%async_computation | async-start | bytes 2621440 | tf_op jit(solution)/shard_map/all_to_all | solution.py:341
  12.6 15.2 %collective-permute-start.2 = (bf16[4,32,1280]{2,1,0:T(8,128)(2,1)S(1)}, bf16[4,32,1280]{2,1,0:T(8,128)(2,1)S(1)}, u32[]{:S(2)}, u32[]{:S(2)}) collective-permute-start(bf16[4,32,1280]{2,1,0:T(8,128)(2,1)S(1)} %tie_kernel.4), channel_id=1, source_target_pairs={{0,8},{4,12},{8,16},{12,20},{16,24},{20,28},{24,0},{28,4},{32,56},... | collective-permute-start | bytes 983048 | tf_op jit(solution)/shard_map/ppermute | solution.py:314
  16.6 14.9 %collective-permute-start.3 = (bf16[1,32,1280]{2,1,0:T(8,128)(2,1)S(1)}, bf16[1,32,1280]{2,1,0:T(8,128)(2,1)S(1)}, u32[]{:S(2)}, u32[]{:S(2)}) collective-permute-start(bf16[1,32,1280]{2,1,0:T(8,128)(2,1)S(1)} %slice.4), channel_id=1, source_target_pairs={{0,16},{4,20},{8,24},{12,28},{16,0},{20,4},{24,8},{28,12},{32,48},... | collective-permute-start | bytes 245768 | tf_op jit(solution)/shard_map/ppermute | solution.py:314
  31.5 2.0 %collective-permute-start.4 = (bf16[7,32,1280]{2,1,0:T(8,128)(2,1)S(1)}, bf16[7,32,1280]{2,1,0:T(8,128)(2,1)S(1)}, u32[]{:S(2)}, u32[]{:S(2)}) collective-permute-start(bf16[7,32,1280]{2,1,0:T(8,128)(2,1)S(1)} %constant_dynamic-update-slice_fusion.own_ref), channel_id=1, source_target_pairs={{0,32},{32,0},{1,33},{33,1},{2,34},{34,2},{3,35},{35,3},{4,36},{36... | collective-permute-start | bytes 1720328 | tf_op jit(solution)/shard_map/ppermute | solution.py:325
  35.4 1.2 %collective-permute-start.5 = (f32[16,128]{1,0:T(8,128)S(1)}, f32[16,128]{1,0:T(8,128)S(1)}, u32[]{:S(2)}, u32[]{:S(2)}) collective-permute-start(f32[16,128]{1,0:T(8,128)S(1)} %get-tuple-element.19), channel_id=1, source_target_pairs={{0,32},{32,0},{1,33},{33,1},{2,34},{34,2},{3,35},{35,3},{4,36},{36... | collective-permute-start | bytes 24584 | tf_op jit(solution)/shard_map/ppermute | solution.py:325
  36.6 10.8 %collective-permute-start.6 = (f32[2,16,128]{2,1,0:T(8,128)S(1)}, f32[2,16,128]{2,1,0:T(8,128)S(1)}, u32[]{:S(2)}, u32[]{:S(2)}) collective-permute-start(f32[2,16,128]{2,1,0:T(8,128)S(1)} %pad_maximum_fusion.2.chip_ref), channel_id=1, source_target_pairs={{0,4},{4,8},{8,12},{12,16},{16,20},{20,24},{24,28},{28,0},{32,60},... | collective-permute-start | bytes 49160 | tf_op jit(solution)/shard_map/ppermute | solution.py:314
  36.6 17.3 %collective-permute-start.8 = (f32[1,16,128]{2,1,0:T(8,128)S(1)}, f32[1,16,128]{2,1,0:T(8,128)S(1)}, u32[]{:S(2)}, u32[]{:S(2)}) collective-permute-start(f32[1,16,128]{2,1,0:T(8,128)S(1)} %bitcast.3), channel_id=1, source_target_pairs={{0,16},{4,20},{8,24},{12,28},{16,0},{20,4},{24,8},{28,12},{32,48},... | collective-permute-start | bytes 24584 | tf_op jit(solution)/shard_map/ppermute | solution.py:314
  41.5 12.5 %all-to-all-start.1 = ((f32[16,8,128]{2,1,0:T(8,128)}), f32[16,8,128]{2,1,0:T(8,128)S(1)}, u32[]{:S(2)}, u32[]{:S(2)}) async-start(f32[16,8,128]{2,1,0:T(8,128)} %get-tuple-element.17), calls=%async_computation.1 | async-start | bytes 131072 | tf_op jit(solution)/shard_map/all_to_all | solution.py:341
  47.4 6.4 %collective-permute-start.7 = (f32[4,16,128]{2,1,0:T(8,128)S(1)}, f32[4,16,128]{2,1,0:T(8,128)S(1)}, u32[]{:S(2)}, u32[]{:S(2)}) collective-permute-start(f32[4,16,128]{2,1,0:T(8,128)S(1)} %tie_kernel.5), channel_id=1, source_target_pairs={{0,8},{4,12},{8,16},{12,20},{16,24},{20,28},{24,0},{28,4},{32,56},... | collective-permute-start | bytes 98312 | tf_op jit(solution)/shard_map/ppermute | solution.py:314
  53.9 1.3 %collective-permute-start.9 = (f32[7,16,128]{2,1,0:T(8,128)S(1)}, f32[7,16,128]{2,1,0:T(8,128)S(1)}, u32[]{:S(2)}, u32[]{:S(2)}) collective-permute-start(f32[7,16,128]{2,1,0:T(8,128)S(1)} %constant_dynamic-update-slice_fusion.3.own_ref), channel_id=1, source_target_pairs={{0,32},{32,0},{1,33},{33,1},{2,34},{34,2},{3,35},{35,3},{4,36},{36... | collective-permute-start | bytes 172040 | tf_op jit(solution)/shard_map/ppermute | solution.py:325
  57.0 2.4 %collective-permute-start.10 = (bf16[8,336,128]{2,1,0:T(8,128)(2,1)S(1)}, bf16[8,336,128]{2,1,0:T(8,128)(2,1)S(1)}, u32[]{:S(2)}, u32[]{:S(2)}) collective-permute-start(bf16[8,336,128]{2,1,0:T(8,128)(2,1)S(1)} %get-tuple-element.21), channel_id=1, source_target_pairs={{0,32},{32,0},{1,33},{33,1},{2,34},{34,2},{3,35},{35,3},{4,36},{36... | collective-permute-start | bytes 2064392 | tf_op jit(solution)/shard_map/ppermute | solution.py:325
  59.6 13.1 %collective-permute-start.11 = (bf16[4,336,128]{2,1,0:T(8,128)(2,1)S(1)}, bf16[4,336,128]{2,1,0:T(8,128)(2,1)S(1)}, u32[]{:S(2)}, u32[]{:S(2)}) collective-permute-start(bf16[4,336,128]{2,1,0:T(8,128)(2,1)S(1)} %get-tuple-element.27), channel_id=1, source_target_pairs={{0,8},{4,12},{8,16},{12,20},{16,24},{20,28},{24,0},{28,4},{32,56},... | collective-permute-start | bytes 1032200 | tf_op jit(solution)/shard_map/ppermute | solution.py:314
  59.9 25.8 %all-to-all-start.2 = ((bf16[16,336,128]{2,1,0:T(8,128)(2,1)}), bf16[16,336,128]{2,1,0:T(8,128)(2,1)S(1)}, u32[]{:S(2)}, u32[]{:S(2)}) async-start(bf16[16,336,128]{2,1,0:T(8,128)(2,1)} %get-tuple-element.25), calls=%async_computation.2 | async-start | bytes 2752512 | tf_op jit(solution)/shard_map/all_to_all | solution.py:341
  72.7 13.0 %copy-start.2 = (bf16[32,1280]{1,0:T(8,128)(2,1)S(1)}, bf16[32,1280]{1,0:T(8,128)(2,1)}, u32[]{:S(2)}) copy-start(bf16[32,1280]{1,0:T(8,128)(2,1)} %pic_ref.3) | copy-start | bytes 245764
  72.7 9.1 %collective-permute-start.12 = (bf16[2,336,128]{2,1,0:T(8,128)(2,1)S(1)}, bf16[2,336,128]{2,1,0:T(8,128)(2,1)S(1)}, u32[]{:S(2)}, u32[]{:S(2)}) collective-permute-start(bf16[2,336,128]{2,1,0:T(8,128)(2,1)S(1)} %relay_kernel.1), channel_id=1, source_target_pairs={{0,4},{4,8},{8,12},{12,16},{16,20},{20,24},{24,28},{28,0},{32,60},... | collective-permute-start | bytes 516104 | tf_op jit(solution)/shard_map/ppermute | solution.py:314
  72.8 9.7 %collective-permute-start.13 = (bf16[336,128]{1,0:T(8,128)(2,1)S(1)}, bf16[336,128]{1,0:T(8,128)(2,1)S(1)}, u32[]{:S(2)}, u32[]{:S(2)}) collective-permute-start(bf16[336,128]{1,0:T(8,128)(2,1)S(1)} %get-tuple-element.29), channel_id=1, source_target_pairs={{0,16},{4,20},{8,24},{12,28},{16,0},{20,4},{24,8},{28,12},{32,48},... | collective-permute-start | bytes 258056 | tf_op jit(solution)/shard_map/ppermute | solution.py:314
  81.9 1.4 %collective-permute-start.14 = (bf16[336,128]{1,0:T(8,128)(2,1)S(1)}, bf16[336,128]{1,0:T(8,128)(2,1)S(1)}, u32[]{:S(2)}, u32[]{:S(2)}) collective-permute-start(bf16[336,128]{1,0:T(8,128)(2,1)S(1)} %pass_kernel.1), channel_id=1, source_target_pairs={{0,32},{32,0},{1,33},{33,1},{2,34},{34,2},{3,35},{35,3},{4,36},{36... | collective-permute-start | bytes 258056 | tf_op jit(solution)/shard_map/ppermute | solution.py:325

commit v5 on v4

--- a/solution.py
+++ b/solution.py
@@ -266,7 +266,7 @@
     out_ref[...] = (one_ref[...].astype(F32) + two_ref[NC:].astype(F32)).astype(BF16)
 
 
-def pass_kernel(one_ref, two_ref, out_ref):
+def pass_kernel(one_ref, two_ref, far_ref, out_ref):
     out_ref[...] = (one_ref[1].astype(F32) + two_ref[1].astype(F32)).astype(BF16)
 
 
@@ -448,10 +448,10 @@
     )(keep, swap(send), terms)
     terms = exchange(terms)
     two = shift(two, 2)
-    far = shift(far, FAR)
+    far = hint(shift(far, FAR), 5)
     [one] = call(relay_kernel, [shape((NC, long, LANE), BF16)], [VM] * 2, cost=cost(10))(one, two)
     one = shift(one, 1)
-    [passed] = call(pass_kernel, [shape((long, LANE), BF16)], [VM] * 2)(one, two)
+    [passed] = call(pass_kernel, [shape((long, LANE), BF16)], [VM] * 3, cost=cost(1))(one, two, far)
     return call(
         final_kernel,
         [shape((OWN, width), BF16), shape((OWN, width), BF16), shape((1,), F32), shape((1,), F32)],

time: 87.7 us -> 87.7 us (level)
    ppermute x9, waiting for transfers between devices: 28.6 us -> 26.1 us  [shift(): return lax.ppermute(values, ('c', 'z'), pairs)]
    all_to_all x3, waiting for transfers between devices: 3.13 us -> 5.58 us  [exchange(): lax.all_to_all(values, ('x', 'c', 'z', 'y'), 0, 0, axis_index_groups=PLAN...]
where the time goes in v5:
time: 87.7 us; the launch traced here: 86.9 us
  starting transfers between devices  39.6 us (45%)
  waiting for transfers between devices  34.9 us (40%)
  Pallas kernels  9.8 us (11%)
  between operations  1.63 us (2%)
  local copies, waits for them, and re-layouts  0.94 us (1%)
    ppermute x9, waiting for transfers between devices, shift(): return lax.ppermute(values, ('c', 'z'), pairs)  26.1 us
    all_to_all x3, starting transfers between devices, exchange(): lax.all_to_all(values, ('x', 'c', 'z', 'y'), 0, 0, axis_index_groups=PLAN...  20.4 us
    ppermute x9, starting transfers between devices, shift(): return lax.ppermute(values, ('c', 'z'), pairs)  18.2 us
    all_to_all x3, waiting for transfers between devices, exchange(): lax.all_to_all(values, ('x', 'c', 'z', 'y'), 0, 0, axis_index_groups=PLAN...  5.58 us
    ppermute x6, waiting for transfers between devices, swap(): return lax.ppermute(values, 'c', [(0, 1), (1, 0)])  3.31 us
    pallas_call x1, Pallas kernels, shards(): call(logits_kernel, [shape((NXY, 2 * NB, LANE), F32), shape((4 * NB, LANE...  2.01 us
    pallas_call x1, Pallas kernels, shards(): call(terms_kernel, [shape((NXY, long, LANE), BF16)], [SM] + [VM] * 3, [AN...  1.8 us
    pallas_call x1, Pallas kernels, shards(): call(grad_kernel, [shape((TILE, TILE), BF16), shape(half, BF16), shape(ha...  1.8 us
  transfers between devices with their start and end apart: 18, of which 13 were waited for; matrix products, arithmetic and copies ran while one was open for 0% of the time, Pallas kernels for 5%

profile of v5, /device:TPU:2, one launch (start us, length us, event | category | flops | bytes accessed | tf_op | source)
XLA Modules:
  0.0 86.9 jit_solution(16478823858062466666)
XLA Ops:
  0.6 0.0 copy-start
  0.6 0.1 collective-permute-start
  0.7 0.0 copy-start.1
  0.8 0.9 %copy-done.1 = bf16[32,1280]{1,0:T(8,128)(2,1)S(1)} copy-done((bf16[32,1280]{1,0:T(8,128)(2,1)S(1)}, bf16[32,1280]{1,0:T(8,128)(2,1)}, u32[]{:S(2)}) %copy-start.1) | copy-done | bytes 81944
  1.6 1.3 %images_kernel.1.after_ref = bf16[16,32,1280]{2,1,0:T(8,128)(2,1)} custom-call(bf16[32,1280]{1,0:T(8,128)(2,1)S(1)} %copy-done.1), custom_call_target="tpu_custom_call" | custom-call | tf_op jit(solution)/shard_map/images_kernel/pallas_call | solution.py:385
  2.9 0.0 collective-permute-done.other_ref
  2.9 0.1 texts_kernel.1.chip_ref
  3.0 2.0 %collective-permute-start.1 = (bf16[2,32,1280]{2,1,0:T(8,128)(2,1)S(1)}, bf16[2,32,1280]{2,1,0:T(8,128)(2,1)S(1)}, u32[]{:S(2)}, u32[]{:S(2)}) collective-permute-start(bf16[2,32,1280]{2,1,0:T(8,128)(2,1)S(1)} %texts_kernel.1.chip_ref), channel_id=1, source_target_pairs={{0,4},{4,8},{8,12},{12,16},{16,20},{20,24},{24,28},{28,0},{32,60},... | collective-permute-start | bytes 491528 | tf_op jit(solution)/shard_map/ppermute | solution.py:314
  5.0 7.5 %all-to-all-start = ((bf16[16,32,1280]{2,1,0:T(8,128)(2,1)}), bf16[16,32,1280]{2,1,0:T(8,128)(2,1)S(1)}, u32[]{:S(2)}, u32[]{:S(2)}) async-start(bf16[16,32,1280]{2,1,0:T(8,128)(2,1)} %images_kernel.1.after_ref), calls=%async_computation | async-start | bytes 2621440 | tf_op jit(solution)/shard_map/all_to_all | solution.py:341
  12.5 0.0 collective-permute-done.1
  12.6 3.3 %collective-permute-start.2 = (bf16[4,32,1280]{2,1,0:T(8,128)(2,1)S(1)}, bf16[4,32,1280]{2,1,0:T(8,128)(2,1)S(1)}, u32[]{:S(2)}, u32[]{:S(2)}) collective-permute-start(bf16[4,32,1280]{2,1,0:T(8,128)(2,1)S(1)} %tie_kernel.5), channel_id=1, source_target_pairs={{0,8},{4,12},{8,16},{12,20},{16,24},{20,28},{24,0},{28,4},{32,56},... | collective-permute-start | bytes 983048 | tf_op jit(solution)/shard_map/ppermute | solution.py:314
  16.6 4.6 %collective-permute-start.3 = (bf16[1,32,1280]{2,1,0:T(8,128)(2,1)S(1)}, bf16[1,32,1280]{2,1,0:T(8,128)(2,1)S(1)}, u32[]{:S(2)}, u32[]{:S(2)}) collective-permute-start(bf16[1,32,1280]{2,1,0:T(8,128)(2,1)S(1)} %slice.4), channel_id=1, source_target_pairs={{0,16},{4,20},{8,24},{12,28},{16,0},{20,4},{24,8},{28,12},{32,48},... | collective-permute-start | bytes 245768 | tf_op jit(solution)/shard_map/ppermute | solution.py:314
  21.2 6.6 %collective-permute-done.2 = bf16[4,32,1280]{2,1,0:T(8,128)(2,1)S(1)} collective-permute-done((bf16[4,32,1280]{2,1,0:T(8,128)(2,1)S(1)}, bf16[4,32,1280]{2,1,0:T(8,128)(2,1)S(1)}, u32[]{:S(2)}, u32[]{:S(2)}) %collective-permute-start.2) | collective-permute-done | bytes 327712 | tf_op jit(solution)/shard_map/ppermute | solution.py:314
  27.8 3.7 %collective-permute-done.3 = bf16[1,32,1280]{2,1,0:T(8,128)(2,1)S(1)} collective-permute-done((bf16[1,32,1280]{2,1,0:T(8,128)(2,1)S(1)}, bf16[1,32,1280]{2,1,0:T(8,128)(2,1)S(1)}, u32[]{:S(2)}, u32[]{:S(2)}) %collective-permute-start.3) | collective-permute-done | bytes 81952 | tf_op jit(solution)/shard_map/ppermute | solution.py:314
  31.5 0.0 collective-permute-start.4
  31.5 0.7 all-to-all-done.ref
  32.1 0.6 early_kernel.1.part_ref
  32.7 0.7 collective-permute-done.4.other_ref
  33.4 2.0 %logits_kernel.1 = (f32[16,8,128]{2,1,0:T(8,128)}, f32[16,128]{1,0:T(8,128)S(1)}) custom-call(f32[1]{0:T(128)S(6)} %copy.21.log_ref, bf16[16,32,1280]{2,1,0:T(8,128)(2,1)S(1)} %tie_kernel.4.img_ref, f32[288,512]{1,0:T(8,128)S(1)} %early_kernel.1.part_ref, bf16[7,32,1280]{2,1,0:T(8,128)(2,1)S(1)} %collective-permute-done.4.other_ref), custom_call_target="tpu_custom_call" | custom-call | tf_op jit(solution)/shard_map/logits_kernel/pallas_call | solution.py:397
  35.4 0.1 collective-permute-start.5
  35.6 1.0 %collective-permute-done.5 = f32[16,128]{1,0:T(8,128)S(1)} collective-permute-done((f32[16,128]{1,0:T(8,128)S(1)}, f32[16,128]{1,0:T(8,128)S(1)}, u32[]{:S(2)}, u32[]{:S(2)}) %collective-permute-start.5) | collective-permute-done | bytes 8224 | tf_op jit(solution)/shard_map/ppermute | solution.py:325
  36.6 0.0 collective-permute-start.6
  36.6 4.9 %collective-permute-start.8 = (f32[1,16,128]{2,1,0:T(8,128)S(1)}, f32[1,16,128]{2,1,0:T(8,128)S(1)}, u32[]{:S(2)}, u32[]{:S(2)}) collective-permute-start(f32[1,16,128]{2,1,0:T(8,128)S(1)} %bitcast.3), channel_id=1, source_target_pairs={{0,16},{4,20},{8,24},{12,28},{16,0},{20,4},{24,8},{28,12},{32,48},... | collective-permute-start | bytes 24584 | tf_op jit(solution)/shard_map/ppermute | solution.py:314
  41.5 5.9 %all-to-all-start.1 = ((f32[16,8,128]{2,1,0:T(8,128)}), f32[16,8,128]{2,1,0:T(8,128)S(1)}, u32[]{:S(2)}, u32[]{:S(2)}) async-start(f32[16,8,128]{2,1,0:T(8,128)} %get-tuple-element.17), calls=%async_computation.1 | async-start | bytes 131072 | tf_op jit(solution)/shard_map/all_to_all | solution.py:341
  47.4 0.0 collective-permute-done.6
  47.4 0.8 collective-permute-start.7
  48.2 5.7 %collective-permute-done.7 = f32[4,16,128]{2,1,0:T(8,128)S(1)} collective-permute-done((f32[4,16,128]{2,1,0:T(8,128)S(1)}, f32[4,16,128]{2,1,0:T(8,128)S(1)}, u32[]{:S(2)}, u32[]{:S(2)}) %collective-permute-start.7) | collective-permute-done | bytes 32800 | tf_op jit(solution)/shard_map/ppermute | solution.py:314
  53.9 0.0 collective-permute-done.8
  53.9 0.1 collective-permute-start.9
  54.0 0.0 all-to-all-done.1.row_ref
  54.0 1.0 %again_kernel.1 = (f32[512,512]{1,0:T(8,128)S(1)}, bf16[512,1280]{1,0:T(8,128)(2,1)S(1)}) custom-call(f32[1]{0:T(128)S(6)} %copy.21.log_ref, bf16[16,32,1280]{2,1,0:T(8,128)(2,1)S(1)} %tie_kernel.4.img_ref, bf16[2,32,1280]{2,1,0:T(8,128)(2,1)S(1)} %texts_kernel.1.chip_ref, bf16[7,32,1280]{2,1,0:T(8,128)(2,1)S(1)} %constant_dynamic-update-slice_fusion.own_ref, ...), custom_call_target="tpu_custom_call" | custom-call | flops 34500001792 | tf_op jit(solution)/shard_map/again_kernel/pallas_call | solution.py:406
  55.0 0.2 collective-permute-done.9.other_ref
  55.2 1.8 %grad_kernel.1 = (bf16[512,512]{1,0:T(8,128)(2,1)S(1)}, bf16[8,336,128]{2,1,0:T(8,128)(2,1)S(1)}, bf16[8,336,128]{2,1,0:T(8,128)(2,1)S(1)}, bf16[16,128]{1,0:T(8,128)(2,1)S(1)}) custom-call(f32[1]{0:T(128)S(6)} %copy.21.log_ref, f32[512,512]{1,0:T(8,128)S(1)} %get-tuple-element.18.logit_ref, bf16[16,32,1280]{2,1,0:T(8,128)(2,1)S(1)} %tie_kernel.4.img_ref, ...), custom_call_target="tpu_custom_call" | custom-call | tf_op jit(solution)/shard_map/grad_kernel/pallas_call | solution.py:413
  57.0 0.5 collective-permute-start.10
  57.6 1.8 %terms_kernel.1.term_ref = bf16[16,336,128]{2,1,0:T(8,128)(2,1)} custom-call(f32[1]{0:T(128)S(6)} %copy.21.log_ref, bf16[512,512]{1,0:T(8,128)(2,1)S(1)} %get-tuple-element.22.grad_ref, bf16[512,1280]{1,0:T(8,128)(2,1)S(1)} %get-tuple-element.23.txt_ref, bf16[16,128]{1,0:T(8,128)(2,1)S(1)} %get-tuple-element.24.columns_ref), custom_call_target="tpu_custom_call" | custom-call | flops 4600000000 | tf_op jit(solution)/shard_map/terms_kernel/pallas_call | solution.py:428
  59.4 0.1 collective-permute-done.10.other_ref
  59.5 0.2 add_kernel.1
  59.6 0.3 collective-permute-start.11
  59.9 7.0 %all-to-all-start.2 = ((bf16[16,336,128]{2,1,0:T(8,128)(2,1)}), bf16[16,336,128]{2,1,0:T(8,128)(2,1)S(1)}, u32[]{:S(2)}, u32[]{:S(2)}) async-start(bf16[16,336,128]{2,1,0:T(8,128)(2,1)} %get-tuple-element.25), calls=%async_computation.2 | async-start | bytes 2752512 | tf_op jit(solution)/shard_map/all_to_all | solution.py:341
  66.9 2.2 %collective-permute-start.13 = (bf16[336,128]{1,0:T(8,128)(2,1)S(1)}, bf16[336,128]{1,0:T(8,128)(2,1)S(1)}, u32[]{:S(2)}, u32[]{:S(2)}) collective-permute-start(bf16[336,128]{1,0:T(8,128)(2,1)S(1)} %get-tuple-element.29), channel_id=1, source_target_pairs={{0,16},{4,20},{8,24},{12,28},{16,0},{20,4},{24,8},{28,12},{32,48},... | collective-permute-start | bytes 258056 | tf_op jit(solution)/shard_map/ppermute | solution.py:314
  69.2 3.5 %collective-permute-done.11.two_ref.refs_1_ = bf16[4,336,128]{2,1,0:T(8,128)(2,1)S(1)} collective-permute-done((bf16[4,336,128]{2,1,0:T(8,128)(2,1)S(1)}, bf16[4,336,128]{2,1,0:T(8,128)(2,1)S(1)}, u32[]{:S(2)}, u32[]{:S(2)}) %collective-permute-start.11) | collective-permute-done | bytes 344096 | tf_op jit(solution)/shard_map/ppermute | solution.py:314
  72.7 0.1 collective-permute-start.12
  72.8 3.7 %collective-permute-done.13.ref = bf16[336,128]{1,0:T(8,128)(2,1)S(1)} collective-permute-done((bf16[336,128]{1,0:T(8,128)(2,1)S(1)}, bf16[336,128]{1,0:T(8,128)(2,1)S(1)}, u32[]{:S(2)}, u32[]{:S(2)}) %collective-permute-start.13) | collective-permute-done | bytes 86048 | tf_op jit(solution)/shard_map/ppermute | solution.py:314
  76.5 2.9 %collective-permute-done.12.one_ref.refs_0_ = bf16[2,336,128]{2,1,0:T(8,128)(2,1)S(1)} collective-permute-done((bf16[2,336,128]{2,1,0:T(8,128)(2,1)S(1)}, bf16[2,336,128]{2,1,0:T(8,128)(2,1)S(1)}, u32[]{:S(2)}, u32[]{:S(2)}) %collective-permute-start.12) | collective-permute-done | bytes 172064 | tf_op jit(solution)/shard_map/ppermute | solution.py:314
  79.5 0.1 collective-permute-start.14
  79.6 1.3 %collective-permute-done.14.refs_4_ = bf16[336,128]{1,0:T(8,128)(2,1)S(1)} collective-permute-done((bf16[336,128]{1,0:T(8,128)(2,1)S(1)}, bf16[336,128]{1,0:T(8,128)(2,1)S(1)}, u32[]{:S(2)}, u32[]{:S(2)}) %collective-permute-start.14) | collective-permute-done | bytes 86048 | tf_op jit(solution)/shard_map/ppermute | solution.py:325
  80.8 4.9 %all-to-all-done.2.term_ref = bf16[16,336,128]{2,1,0:T(8,128)(2,1)S(1)} async-done(((bf16[16,336,128]{2,1,0:T(8,128)(2,1)}), bf16[16,336,128]{2,1,0:T(8,128)(2,1)S(1)}, u32[]{:S(2)}, u32[]{:S(2)}) %all-to-all-start.2) | async-done | bytes 1376288 | tf_op jit(solution)/shard_map/all_to_all | solution.py:341
  85.7 1.0 %final_kernel.1 = (bf16[32,1280]{1,0:T(8,128)(2,1)}, bf16[32,1280]{1,0:T(8,128)(2,1)}, f32[1]{0:T(128)}, f32[1]{0:T(128)}) custom-call(bf16[32,1280]{1,0:T(8,128)(2,1)S(1)} %copy-done.2, bf16[32,1280]{1,0:T(8,128)(2,1)S(1)} %copy-done, bf16[16,336,128]{2,1,0:T(8,128)(2,1)S(1)} %all-to-all-done.2.term_ref, ...), custom_call_target="tpu_custom_call" | custom-call | tf_op jit(solution)/shard_map/final_kernel/pallas_call | solution.py:455
  (19 shorter events, 0.2 us)
Async XLA Ops:
  0.6 2.3 %copy-start = (bf16[32,1280]{1,0:T(8,128)(2,1)S(1)}, bf16[32,1280]{1,0:T(8,128)(2,1)}, u32[]{:S(2)}) copy-start(bf16[32,1280]{1,0:T(8,128)(2,1)} %cap_ref.3) | copy-start | bytes 245764
  0.6 2.3 %collective-permute-start = (bf16[32,1280]{1,0:T(8,128)(2,1)}, bf16[32,1280]{1,0:T(8,128)(2,1)S(1)}, u32[]{:S(2)}, u32[]{:S(2)}) collective-permute-start(bf16[32,1280]{1,0:T(8,128)(2,1)} %cap_ref.3), channel_id=1, source_target_pairs={{0,32},{32,0},{1,33},{33,1},{2,34},{34,2},{3,35},{35,3},{4,36},{36... | collective-permute-start | bytes 245768 | tf_op jit(solution)/shard_map/ppermute | solution.py:325
  0.7 0.9 %copy-start.1 = (bf16[32,1280]{1,0:T(8,128)(2,1)S(1)}, bf16[32,1280]{1,0:T(8,128)(2,1)}, u32[]{:S(2)}) copy-start(bf16[32,1280]{1,0:T(8,128)(2,1)} %pic_ref.3) | copy-start | bytes 245764
  3.0 9.5 %collective-permute-start.1 = (bf16[2,32,1280]{2,1,0:T(8,128)(2,1)S(1)}, bf16[2,32,1280]{2,1,0:T(8,128)(2,1)S(1)}, u32[]{:S(2)}, u32[]{:S(2)}) collective-permute-start(bf16[2,32,1280]{2,1,0:T(8,128)(2,1)S(1)} %texts_kernel.1.chip_ref), channel_id=1, source_target_pairs={{0,4},{4,8},{8,12},{12,16},{16,20},{20,24},{24,28},{28,0},{32,60},... | collective-permute-start | bytes 491528 | tf_op jit(solution)/shard_map/ppermute | solution.py:314
  5.0 27.1 %all-to-all-start = ((bf16[16,32,1280]{2,1,0:T(8,128)(2,1)}), bf16[16,32,1280]{2,1,0:T(8,128)(2,1)S(1)}, u32[]{:S(2)}, u32[]{:S(2)}) async-start(bf16[16,32,1280]{2,1,0:T(8,128)(2,1)} %images_kernel.1.after_ref), calls=%async_computation | async-start | bytes 2621440 | tf_op jit(solution)/shard_map/all_to_all | solution.py:341
  12.6 15.2 %collective-permute-start.2 = (bf16[4,32,1280]{2,1,0:T(8,128)(2,1)S(1)}, bf16[4,32,1280]{2,1,0:T(8,128)(2,1)S(1)}, u32[]{:S(2)}, u32[]{:S(2)}) collective-permute-start(bf16[4,32,1280]{2,1,0:T(8,128)(2,1)S(1)} %tie_kernel.5), channel_id=1, source_target_pairs={{0,8},{4,12},{8,16},{12,20},{16,24},{20,28},{24,0},{28,4},{32,56},... | collective-permute-start | bytes 983048 | tf_op jit(solution)/shard_map/ppermute | solution.py:314
  16.6 14.9 %collective-permute-start.3 = (bf16[1,32,1280]{2,1,0:T(8,128)(2,1)S(1)}, bf16[1,32,1280]{2,1,0:T(8,128)(2,1)S(1)}, u32[]{:S(2)}, u32[]{:S(2)}) collective-permute-start(bf16[1,32,1280]{2,1,0:T(8,128)(2,1)S(1)} %slice.4), channel_id=1, source_target_pairs={{0,16},{4,20},{8,24},{12,28},{16,0},{20,4},{24,8},{28,12},{32,48},... | collective-permute-start | bytes 245768 | tf_op jit(solution)/shard_map/ppermute | solution.py:314
  31.5 2.0 %collective-permute-start.4 = (bf16[7,32,1280]{2,1,0:T(8,128)(2,1)S(1)}, bf16[7,32,1280]{2,1,0:T(8,128)(2,1)S(1)}, u32[]{:S(2)}, u32[]{:S(2)}) collective-permute-start(bf16[7,32,1280]{2,1,0:T(8,128)(2,1)S(1)} %constant_dynamic-update-slice_fusion.own_ref), channel_id=1, source_target_pairs={{0,32},{32,0},{1,33},{33,1},{2,34},{34,2},{3,35},{35,3},{4,36},{36... | collective-permute-start | bytes 1720328 | tf_op jit(solution)/shard_map/ppermute | solution.py:325
  35.4 1.2 %collective-permute-start.5 = (f32[16,128]{1,0:T(8,128)S(1)}, f32[16,128]{1,0:T(8,128)S(1)}, u32[]{:S(2)}, u32[]{:S(2)}) collective-permute-start(f32[16,128]{1,0:T(8,128)S(1)} %get-tuple-element.19), channel_id=1, source_target_pairs={{0,32},{32,0},{1,33},{33,1},{2,34},{34,2},{3,35},{35,3},{4,36},{36... | collective-permute-start | bytes 24584 | tf_op jit(solution)/shard_map/ppermute | solution.py:325
  36.6 10.8 %collective-permute-start.6 = (f32[2,16,128]{2,1,0:T(8,128)S(1)}, f32[2,16,128]{2,1,0:T(8,128)S(1)}, u32[]{:S(2)}, u32[]{:S(2)}) collective-permute-start(f32[2,16,128]{2,1,0:T(8,128)S(1)} %pad_maximum_fusion.2.chip_ref), channel_id=1, source_target_pairs={{0,4},{4,8},{8,12},{12,16},{16,20},{20,24},{24,28},{28,0},{32,60},... | collective-permute-start | bytes 49160 | tf_op jit(solution)/shard_map/ppermute | solution.py:314
  36.6 17.3 %collective-permute-start.8 = (f32[1,16,128]{2,1,0:T(8,128)S(1)}, f32[1,16,128]{2,1,0:T(8,128)S(1)}, u32[]{:S(2)}, u32[]{:S(2)}) collective-permute-start(f32[1,16,128]{2,1,0:T(8,128)S(1)} %bitcast.3), channel_id=1, source_target_pairs={{0,16},{4,20},{8,24},{12,28},{16,0},{20,4},{24,8},{28,12},{32,48},... | collective-permute-start | bytes 24584 | tf_op jit(solution)/shard_map/ppermute | solution.py:314
  41.5 12.5 %all-to-all-start.1 = ((f32[16,8,128]{2,1,0:T(8,128)}), f32[16,8,128]{2,1,0:T(8,128)S(1)}, u32[]{:S(2)}, u32[]{:S(2)}) async-start(f32[16,8,128]{2,1,0:T(8,128)} %get-tuple-element.17), calls=%async_computation.1 | async-start | bytes 131072 | tf_op jit(solution)/shard_map/all_to_all | solution.py:341
  47.4 6.4 %collective-permute-start.7 = (f32[4,16,128]{2,1,0:T(8,128)S(1)}, f32[4,16,128]{2,1,0:T(8,128)S(1)}, u32[]{:S(2)}, u32[]{:S(2)}) collective-permute-start(f32[4,16,128]{2,1,0:T(8,128)S(1)} %tie_kernel.6), channel_id=1, source_target_pairs={{0,8},{4,12},{8,16},{12,20},{16,24},{20,28},{24,0},{28,4},{32,56},... | collective-permute-start | bytes 98312 | tf_op jit(solution)/shard_map/ppermute | solution.py:314
  53.9 1.3 %collective-permute-start.9 = (f32[7,16,128]{2,1,0:T(8,128)S(1)}, f32[7,16,128]{2,1,0:T(8,128)S(1)}, u32[]{:S(2)}, u32[]{:S(2)}) collective-permute-start(f32[7,16,128]{2,1,0:T(8,128)S(1)} %constant_dynamic-update-slice_fusion.3.own_ref), channel_id=1, source_target_pairs={{0,32},{32,0},{1,33},{33,1},{2,34},{34,2},{3,35},{35,3},{4,36},{36... | collective-permute-start | bytes 172040 | tf_op jit(solution)/shard_map/ppermute | solution.py:325
  57.0 2.4 %collective-permute-start.10 = (bf16[8,336,128]{2,1,0:T(8,128)(2,1)S(1)}, bf16[8,336,128]{2,1,0:T(8,128)(2,1)S(1)}, u32[]{:S(2)}, u32[]{:S(2)}) collective-permute-start(bf16[8,336,128]{2,1,0:T(8,128)(2,1)S(1)} %get-tuple-element.21), channel_id=1, source_target_pairs={{0,32},{32,0},{1,33},{33,1},{2,34},{34,2},{3,35},{35,3},{4,36},{36... | collective-permute-start | bytes 2064392 | tf_op jit(solution)/shard_map/ppermute | solution.py:325
  59.6 13.1 %collective-permute-start.11 = (bf16[4,336,128]{2,1,0:T(8,128)(2,1)S(1)}, bf16[4,336,128]{2,1,0:T(8,128)(2,1)S(1)}, u32[]{:S(2)}, u32[]{:S(2)}) collective-permute-start(bf16[4,336,128]{2,1,0:T(8,128)(2,1)S(1)} %get-tuple-element.27), channel_id=1, source_target_pairs={{0,8},{4,12},{8,16},{12,20},{16,24},{20,28},{24,0},{28,4},{32,56},... | collective-permute-start | bytes 1032200 | tf_op jit(solution)/shard_map/ppermute | solution.py:314
  59.9 25.8 %all-to-all-start.2 = ((bf16[16,336,128]{2,1,0:T(8,128)(2,1)}), bf16[16,336,128]{2,1,0:T(8,128)(2,1)S(1)}, u32[]{:S(2)}, u32[]{:S(2)}) async-start(bf16[16,336,128]{2,1,0:T(8,128)(2,1)} %get-tuple-element.25), calls=%async_computation.2 | async-start | bytes 2752512 | tf_op jit(solution)/shard_map/all_to_all | solution.py:341
  66.9 9.6 %collective-permute-start.13 = (bf16[336,128]{1,0:T(8,128)(2,1)S(1)}, bf16[336,128]{1,0:T(8,128)(2,1)S(1)}, u32[]{:S(2)}, u32[]{:S(2)}) collective-permute-start(bf16[336,128]{1,0:T(8,128)(2,1)S(1)} %get-tuple-element.29), channel_id=1, source_target_pairs={{0,16},{4,20},{8,24},{12,28},{16,0},{20,4},{24,8},{28,12},{32,48},... | collective-permute-start | bytes 258056 | tf_op jit(solution)/shard_map/ppermute | solution.py:314
  72.7 6.7 %collective-permute-start.12 = (bf16[2,336,128]{2,1,0:T(8,128)(2,1)S(1)}, bf16[2,336,128]{2,1,0:T(8,128)(2,1)S(1)}, u32[]{:S(2)}, u32[]{:S(2)}) collective-permute-start(bf16[2,336,128]{2,1,0:T(8,128)(2,1)S(1)} %relay_kernel.1), channel_id=1, source_target_pairs={{0,4},{4,8},{8,12},{12,16},{16,20},{20,24},{24,28},{28,0},{32,60},... | collective-permute-start | bytes 516104 | tf_op jit(solution)/shard_map/ppermute | solution.py:314
  76.5 9.2 %copy-start.2 = (bf16[32,1280]{1,0:T(8,128)(2,1)S(1)}, bf16[32,1280]{1,0:T(8,128)(2,1)}, u32[]{:S(2)}) copy-start(bf16[32,1280]{1,0:T(8,128)(2,1)} %pic_ref.3) | copy-start | bytes 245764
  79.5 1.4 %collective-permute-start.14 = (bf16[336,128]{1,0:T(8,128)(2,1)S(1)}, bf16[336,128]{1,0:T(8,128)(2,1)S(1)}, u32[]{:S(2)}, u32[]{:S(2)}) collective-permute-start(bf16[336,128]{1,0:T(8,128)(2,1)S(1)} %pass_kernel.1), channel_id=1, source_target_pairs={{0,32},{32,0},{1,33},{33,1},{2,34},{34,2},{3,35},{35,3},{4,36},{36... | collective-permute-start | bytes 258056 | tf_op jit(solution)/shard_map/ppermute | solution.py:325
